TPU v7x, 32 devices: a whole 2x2x4 slice. The times are simulated.
32 devices in a mesh: ctx: 8 (over z, core), fsdp: 4 (over y, x).
Axes of the slice: x: 2, y: 2, z: 4, core: 2. Of those that a mesh axis runs over, the one named last changes fastest.
Arguments:
- tokens: bfloat16 [4, 1024, 2048], P('fsdp', 'ctx'), may hold values from -6 to 6
- block_order: int32 [8], replicated, may hold values from 0 to 7, each once
- norm_attn: bfloat16 [2048], P(('ctx', 'fsdp')), may hold values from 0.5 to 1.5
- w_query: bfloat16 [2048, 2048], P(('ctx', 'fsdp')), may hold values from -0.125 to 0.125
- w_key: bfloat16 [2048, 256], P(('ctx', 'fsdp')), may hold values from -0.125 to 0.125
- w_value: bfloat16 [2048, 256], P(('ctx', 'fsdp')), may hold values from -0.125 to 0.125
- w_out: bfloat16 [2048, 2048], P(('ctx', 'fsdp')), may hold values from -3 to 3
- norm_ffn: bfloat16 [2048], P(('ctx', 'fsdp')), may hold values from 0.5 to 1.5
- w_gate: bfloat16 [2048, 5632], P(('ctx', 'fsdp')), may hold values from -0.125 to 0.125
- w_up: bfloat16 [2048, 5632], P(('ctx', 'fsdp')), may hold values from -0.125 to 0.125
- w_down: bfloat16 [5632, 2048], P(('ctx', 'fsdp')), may hold values from -0.078125 to 0.078125
- cotangent: bfloat16 [4, 1024, 2048], P('fsdp', 'ctx'), may hold values from -6 to 6
Outputs:
- output: bfloat16 [4, 1024, 2048], P('fsdp', 'ctx')
- grad_tokens: bfloat16 [4, 1024, 2048], P('fsdp', 'ctx')
- grad_norm_attn: float32 [2048], P(('ctx', 'fsdp'))
- grad_query: float32 [2048, 2048], P(('ctx', 'fsdp'))
- grad_key: float32 [2048, 256], P(('ctx', 'fsdp'))
- grad_value: float32 [2048, 256], P(('ctx', 'fsdp'))
- grad_out: float32 [2048, 2048], P(('ctx', 'fsdp'))
- grad_norm_ffn: float32 [2048], P(('ctx', 'fsdp'))
- grad_gate: float32 [2048, 5632], P(('ctx', 'fsdp'))
- grad_up: float32 [2048, 5632], P(('ctx', 'fsdp'))
- grad_down: float32 [5632, 2048], P(('ctx', 'fsdp'))
Inputs may be any that keep to these rules, and one draw needn't show every extreme that they name: Every value appears once; index c of ctx holds blocks block_order[c] and 2 * 8 - 1 - block_order[c] of every sequence it has.
All inputs are finite; a program needn't handle non-finite values.
Results may differ from a plain program's by a relative error of at most 0.014.
Values may be sent and summed in bfloat16 or wider, within the bound.
No kernel may reach another device: no remote copies, remote signals or barrier semaphores. Data moves between devices by JAX's collectives and lax.ppermute only.
A program may use at most 192 MiB of HBM per device.

v0:
```python
import jax
import jax.numpy as jnp
from jax import lax
from jax.sharding import PartitionSpec as P

H = 32
KVH = 4
HD = 64
KVW = 256


EPS = 1e-05
THETA = 10000.0


def rms_parts(values):
    recip = lax.rsqrt(jnp.mean(values * values, axis=-1, keepdims=True) + EPS)
    return (values * recip, recip)


def norm_back(grad_in, normed, recip):
    return recip * (grad_in - normed * jnp.mean(grad_in * normed, axis=-1, keepdims=True))


def positions(block_order, first_row, row_count, tok_rows, ctx_count):
    row_ids = first_row + jnp.arange(row_count, dtype=jnp.int32)
    owner_index = row_ids // tok_rows
    within = row_ids % tok_rows
    half_rows = tok_rows // 2
    match = owner_index[:, None] == jnp.arange(ctx_count, dtype=jnp.int32)[None, :]
    paired = jnp.sum(jnp.where(match, block_order[None, :], 0), axis=1)
    block_id = jnp.where(within < half_rows, paired, 2 * ctx_count - 1 - paired)
    return block_id * half_rows + within % half_rows


def rope_tables(pos):
    freqs = THETA ** (-(jnp.arange(HD // 2, dtype=jnp.float32) * 2.0 / HD))
    angles = pos.astype(jnp.float32)[:, None] * freqs[None, :]
    return (jnp.cos(angles)[:, None, :], jnp.sin(angles)[:, None, :])


def rotate(values, cos_table, sin_table):
    first_half = values[..., : HD // 2]
    second_half = values[..., HD // 2 :]
    return jnp.concatenate(
        [
            first_half * cos_table - second_half * sin_table,
            second_half * cos_table + first_half * sin_table,
        ],
        axis=-1,
    )


def group_scores(group_index, queries, keys_all, q_pos, k_pos):
    groups = H // KVH
    tok_rows = queries.shape[0]
    q_part = lax.dynamic_slice_in_dim(queries, group_index * groups * HD, groups * HD, 1).reshape(
        tok_rows, groups, HD
    )
    k_part = lax.dynamic_slice_in_dim(keys_all, group_index * HD, HD, 1)
    scores = jnp.einsum("qjd,kd->jqk", q_part, k_part, preferred_element_type=jnp.float32) * HD ** (
        -0.5
    )
    visible = k_pos[None, :] <= q_pos[:, None]
    return (jnp.where(visible[None], scores, -jnp.inf), q_part, k_part)


def on_device(
    tokens,
    block_order,
    norm_attn,
    w_query,
    w_key,
    w_value,
    w_out,
    norm_ffn,
    w_gate,
    w_up,
    w_down,
    cotangent,
):
    ctx_count = lax.axis_size("ctx")
    fsdp_count = lax.axis_size("fsdp")
    tok_rows = tokens.shape[1]
    seq_length = tok_rows * ctx_count
    groups = H // KVH
    scale = HD ** (-0.5)
    ctx_index = lax.axis_index("ctx")
    q_pos = positions(block_order, ctx_index * tok_rows, tok_rows, tok_rows, ctx_count)
    k_pos = positions(block_order, 0, seq_length, tok_rows, ctx_count)
    cos_table, sin_table = rope_tables(q_pos)
    gain_a, weight_q, weight_k, weight_v, weight_o, gain_f = (
        lax.all_gather(norm_attn, ("ctx", "fsdp"), axis=0, tiled=True),
        lax.all_gather(w_query, ("ctx", "fsdp"), axis=0, tiled=True),
        lax.all_gather(w_key, ("ctx", "fsdp"), axis=0, tiled=True),
        lax.all_gather(w_value, ("ctx", "fsdp"), axis=0, tiled=True),
        lax.all_gather(w_out, ("ctx", "fsdp"), axis=0, tiled=True),
        lax.all_gather(norm_ffn, ("ctx", "fsdp"), axis=0, tiled=True),
    )
    source = tokens[0].astype(jnp.float32)
    normed_a, recip_a = rms_parts(source)
    hidden_a = (normed_a * gain_a.astype(jnp.float32)).astype(jnp.bfloat16)
    proj_q = jnp.dot(hidden_a, weight_q, preferred_element_type=jnp.float32)
    proj_k = jnp.dot(hidden_a, weight_k, preferred_element_type=jnp.float32)
    proj_v = jnp.dot(hidden_a, weight_v, preferred_element_type=jnp.float32)
    query_rot = (
        rotate(proj_q.reshape(tok_rows, H, HD), cos_table, sin_table)
        .reshape(tok_rows, H * HD)
        .astype(jnp.bfloat16)
    )
    key_rot = (
        rotate(proj_k.reshape(tok_rows, KVH, HD), cos_table, sin_table)
        .reshape(tok_rows, KVW)
        .astype(jnp.bfloat16)
    )
    value_low = proj_v.astype(jnp.bfloat16)
    keys_all, values_all = (
        lax.all_gather(key_rot, "ctx", axis=0, tiled=True),
        lax.all_gather(value_low, "ctx", axis=0, tiled=True),
    )

    def forward_group(group_index):
        scores, q_part, k_part = group_scores(group_index, query_rot, keys_all, q_pos, k_pos)
        v_part = lax.dynamic_slice_in_dim(values_all, group_index * HD, HD, 1)
        row_max = jnp.max(scores, axis=-1, keepdims=True)
        exponent = jnp.exp(scores - row_max)
        row_total = jnp.sum(exponent, axis=-1, keepdims=True)
        probability = (exponent / row_total).astype(jnp.bfloat16)
        attended = jnp.einsum(
            "jqk,kd->qjd", probability, v_part, preferred_element_type=jnp.float32
        )
        return (attended.reshape(tok_rows, groups * HD), (row_max + jnp.log(row_total))[..., 0])

    attended_all, log_sums = lax.map(forward_group, jnp.arange(KVH, dtype=jnp.int32))
    attended_low = attended_all.transpose(1, 0, 2).reshape(tok_rows, H * HD).astype(jnp.bfloat16)
    residual = source + jnp.dot(attended_low, weight_o, preferred_element_type=jnp.float32)
    normed_f, recip_f = rms_parts(residual)
    hidden_f = (normed_f * gain_f.astype(jnp.float32)).astype(jnp.bfloat16)
    grad_low = cotangent[0]
    rows_shard = w_gate.shape[0]
    ff_total = w_gate.shape[1]
    piece_cols = ff_total // (ctx_count * fsdp_count)
    gate_cols, up_cols = (
        lax.all_to_all(
            w_gate.reshape(rows_shard, ctx_count, fsdp_count, piece_cols),
            "fsdp",
            split_axis=2,
            concat_axis=0,
            tiled=True,
        ),
        lax.all_to_all(
            w_up.reshape(rows_shard, ctx_count, fsdp_count, piece_cols),
            "fsdp",
            split_axis=2,
            concat_axis=0,
            tiled=True,
        ),
    )
    gate_rows, up_rows, weight_d = (
        lax.all_gather(gate_cols, "ctx", axis=0, tiled=True),
        lax.all_gather(up_cols, "ctx", axis=0, tiled=True),
        lax.all_gather(w_down, "ctx", axis=0, tiled=True),
    )
    weight_g = gate_rows.reshape(gate_rows.shape[0], ctx_count * piece_cols)
    weight_u = up_rows.reshape(up_rows.shape[0], ctx_count * piece_cols)
    ffn_in, ffn_grad = (
        lax.all_gather(hidden_f, "fsdp", axis=0, tiled=True),
        lax.all_gather(grad_low, "fsdp", axis=0, tiled=True),
    )
    gate_pre = jnp.dot(ffn_in, weight_g, preferred_element_type=jnp.float32)
    up_pre = jnp.dot(ffn_in, weight_u, preferred_element_type=jnp.float32)
    sigmoid_gate = jax.nn.sigmoid(gate_pre)
    activated = gate_pre * sigmoid_gate
    gated_values = (activated * up_pre).astype(jnp.bfloat16)
    down_part = jnp.dot(gated_values, weight_d, preferred_element_type=jnp.float32)
    down_part = lax.psum_scatter(down_part, "fsdp", scatter_dimension=0, tiled=True)
    result = (residual + down_part).astype(jnp.bfloat16)
    grad_down_full = jnp.einsum(
        "tf,td->fd", gated_values, ffn_grad, preferred_element_type=jnp.float32
    )
    grad_inner = jnp.einsum("td,fd->tf", ffn_grad, weight_d, preferred_element_type=jnp.float32)
    grad_up_pre = (grad_inner * activated).astype(jnp.bfloat16)
    grad_gate_pre = (
        grad_inner * up_pre * sigmoid_gate * (1.0 + gate_pre * (1.0 - sigmoid_gate))
    ).astype(jnp.bfloat16)
    grad_gate_full = jnp.einsum(
        "td,tf->df", ffn_in, grad_gate_pre, preferred_element_type=jnp.float32
    )
    grad_up_full = jnp.einsum("td,tf->df", ffn_in, grad_up_pre, preferred_element_type=jnp.float32)
    grad_hidden_f = jnp.einsum(
        "tf,df->td", grad_gate_pre, weight_g, preferred_element_type=jnp.float32
    ) + jnp.einsum("tf,df->td", grad_up_pre, weight_u, preferred_element_type=jnp.float32)
    grad_hidden_f = lax.psum_scatter(grad_hidden_f, "fsdp", scatter_dimension=0, tiled=True)
    width_rows = grad_gate_full.shape[0]
    part_gate, part_up, shard_down = (
        lax.psum_scatter(
            grad_gate_full.reshape(width_rows, ctx_count, 1, piece_cols),
            "ctx",
            scatter_dimension=0,
            tiled=True,
        ),
        lax.psum_scatter(
            grad_up_full.reshape(width_rows, ctx_count, 1, piece_cols),
            "ctx",
            scatter_dimension=0,
            tiled=True,
        ),
        lax.psum_scatter(grad_down_full, "ctx", scatter_dimension=0, tiled=True),
    )
    owned_gate, owned_up = (
        lax.all_to_all(part_gate, "fsdp", split_axis=0, concat_axis=2, tiled=True),
        lax.all_to_all(part_up, "fsdp", split_axis=0, concat_axis=2, tiled=True),
    )
    shard_gate = owned_gate.reshape(rows_shard, ff_total)
    shard_up = owned_up.reshape(rows_shard, ff_total)
    grad_gain_f = jnp.sum(grad_hidden_f * normed_f, axis=0)
    grad_residual = grad_low.astype(jnp.float32) + norm_back(
        grad_hidden_f * gain_f.astype(jnp.float32), normed_f, recip_f
    )
    gain_a, weight_q, weight_k, weight_v, weight_o = (
        lax.all_gather(norm_attn, ("ctx", "fsdp"), axis=0, tiled=True),
        lax.all_gather(w_query, ("ctx", "fsdp"), axis=0, tiled=True),
        lax.all_gather(w_key, ("ctx", "fsdp"), axis=0, tiled=True),
        lax.all_gather(w_value, ("ctx", "fsdp"), axis=0, tiled=True),
        lax.all_gather(w_out, ("ctx", "fsdp"), axis=0, tiled=True),
    )
    branch_low = grad_residual.astype(jnp.bfloat16)
    grad_out_full = jnp.einsum(
        "tq,td->qd", attended_low, branch_low, preferred_element_type=jnp.float32
    )
    grad_attended = jnp.einsum(
        "td,qd->tq", branch_low, weight_o, preferred_element_type=jnp.float32
    ).astype(jnp.bfloat16)

    def backward_group(pieces):
        group_index, log_part = pieces
        scores, q_part, k_part = group_scores(group_index, query_rot, keys_all, q_pos, k_pos)
        v_part = lax.dynamic_slice_in_dim(values_all, group_index * HD, HD, 1)
        grad_part = lax.dynamic_slice_in_dim(
            grad_attended, group_index * groups * HD, groups * HD, 1
        ).reshape(tok_rows, groups, HD)
        probability = jnp.exp(scores - log_part[..., None])
        prob_low = probability.astype(jnp.bfloat16)
        grad_prob = jnp.einsum("qjd,kd->jqk", grad_part, v_part, preferred_element_type=jnp.float32)
        row_delta = jnp.sum(probability * grad_prob, axis=-1, keepdims=True)
        grad_score = (probability * (grad_prob - row_delta)).astype(jnp.bfloat16)
        grad_q_part = (
            jnp.einsum("jqk,kd->qjd", grad_score, k_part, preferred_element_type=jnp.float32)
            * scale
        )
        grad_k_part = (
            jnp.einsum("jqk,qjd->kd", grad_score, q_part, preferred_element_type=jnp.float32)
            * scale
        )
        grad_v_part = jnp.einsum(
            "jqk,qjd->kd", prob_low, grad_part, preferred_element_type=jnp.float32
        )
        return (grad_q_part.reshape(tok_rows, groups * HD), grad_k_part, grad_v_part)

    grad_q_all, grad_k_all, grad_v_all = lax.map(
        backward_group, (jnp.arange(KVH, dtype=jnp.int32), log_sums)
    )
    grad_q_rot = grad_q_all.transpose(1, 0, 2).reshape(tok_rows, H, HD)
    grad_k_terms = grad_k_all.transpose(1, 0, 2).reshape(seq_length, KVW)
    grad_v_terms = grad_v_all.transpose(1, 0, 2).reshape(seq_length, KVW)
    grad_k_rows, grad_v_rows = (
        lax.psum_scatter(grad_k_terms, "ctx", scatter_dimension=0, tiled=True),
        lax.psum_scatter(grad_v_terms, "ctx", scatter_dimension=0, tiled=True),
    )
    grad_q_low = (
        rotate(grad_q_rot, cos_table, -sin_table).reshape(tok_rows, H * HD).astype(jnp.bfloat16)
    )
    grad_k_low = (
        rotate(grad_k_rows.reshape(tok_rows, KVH, HD), cos_table, -sin_table)
        .reshape(tok_rows, KVW)
        .astype(jnp.bfloat16)
    )
    grad_v_low = grad_v_rows.astype(jnp.bfloat16)
    grad_q_full = jnp.einsum("td,tq->dq", hidden_a, grad_q_low, preferred_element_type=jnp.float32)
    grad_k_full = jnp.einsum("td,tk->dk", hidden_a, grad_k_low, preferred_element_type=jnp.float32)
    grad_v_full = jnp.einsum("td,tk->dk", hidden_a, grad_v_low, preferred_element_type=jnp.float32)
    grad_hidden_a = (
        jnp.einsum("tq,dq->td", grad_q_low, weight_q, preferred_element_type=jnp.float32)
        + jnp.einsum("tk,dk->td", grad_k_low, weight_k, preferred_element_type=jnp.float32)
        + jnp.einsum("tk,dk->td", grad_v_low, weight_v, preferred_element_type=jnp.float32)
    )
    grad_gain_a = jnp.sum(grad_hidden_a * normed_a, axis=0)
    grad_source = grad_residual + norm_back(
        grad_hidden_a * gain_a.astype(jnp.float32), normed_a, recip_a
    )
    shard_gain_a, shard_query, shard_key, shard_value, shard_out, shard_gain_f = (
        lax.psum_scatter(grad_gain_a, ("ctx", "fsdp"), scatter_dimension=0, tiled=True),
        lax.psum_scatter(grad_q_full, ("ctx", "fsdp"), scatter_dimension=0, tiled=True),
        lax.psum_scatter(grad_k_full, ("ctx", "fsdp"), scatter_dimension=0, tiled=True),
        lax.psum_scatter(grad_v_full, ("ctx", "fsdp"), scatter_dimension=0, tiled=True),
        lax.psum_scatter(grad_out_full, ("ctx", "fsdp"), scatter_dimension=0, tiled=True),
        lax.psum_scatter(grad_gain_f, ("ctx", "fsdp"), scatter_dimension=0, tiled=True),
    )
    return (
        result[None],
        grad_source.astype(jnp.bfloat16)[None],
        shard_gain_a,
        shard_query,
        shard_key,
        shard_value,
        shard_out,
        shard_gain_f,
        shard_gate,
        shard_up,
        shard_down,
    )


def solution(mesh):
    in_specs = (
        P("fsdp", "ctx", None),
        P(),
        P(("ctx", "fsdp")),
        P(("ctx", "fsdp"), None),
        P(("ctx", "fsdp"), None),
        P(("ctx", "fsdp"), None),
        P(("ctx", "fsdp"), None),
        P(("ctx", "fsdp")),
        P(("ctx", "fsdp"), None),
        P(("ctx", "fsdp"), None),
        P(("ctx", "fsdp"), None),
        P("fsdp", "ctx", None),
    )
    out_specs = (
        P("fsdp", "ctx", None),
        P("fsdp", "ctx", None),
        P(("ctx", "fsdp")),
        P(("ctx", "fsdp"), None),
        P(("ctx", "fsdp"), None),
        P(("ctx", "fsdp"), None),
        P(("ctx", "fsdp"), None),
        P(("ctx", "fsdp")),
        P(("ctx", "fsdp"), None),
        P(("ctx", "fsdp"), None),
        P(("ctx", "fsdp"), None),
    )
    return jax.shard_map(
        on_device, mesh=mesh, in_specs=in_specs, out_specs=out_specs, check_vma=False
    )
```

profile of v0, /device:TPU:9, one launch (start us, length us, event | category | flops | bytes accessed | tf_op | source)
XLA Modules:
  0.0 2264.6 jit_solution(14981274660329866690)
XLA Ops:
  10.0 4.4 reshape.427
  19.6 47.0 %all-reduce.5 = (bf16[2048]{0:T(1024)(128)(2,1)S(1)}, bf16[2048]{0:T(1024)(128)(2,1)S(1)}) all-reduce(bf16[2048]{0:T(1024)(128)(2,1)S(1)} %dynamic-update-slice, bf16[2048]{0:T(1024)(128)(2,1)S(1)} %dynamic-update-slice.1), channel_id=1, replica_groups=mesh['ctx'=8,'fsdp'=4] {'ctx','fsdp'}, use_global_device_ids=true, to_apply=%add | all-reduce | flops 4096 | bytes 16384
  71.3 14.5 all_gather.46
  86.0 38.1 %all-gather.13.cloned.1.call-done = bf16[2048,256]{1,0:T(8,128)(2,1)} async-done(((bf16[64,256]{1,0:T(8,128)(2,1)}), bf16[2048,256]{1,0:T(8,128)(2,1)}) %all-gather.13.cloned.1.call-update) | async-done | bytes 1048592 | tf_op jit(solution)/shard_map/all_gather | solution.py:95
  126.1 14.7 all_gather.48
  140.8 63.2 %all-gather.15.cloned.1.call-done = bf16[2048,2048]{1,0:T(8,128)(2,1)} async-done(((bf16[64,2048]{1,0:T(8,128)(2,1)}), bf16[2048,2048]{1,0:T(8,128)(2,1)}) %all-gather.15.cloned.1.call-update) | async-done | bytes 8388624 | tf_op jit(solution)/shard_map/all_gather | solution.py:94
  204.0 12.3 copy.88
  216.4 5.8 fusion.66
  222.4 19.9 while.32
  242.4 40.6 %all-gather.17.cloned.1.call-done = bf16[2048,2048]{1,0:T(8,128)(2,1)} async-done(((bf16[64,2048]{1,0:T(8,128)(2,1)}), bf16[2048,2048]{1,0:T(8,128)(2,1)}) %all-gather.17.cloned.1.call-update) | async-done | bytes 8388624 | tf_op jit(solution)/shard_map/all_gather | solution.py:97
  283.0 4.7 multiply_reduce_fusion.2
  288.8 4.4 reshape.429
  293.3 16.0 all_to_all.66
  312.6 28.8 %all-gather.21.cloned.1.call-done = bf16[2048,8,1,176]{0,3,2,1:T(8,128)(2,1)} async-done(((bf16[256,8,1,176]{0,3,2,1:T(8,128)(2,1)}), bf16[2048,8,1,176]{0,3,2,1:T(8,128)(2,1)}) %all-gather.21.cloned.1.call-update) | async-done | bytes 5767184 | tf_op jit(solution)/shard_map/all_gather | solution.py:160
  341.4 38.4 %all-gather.19.cloned.1.call-done = bf16[512,2048]{1,0:T(8,128)(2,1)} async-done(((bf16[128,2048]{1,0:T(8,128)(2,1)}), bf16[512,2048]{1,0:T(8,128)(2,1)}) %all-gather.19.cloned.1.call-update) | async-done | bytes 2097168 | tf_op jit(solution)/shard_map/all_gather | solution.py:167
  379.8 8.3 fusion.100
  388.1 52.1 %all-gather.23.cloned.1.call-done = bf16[2048,8,1,176]{0,3,2,1:T(8,128)(2,1)} async-done(((bf16[256,8,1,176]{0,3,2,1:T(8,128)(2,1)}), bf16[2048,8,1,176]{0,3,2,1:T(8,128)(2,1)}) %all-gather.23.cloned.1.call-update) | async-done | bytes 5767184 | tf_op jit(solution)/shard_map/all_gather | solution.py:161
  440.3 8.3 fusion.101
  448.5 29.7 %all-gather.27.cloned.1.call-done = bf16[1,512,2048]{2,1,0:T(8,128)(2,1)} async-done(((bf16[1,128,2048]{2,1,0:T(8,128)(2,1)}), bf16[1,512,2048]{2,1,0:T(8,128)(2,1)}) %all-gather.27.cloned.1.call-update) | async-done | bytes 2097168 | tf_op jit(solution)/shard_map/all_gather | solution.py:168
  478.2 60.5 %all-gather.25.cloned.1.call-done = bf16[1408,2048]{1,0:T(8,128)(2,1)} async-done(((bf16[176,2048]{1,0:T(8,128)(2,1)}), bf16[1408,2048]{1,0:T(8,128)(2,1)}) %all-gather.25.cloned.1.call-update) | async-done | bytes 5767184 | tf_op jit(solution)/shard_map/all_gather | solution.py:162
  538.7 10.4 multiply_convert_fusion
  549.1 6.6 fusion.103
  555.7 5.0 convolution_add_fusion
  561.0 8.6 fusion.102
  569.7 44.2 %reduce-scatter.14.cloned.1.call-done = f32[128,2048]{1,0:T(8,128)} async-done(((f32[512,2048]{1,0:T(8,128)}), f32[128,2048]{1,0:T(8,128)}) %reduce-scatter.14.cloned.1.call-update) | async-done | bytes 1048592 | tf_op jit(solution)/shard_map/reduce_scatter | solution.py:193
  615.5 54.4 %reduce-scatter.12.cloned.1.call-done = f32[128,2048]{1,0:T(8,128)} async-done(((f32[512,2048]{1,0:T(8,128)}), f32[128,2048]{1,0:T(8,128)}) %reduce-scatter.12.cloned.1.call-update) | async-done | bytes 1048592 | tf_op jit(solution)/shard_map/reduce_scatter | solution.py:176
  672.8 6.3 convolution_convert_fusion
  679.0 60.4 %while.33 = (s32[]{:T(128)}, f32[4,128,512]{1,2,0:T(8,128)}, f32[4,1024,64]{1,2,0:T(8,128)}, f32[4,1024,64]{1,2,0:T(8,128)}, s32[4]{0:T(128)S(1)}, /*index=5*/bf...) while((s32[]{:T(128)}, f32[4,128,512]{1,2,0:T(8,128)}, ...), condition=%wide.region_13.14_spmd.clone, body=%wide.region_11.13_spmd.sunk.clone | while | flops 687078400 | bytes 51807028 | solution.py:260
  684.9 3.6 fusion.197
  700.0 3.6 fusion.197
  740.6 9.5 fusion.105
  750.1 17.7 copy.96
  769.2 9.0 fusion.106
  778.2 17.8 copy.98
  802.5 9.0 fusion.44
  813.2 8.2 fusion.72
  822.4 8.1 fusion.74
  830.5 141.7 %reduce-scatter.28.cloned.1.call-done = f32[256,8,1,176]{3,1,2,0:T(8,128)} async-done(((f32[2048,8,1,176]{3,1,2,0:T(8,128)}), f32[256,8,1,176]{3,1,2,0:T(8,128)}) %reduce-scatter.28.cloned.1.call-update) | async-done | bytes 1441808 | tf_op jit(solution)/shard_map/reduce_scatter | solution.py:196
  972.1 4.4 all-to-all-start.2
  976.6 7.3 fusion.104
  983.9 157.1 %reduce-scatter.30.cloned.1.call-done = f32[256,8,1,176]{3,1,2,0:T(8,128)} async-done(((f32[2048,8,1,176]{3,1,2,0:T(8,128)}), f32[256,8,1,176]{3,1,2,0:T(8,128)}) %reduce-scatter.30.cloned.1.call-update) | async-done | bytes 1441808 | tf_op jit(solution)/shard_map/reduce_scatter | solution.py:202
  1141.0 4.4 all-to-all-start.3
  1149.0 67.1 %all-reduce.4 = (f32[2048]{0:T(1024)S(1)}, f32[2048]{0:T(1024)S(1)}) all-reduce(f32[2048]{0:T(1024)S(1)} %get-tuple-element.388, f32[2048]{0:T(1024)S(1)} %get-tuple-element.386), channel_id=7, replica_groups=mesh['ctx'=8,'fsdp'=4] {'ctx','fsdp'}, use_global_device_ids=true, to_apply=%region_18.19.clone | all-reduce | flops 4096 | bytes 32768
  1231.4 33.7 %reduce-scatter.22.cloned.1.call-done = f32[64,256]{1,0:T(8,128)} async-done(((f32[2048,256]{1,0:T(8,128)}), f32[64,256]{1,0:T(8,128)}) %reduce-scatter.22.cloned.1.call-update) | async-done | bytes 65552 | tf_op jit(solution)/shard_map/reduce_scatter | solution.py:294
  1265.1 137.4 %reduce-scatter.24.cloned.1.call-done = f32[64,256]{1,0:T(8,128)} async-done(((f32[2048,256]{1,0:T(8,128)}), f32[64,256]{1,0:T(8,128)}) %reduce-scatter.24.cloned.1.call-update) | async-done | bytes 65552 | tf_op jit(solution)/shard_map/reduce_scatter | solution.py:295
  1402.5 133.0 %reduce-scatter.32.cloned.1.call-done = f32[176,2048]{1,0:T(8,128)} async-done(((f32[1408,2048]{1,0:T(8,128)}), f32[176,2048]{1,0:T(8,128)}) %reduce-scatter.32.cloned.1.call-update) | async-done | bytes 1441808 | tf_op jit(solution)/shard_map/reduce_scatter | solution.py:208
  1535.5 360.3 %reduce-scatter.20.cloned.1.call-done = f32[64,2048]{1,0:T(8,128)} async-done(((f32[2048,2048]{1,0:T(8,128)}), f32[64,2048]{1,0:T(8,128)}) %reduce-scatter.20.cloned.1.call-update) | async-done | bytes 524304 | tf_op jit(solution)/shard_map/reduce_scatter | solution.py:293
  1895.8 361.8 %reduce-scatter.26.cloned.1.call-done = f32[64,2048]{1,0:T(8,128)} async-done(((f32[2048,2048]{1,0:T(8,128)}), f32[64,2048]{1,0:T(8,128)}) %reduce-scatter.26.cloned.1.call-update) | async-done | bytes 524304 | tf_op jit(solution)/shard_map/reduce_scatter | solution.py:296
  (239 shorter events, 116.8 us)
Async XLA Ops:
  7.2 11.9 copy-start.18
  7.2 12.2 copy-start.19
  7.2 59.5 %copy-start.16 = (s32[8]{0:T(128)S(1)}, s32[8]{0:T(128)}, u32[]{:S(2)}) copy-start(s32[8]{0:T(128)} %param.17) | copy-start | bytes 100
  7.2 59.7 %copy-start.1 = (bf16[1,128,2048]{2,1,0:T(8,128)(2,1)S(1)}, bf16[1,128,2048]{2,1,0:T(8,128)(2,1)}, u32[]{:S(2)}) copy-start(bf16[1,128,2048]{2,1,0:T(8,128)(2,1)} %param.16) | copy-start | bytes 1572868
  7.2 62.4 %all-gather.11.cloned.1.call-start = ((), (), s32[]{:S(2)}) async-start(), calls=%async_computation.15 | async-start | bytes 1081344 | tf_op jit(solution)/shard_map/all_gather | solution.py:96
  8.0 116.1 %all-gather.13.cloned.1.call-start = ((), (), s32[]{:S(2)}) async-start(), calls=%async_computation.16 | async-start | bytes 1081344 | tf_op jit(solution)/shard_map/all_gather | solution.py:95
  8.7 195.3 %all-gather.15.cloned.1.call-start = ((), (), s32[]{:S(2)}) async-start(), calls=%async_computation.17 | async-start | bytes 8650752 | tf_op jit(solution)/shard_map/all_gather | solution.py:94
  9.4 273.5 %all-gather.17.cloned.1.call-start = ((), (), s32[]{:S(2)}) async-start(), calls=%async_computation.18 | async-start | bytes 8650752 | tf_op jit(solution)/shard_map/all_gather | solution.py:97
  15.5 52.5 %all-to-all-start = ((bf16[64,8,4,176]{3,1,0,2:T(8,128)(2,1)}), bf16[64,8,4,176]{3,1,0,2:T(8,128)(2,1)S(1)}, u32[]{:S(2)}, u32[]{:S(2)}) async-start(bf16[64,8,4,176]{3,1,0,2:T(8,128)(2,1)} %copy.90), calls=%async_computation | async-start | bytes 2097152 | tf_op jit(solution)/shard_map/all_to_all | solution.py:144
  19.0 322.4 %all-gather.21.cloned.1.call-start = ((), (), s32[]{:S(2)}) async-start(), calls=%async_computation.20 | async-start | bytes 6488064 | tf_op jit(solution)/shard_map/all_gather | solution.py:160
  66.7 149.7 %copy-start.9 = (f32[2048]{0:T(1024)}, f32[2048]{0:T(1024)S(1)}, u32[]{:S(2)}) copy-start(f32[2048]{0:T(1024)S(1)} %convert_element_type.134) | copy-start | bytes 24580
  67.1 149.2 %copy-start.14 = (f32[128]{0:T(128)}, f32[128]{0:T(128)S(1)}, u32[]{:S(2)}) copy-start(f32[128]{0:T(128)S(1)} %add_rsqrt_fusion.1) | copy-start | bytes 1540
  67.9 154.3 %copy-start.11 = (f32[128,32]{0,1:T(8,128)}, f32[128,32]{0,1:T(8,128)S(1)}, u32[]{:S(2)}) copy-start(f32[128,32]{0,1:T(8,128)S(1)} %get-tuple-element.457) | copy-start | bytes 49156
  69.6 310.2 %all-gather.19.cloned.1.call-start = ((), (), s32[]{:S(2)}) async-start(), calls=%async_computation.19 | async-start | bytes 2621440 | tf_op jit(solution)/shard_map/all_gather | solution.py:167
  242.3 40.6 %copy-start.6 = (bf16[1024,256]{0,1:T(8,128)(2,1)}, bf16[1024,256]{0,1:T(8,128)(2,1)S(1)}, u32[]{:S(2)}) copy-start(bf16[1024,256]{0,1:T(8,128)(2,1)S(1)} %get-tuple-element.789) | copy-start | bytes 1572868
  242.4 45.3 %copy-start.2 = (bf16[4,128,512]{1,2,0:T(8,128)(2,1)}, bf16[4,128,512]{1,2,0:T(8,128)(2,1)S(1)}, u32[]{:S(2)}) copy-start(bf16[4,128,512]{1,2,0:T(8,128)(2,1)S(1)} %get-tuple-element.276) | copy-start | bytes 1572868
  242.4 45.3 %copy-start.4 = (bf16[128,2048]{0,1:T(8,128)(2,1)}, bf16[128,2048]{0,1:T(8,128)(2,1)S(1)}, u32[]{:S(2)}) copy-start(bf16[128,2048]{0,1:T(8,128)(2,1)S(1)} %get-tuple-element.777) | copy-start | bytes 1572868
  288.7 151.5 %all-gather.23.cloned.1.call-start = ((), (), s32[]{:S(2)}) async-start(), calls=%async_computation.21 | async-start | bytes 6488064 | tf_op jit(solution)/shard_map/all_gather | solution.py:161
  310.9 167.3 %all-gather.27.cloned.1.call-start = ((), (), s32[]{:S(2)}) async-start(), calls=%async_computation.34 | async-start | bytes 2621440 | tf_op jit(solution)/shard_map/all_gather | solution.py:168
  311.6 227.1 %all-gather.25.cloned.1.call-start = ((), (), s32[]{:S(2)}) async-start(), calls=%async_computation.22 | async-start | bytes 6488064 | tf_op jit(solution)/shard_map/all_gather | solution.py:162
  312.4 301.6 %reduce-scatter.14.cloned.1.call-start = ((), (), s32[]{:S(2)}) async-start(), calls=%async_computation.24 | async-start | bytes 5242880 | tf_op jit(solution)/shard_map/reduce_scatter | solution.py:193
  549.1 6.6 copy-start.23
  549.1 6.6 copy-start.21
  549.1 6.6 copy-start.17
  560.8 109.1 %reduce-scatter.12.cloned.1.call-start = ((), (), s32[]{:S(2)}) async-start(), calls=%async_computation.23 | async-start | bytes 5242880 | tf_op jit(solution)/shard_map/reduce_scatter | solution.py:176
  569.6 226.5 %reduce-scatter.16.cloned.1.call-start = ((), (), s32[]{:S(2)}) async-start(), calls=%async_computation.25 | async-start | bytes 1179648 | tf_op jit(solution)/shard_map/reduce_scatter | solution.py:267
  684.9 3.6 copy-start
  700.0 3.6 copy-start
  715.1 3.6 copy-start
  730.2 3.6 copy-start
  739.4 60.2 %reduce-scatter.18.cloned.1.call-start = ((), (), s32[]{:S(2)}) async-start(), calls=%async_computation.26 | async-start | bytes 1179648 | tf_op jit(solution)/shard_map/reduce_scatter | solution.py:268
  740.2 232.0 %reduce-scatter.28.cloned.1.call-start = ((), (), s32[]{:S(2)}) async-start(), calls=%async_computation.31 | async-start | bytes 18874368 | tf_op jit(solution)/shard_map/reduce_scatter | solution.py:196
  767.8 1.4 copy-start.22
  767.9 373.1 %reduce-scatter.30.cloned.1.call-start = ((), (), s32[]{:S(2)}) async-start(), calls=%async_computation.32 | async-start | bytes 18874368 | tf_op jit(solution)/shard_map/reduce_scatter | solution.py:202
  796.0 1.6 copy-start.10
  796.0 1.7 copy-start.15
  796.0 469.1 %reduce-scatter.22.cloned.1.call-start = ((), (), s32[]{:S(2)}) async-start(), calls=%async_computation.28 | async-start | bytes 2162688 | tf_op jit(solution)/shard_map/reduce_scatter | solution.py:294
  797.7 4.9 copy-start.20
  799.6 602.9 %reduce-scatter.24.cloned.1.call-start = ((), (), s32[]{:S(2)}) async-start(), calls=%async_computation.29 | async-start | bytes 2162688 | tf_op jit(solution)/shard_map/reduce_scatter | solution.py:295
  802.5 733.0 %reduce-scatter.32.cloned.1.call-start = ((), (), s32[]{:S(2)}) async-start(), calls=%async_computation.33 | async-start | bytes 12976128 | tf_op jit(solution)/shard_map/reduce_scatter | solution.py:208
  811.5 1.4 copy-start.7
  811.5 1084.2 %reduce-scatter.20.cloned.1.call-start = ((), (), s32[]{:S(2)}) async-start(), calls=%async_computation.27 | async-start | bytes 17301504 | tf_op jit(solution)/shard_map/reduce_scatter | solution.py:293
  821.4 1.0 copy-start.3
  821.4 1436.2 %reduce-scatter.26.cloned.1.call-start = ((), (), s32[]{:S(2)}) async-start(), calls=%async_computation.30 | async-start | bytes 17301504 | tf_op jit(solution)/shard_map/reduce_scatter | solution.py:296
  972.1 168.8 %all-to-all-start.2 = ((f32[256,8,1,176]{3,1,2,0:T(8,128)}), f32[256,8,1,176]{3,1,2,0:T(8,128)}, u32[]{:S(2)}, u32[]{:S(2)}) async-start(f32[256,8,1,176]{3,1,2,0:T(8,128)} %reduce-scatter.28.cloned.1.call-done), calls=%async_computation.11 | async-start | bytes 4194304 | tf_op jit(solution)/shard_map/all_to_all | solution.py:211
  983.9 161.6 %copy-start.5 = (f32[128,2048]{1,0:T(8,128)S(1)}, f32[128,2048]{1,0:T(8,128)}, u32[]{:S(2)}) copy-start(f32[128,2048]{1,0:T(8,128)} %fusion.104) | copy-start | bytes 3145732
  983.9 163.3 %copy-start.8 = (f32[128,256]{0,1:T(8,128)S(1)}, f32[128,256]{0,1:T(8,128)}, u32[]{:S(2)}) copy-start(f32[128,256]{0,1:T(8,128)} %reduce-scatter.18.cloned.1.call-done) | copy-start | bytes 393220
  1141.0 84.0 %all-to-all-start.3 = ((f32[256,8,1,176]{3,1,2,0:T(8,128)}), f32[256,8,1,176]{3,1,2,0:T(8,128)}, u32[]{:S(2)}, u32[]{:S(2)}) async-start(f32[256,8,1,176]{3,1,2,0:T(8,128)} %reduce-scatter.30.cloned.1.call-done), calls=%async_computation.13 | async-start | bytes 4194304 | tf_op jit(solution)/shard_map/all_to_all | solution.py:212
  (2 other events, 1.5 us)
Sparse Core Ops, SparseCore 0:
  11.1 57.1 all-gather.10
  71.3 52.7 all-gather.12
  126.9 77.0 all-gather.14
  206.8 76.1 all-gather.16
  285.0 56.4 all-gather.20
  343.7 36.0 all-gather.18
  381.9 58.2 all-gather.22
  442.1 36.0 all-gather.26
  479.8 58.8 all-gather.24
  560.9 52.9 reduce-scatter.13
  617.2 52.6 reduce-scatter.11
  739.6 25.8 reduce-scatter.15
  767.7 30.5 reduce-scatter.17
  800.5 171.5 reduce-scatter.27
  974.3 166.5 reduce-scatter.29
  1143.7 121.4 reduce-scatter.21
  1267.9 134.5 reduce-scatter.23
  1405.3 130.1 reduce-scatter.31
  1538.3 357.4 reduce-scatter.19
  1898.5 358.9 reduce-scatter.25
where the time goes:
time: 2270 us; the launch traced here: 2260 us
  waiting for transfers between devices  1780 us (78%)
  matrix products  173 us (8%)
  blocking collectives  159 us (7%)
  local copies, waits for them, and re-layouts  93.5 us (4%)
    reduce_scatter x1, waiting for transfers between devices, on_device(): lax.psum_scatter(grad_out_full, ('ctx', 'fsdp'), scatter_dimension=0, til...  362 us
    reduce_scatter x1, waiting for transfers between devices, on_device(): lax.psum_scatter(grad_q_full, ('ctx', 'fsdp'), scatter_dimension=0, tiled...  360 us
    reduce_scatter x1, waiting for transfers between devices, on_device(): lax.psum_scatter(grad_up_full.reshape(width_rows, ctx_count, 1, piece_col...  157 us
    reduce_scatter x1, waiting for transfers between devices, on_device(): lax.psum_scatter(grad_gate_full.reshape(width_rows, ctx_count, 1, piece_c...  142 us
    reduce_scatter x1, waiting for transfers between devices, on_device(): lax.psum_scatter(grad_v_full, ('ctx', 'fsdp'), scatter_dimension=0, tiled...  137 us
    reduce_scatter x1, waiting for transfers between devices, on_device(): lax.psum_scatter(grad_down_full, 'ctx', scatter_dimension=0, tiled=True)  133 us
    unnamed x2, blocking collectives  114 us
    all_gather x1, waiting for transfers between devices, on_device(): lax.all_gather(w_query, ('ctx', 'fsdp'), axis=0, tiled=True)  63.2 us
  transfers between devices with their start and end apart: 23, of which 17 were waited for; matrix products, arithmetic and copies ran while one was open for 9% of the time, Pallas kernels for 0%

commit v1 on v0

v1 whole, which is shorter than its diff:
```python
import jax
import jax.numpy as jnp
from jax import lax
from jax.sharding import PartitionSpec as P

H = 32
KVH = 4
HD = 64

EPS = 1e-05
THETA = 10000.0
BF = jnp.bfloat16
F32 = jnp.float32


def rms_parts(values):
    recip = lax.rsqrt(jnp.mean(values * values, axis=-1, keepdims=True) + EPS)
    return (values * recip, recip)


def norm_back(grad_in, normed, recip):
    return recip * (grad_in - normed * jnp.mean(grad_in * normed, axis=-1, keepdims=True))


def positions(block_order, row_count, tok_rows, ctx_count):
    row_ids = jnp.arange(row_count, dtype=jnp.int32)
    owner_index = row_ids // tok_rows
    within = row_ids % tok_rows
    half_rows = tok_rows // 2
    match = owner_index[:, None] == jnp.arange(ctx_count, dtype=jnp.int32)[None, :]
    paired = jnp.sum(jnp.where(match, block_order[None, :], 0), axis=1)
    block_id = jnp.where(within < half_rows, paired, 2 * ctx_count - 1 - paired)
    return block_id * half_rows + within % half_rows


def rope_tables(pos):
    freqs = THETA ** (-(jnp.arange(HD // 2, dtype=F32) * 2.0 / HD))
    angles = pos.astype(F32)[:, None] * freqs[None, :]
    return (jnp.cos(angles)[:, None, :], jnp.sin(angles)[:, None, :])


def rotate(values, cos_table, sin_table):
    first_half = values[..., : HD // 2]
    second_half = values[..., HD // 2 :]
    return jnp.concatenate(
        [
            first_half * cos_table - second_half * sin_table,
            second_half * cos_table + first_half * sin_table,
        ],
        axis=-1,
    )


def swap_f(value, step, f_count):
    return lax.ppermute(value, "fsdp", [(i, i ^ step) for i in range(f_count)])


def gather_f(value, f_index, f_count):
    out = jnp.zeros((f_count,) + value.shape, value.dtype)
    out = lax.dynamic_update_index_in_dim(out, value, f_index, 0)
    for step in range(1, f_count):
        out = lax.dynamic_update_index_in_dim(
            out, swap_f(value, step, f_count), f_index ^ step, 0
        )
    return out


def reduce_f(parts, f_index, f_count):
    total = lax.dynamic_index_in_dim(parts, f_index, 0, keepdims=False).astype(F32)
    low = parts.astype(BF)
    for step in range(1, f_count):
        piece = lax.dynamic_index_in_dim(low, f_index ^ step, 0, keepdims=False)
        total = total + swap_f(piece, step, f_count).astype(F32)
    return total


def dot(a, b):
    return jnp.dot(a, b, preferred_element_type=F32)


def dot_nt(a, b):
    return lax.dot_general(a, b, (((1,), (1,)), ((), ())), preferred_element_type=F32)


def dot_tn(a, b):
    return lax.dot_general(a, b, (((0,), (0,)), ((), ())), preferred_element_type=F32)


def on_device(
    tokens,
    block_order,
    norm_attn,
    w_query,
    w_key,
    w_value,
    w_out,
    norm_ffn,
    w_gate,
    w_up,
    w_down,
    cotangent,
):
    c_count = lax.axis_size("ctx")
    f_count = lax.axis_size("fsdp")
    f_index = lax.axis_index("fsdp")
    c_index = lax.axis_index("ctx")
    tok_rows = tokens.shape[1]
    width = tokens.shape[2]
    seq = tok_rows * c_count
    heads = H // c_count
    share = c_count // KVH
    q_cols = heads * HD
    rows = w_query.shape[0]
    ff_cols = w_gate.shape[1] // c_count
    scale = HD ** (-0.5)

    def to_columns(packed):
        moved = lax.all_to_all(packed, "ctx", split_axis=0, concat_axis=0, tiled=True)
        full = gather_f(moved, f_index, f_count)
        return full.transpose(1, 0, 2, 3).reshape(c_count * f_count * rows, packed.shape[2])

    def kv_pack(w):
        return jnp.repeat(w.reshape(rows, KVH, HD).transpose(1, 0, 2), share, axis=0)

    x_all = lax.all_gather(tokens[0], "ctx", axis=0, tiled=True)
    qkv_pack = jnp.concatenate(
        [
            w_query.reshape(rows, c_count, q_cols).transpose(1, 0, 2),
            kv_pack(w_key),
            kv_pack(w_value),
        ],
        axis=2,
    )
    w_qkv = to_columns(qkv_pack)
    gains = lax.all_gather(
        jnp.concatenate([norm_attn, norm_ffn])[None], ("ctx", "fsdp"), axis=0, tiled=True
    )
    gain_a = gains[:, :rows].reshape(width).astype(F32)
    gain_f = gains[:, rows:].reshape(width).astype(F32)
    w_o = gather_f(w_out, f_index, f_count).reshape(f_count * rows, width)
    gu_pack = jnp.concatenate(
        [
            w_gate.reshape(rows, c_count, ff_cols).transpose(1, 0, 2),
            w_up.reshape(rows, c_count, ff_cols).transpose(1, 0, 2),
        ],
        axis=2,
    )
    w_gu = to_columns(gu_pack)
    w_d = gather_f(w_down, f_index, f_count).reshape(ff_cols, width)
    g_all = lax.all_gather(cotangent[0], "ctx", axis=0, tiled=True)

    pos = positions(block_order, seq, tok_rows, c_count)
    cos_table, sin_table = rope_tables(pos)

    normed_all, _ = rms_parts(x_all.astype(F32))
    h1 = (normed_all * gain_a).astype(BF)
    qkv = dot(h1, w_qkv)
    q = rotate(qkv[:, :q_cols].reshape(seq, heads, HD), cos_table, sin_table).astype(BF)
    k = rotate(qkv[:, None, q_cols : q_cols + HD], cos_table, sin_table)[:, 0].astype(BF)
    v = qkv[:, q_cols + HD :].astype(BF)
    scores = jnp.einsum("qjd,kd->jqk", q, k, preferred_element_type=F32) * scale
    scores = jnp.where((pos[None, :] <= pos[:, None])[None], scores, -jnp.inf)
    row_max = jnp.max(scores, axis=-1, keepdims=True)
    exponent = jnp.exp(scores - row_max)
    prob = exponent / jnp.sum(exponent, axis=-1, keepdims=True)
    prob_low = prob.astype(BF)
    o = jnp.einsum("jqk,kd->qjd", prob_low, v, preferred_element_type=F32)
    o = o.astype(BF).reshape(seq, q_cols)
    y_rows = lax.psum_scatter(dot(o, w_o).astype(BF), "ctx", scatter_dimension=0, tiled=True)
    source = tokens[0].astype(F32)
    residual = source + y_rows.astype(F32)
    normed_f, recip_f = rms_parts(residual)
    h2 = lax.all_gather((normed_f * gain_f).astype(BF), "ctx", axis=0, tiled=True)

    gu = dot(h2, w_gu)
    gate = gu[:, :ff_cols]
    up = gu[:, ff_cols:]
    sig = jax.nn.sigmoid(gate)
    act = gate * sig
    z = (act * up).astype(BF)
    out_rows = lax.psum_scatter(dot(z, w_d).astype(BF), "ctx", scatter_dimension=0, tiled=True)
    result = (residual + out_rows.astype(F32)).astype(BF)
    dz = dot_nt(g_all, w_d)
    dub = (dz * act).astype(BF)
    dgb = (dz * up * sig * (1.0 + gate * (1.0 - sig))).astype(BF)
    dgu = jnp.concatenate([dgb, dub], axis=1)
    dh2 = lax.psum_scatter(dot_nt(dgu, w_gu).astype(BF), "ctx", scatter_dimension=0, tiled=True)
    dh2 = dh2.astype(F32)

    def from_columns(full):
        cols = full.shape[1]
        parts = full.reshape(c_count, f_count, rows, cols).transpose(1, 0, 2, 3)
        owned = reduce_f(parts, f_index, f_count)
        return lax.all_to_all(owned.astype(BF), "ctx", split_axis=0, concat_axis=0, tiled=True)

    grad_gu = from_columns(dot_tn(h2, dgu))
    shard_down = reduce_f(dot_tn(z, g_all).reshape(f_count, -1, width), f_index, f_count)
    shard_gate = grad_gu[:, :, :ff_cols].transpose(1, 0, 2).reshape(rows, -1).astype(F32)
    shard_up = grad_gu[:, :, ff_cols:].transpose(1, 0, 2).reshape(rows, -1).astype(F32)

    grad_gain_f = jnp.sum(dh2 * normed_f, axis=0)
    d_res = cotangent[0].astype(F32) + norm_back(dh2 * gain_f, normed_f, recip_f)
    ab = lax.all_gather(d_res.astype(BF), "ctx", axis=0, tiled=True)
    shard_out = reduce_f(dot_tn(o, ab).reshape(f_count, rows, width), f_index, f_count)
    d_o = dot_nt(ab, w_o).astype(BF).reshape(seq, heads, HD)
    d_prob = jnp.einsum("qjd,kd->jqk", d_o, v, preferred_element_type=F32)
    delta = jnp.sum(prob * d_prob, axis=-1, keepdims=True)
    d_s = (prob * (d_prob - delta)).astype(BF)
    dq = jnp.einsum("jqk,kd->qjd", d_s, k, preferred_element_type=F32) * scale
    dk = jnp.einsum("jqk,qjd->kd", d_s, q, preferred_element_type=F32) * scale
    dv = jnp.einsum("jqk,qjd->kd", prob_low, d_o, preferred_element_type=F32)
    dq = rotate(dq, cos_table, -sin_table).astype(BF).reshape(seq, q_cols)
    dk = rotate(dk[:, None], cos_table, -sin_table)[:, 0].astype(BF)
    dqkv = jnp.concatenate([dq, dk, dv.astype(BF)], axis=1)
    dh1_part = dot_nt(dqkv, w_qkv)
    dh1 = lax.psum_scatter(dh1_part.astype(BF), "ctx", scatter_dimension=0, tiled=True)
    dh1 = dh1.astype(F32)
    grad_qkv = from_columns(dot_tn(h1, dqkv))
    shard_query = grad_qkv[:, :, :q_cols].transpose(1, 0, 2).reshape(rows, -1).astype(F32)
    grad_kv = jnp.sum(
        grad_qkv[:, :, q_cols:].reshape(KVH, share, rows, 2 * HD).astype(F32), axis=1
    )
    shard_key = grad_kv[:, :, :HD].transpose(1, 0, 2).reshape(rows, -1)
    shard_value = grad_kv[:, :, HD:].transpose(1, 0, 2).reshape(rows, -1)

    normed_a, recip_a = rms_parts(source)
    grad_gain_a = jnp.sum(dh1 * normed_a, axis=0)
    grad_tokens = d_res + norm_back(dh1 * gain_a, normed_a, recip_a)
    shard_gain_a = lax.psum_scatter(grad_gain_a, ("ctx", "fsdp"), scatter_dimension=0, tiled=True)
    shard_gain_f = lax.psum_scatter(grad_gain_f, ("ctx", "fsdp"), scatter_dimension=0, tiled=True)
    return (
        result[None],
        grad_tokens.astype(BF)[None],
        shard_gain_a,
        shard_query,
        shard_key,
        shard_value,
        shard_out,
        shard_gain_f,
        shard_gate,
        shard_up,
        shard_down,
    )


def solution(mesh):
    both = ("ctx", "fsdp")
    row = P(both, None)
    in_specs = (
        P("fsdp", "ctx", None),
        P(),
        P(both),
        row,
        row,
        row,
        row,
        P(both),
        row,
        row,
        row,
        P("fsdp", "ctx", None),
    )
    out_specs = (
        P("fsdp", "ctx", None),
        P("fsdp", "ctx", None),
        P(both),
        row,
        row,
        row,
        row,
        P(both),
        row,
        row,
        row,
    )
    return jax.shard_map(
        on_device, mesh=mesh, in_specs=in_specs, out_specs=out_specs, check_vma=False
    )
```

time: 2270 us -> 773 us (0.34)
  waiting for transfers between devices: 1780 us -> 377 us
  matrix products: 173 us -> 113 us
  blocking collectives: 159 us -> 103 us
  starting transfers between devices: 14.2 us -> 59.4 us
  local copies, waits for them, and re-layouts: 93.5 us -> 51.6 us
  other arithmetic: 18.8 us -> 41.9 us
    reduce_scatter x11 -> x4, waiting for transfers between devices: 1420 us -> 101 us  [the longest x1 51 us: on_device(): lax.psum_scatter(dot(o, w_o).astype(BF), 'ctx', scatter_dimension=0, tile...]
    all_gather x9 -> x4, waiting for transfers between devices: 351 us -> 45.6 us  [the longest x1 45.6 us: on_device(): ab = lax.all_gather(d_res.astype(BF), 'ctx', axis=0, tiled=True)]
    ppermute x0 -> x24, waiting for transfers between devices: none -> 179 us  [swap_f(): return lax.ppermute(value, 'fsdp', [(i, i ^ step) for i in range(f_count)])]
    unnamed x2 -> x1, blocking collectives: 114 us -> 39.9 us
    dot_general x49 -> x17, matrix products: 173 us -> 104 us  [the longest x4 29.1 us: dot_nt(): lax.dot_general(a, b, (((1,), (1,)), ((), ())), preferred_element_type=F32)]
    all_to_all x3 -> x4, waiting for transfers between devices: 0.01 us -> 50.2 us  [the longest x2 43.6 us: to_columns(): lax.all_to_all(packed, 'ctx', split_axis=0, concat_axis=0, tiled=True)]
    reshape x8 -> x6, local copies, waits for them, and re-layouts: 52.5 us -> 4.57 us  [the longest x2 1.72 us: kv_pack(): w.reshape(rows, KVH, HD).transpose(1, 0, 2)]
    all_gather x2 -> x1, blocking collectives: 29.2 us -> 63.3 us  [on_device(): lax.all_gather(jnp.concatenate([norm_attn, norm_ffn])[None], ('ctx', 'fsd...]
  transfers between devices with their start and end apart: 23 -> 36, of which waited for: 17 -> 15; matrix products, arithmetic and copies ran while one was open for 9% -> 13% of each run, Pallas kernels for 0% -> 0%
where the time goes in v1:
time: 773 us; the launch traced here: 762 us
  waiting for transfers between devices  377 us (49%)
  matrix products  113 us (15%)
  blocking collectives  103 us (13%)
  starting transfers between devices  59.4 us (8%)
  local copies, waits for them, and re-layouts  51.6 us (7%)
  other arithmetic  41.9 us (5%)
  between operations  15.5 us (2%)
    ppermute x24, waiting for transfers between devices, swap_f(): return lax.ppermute(value, 'fsdp', [(i, i ^ step) for i in range(f_count)])  179 us
    all_gather x1, blocking collectives, on_device(): lax.all_gather(jnp.concatenate([norm_attn, norm_ffn])[None], ('ctx', 'fsd...  63.3 us
    reduce_scatter x1, waiting for transfers between devices, on_device(): lax.psum_scatter(dot(o, w_o).astype(BF), 'ctx', scatter_dimension=0, tile...  51 us
    reduce_scatter x1, waiting for transfers between devices, on_device(): lax.psum_scatter(dot_nt(dgu, w_gu).astype(BF), 'ctx', scatter_dimension=0...  50.4 us
    all_gather x1, waiting for transfers between devices, on_device(): ab = lax.all_gather(d_res.astype(BF), 'ctx', axis=0, tiled=True)  45.6 us
    all_to_all x2, waiting for transfers between devices, to_columns(): lax.all_to_all(packed, 'ctx', split_axis=0, concat_axis=0, tiled=True)  43.6 us
    unnamed x1, blocking collectives  39.9 us
    dot_general x4, matrix products, dot_nt(): lax.dot_general(a, b, (((1,), (1,)), ((), ())), preferred_element_type=F32)  29.1 us
  transfers between devices with their start and end apart: 36, of which 15 were waited for; matrix products, arithmetic and copies ran while one was open for 13% of the time, Pallas kernels for 0%

profile of v1, /device:TPU:9, one launch (start us, length us, event | category | flops | bytes accessed | tf_op | source)
XLA Modules:
  0.0 761.9 jit_solution(16179661330595919592)
XLA Ops:
  14.5 6.5 all-to-all-start
  21.1 63.3 %all-gather.3 = bf16[32,1,128]{2,1,0:T(2,128)(2,1)S(1)} all-gather(bf16[1,1,128]{2,1,0:T(2,128)(2,1)S(1)} %maximum_bitcast_fusion.7), channel_id=3, replica_groups=mesh['ctx'=8,'fsdp'=4] {'ctx','fsdp'}, dimensions={0}, use_global_device_ids=true | all-gather | bytes 8448 | tf_op jit(solution)/shard_map/all_gather | solution.py:135
  88.5 2.8 collective-permute-start.2
  92.7 5.7 collective-permute-done
  98.5 12.0 %collective-permute-done.1 = bf16[8,64,384]{2,1,0:T(8,128)(2,1)S(1)} collective-permute-done((bf16[8,64,384]{2,1,0:T(8,128)(2,1)S(1)}, bf16[8,64,384]{2,1,0:T(8,128)(2,1)S(1)}, u32[]{:S(2)}, u32[]{:S(2)}) %collective-permute-start.1) | collective-permute-done | bytes 393248 | tf_op jit(solution)/shard_map/ppermute | solution.py:55
  110.8 3.7 fusion.5
  118.7 9.3 %fusion.123 = (f32[4,1024]{1,0:T(4,128)S(1)}, f32[4,1024,1024]{1,2,0:T(8,128)}) fusion(pred[1024,1024]{0,1:T(8,128)(4,1)S(1)} %copy-done.13, bf16[1024,4,32]{0,2,1:T(8,128)(2,1)S(1)} %get-tuple-element.37, bf16[1024,4,32]{0,2,1:T(8,128)(2,1)S(1)} %get-tuple-element.36, bf16[1024,1,32]{0,2,1:T(8,128)(2,1)S(1)} %get-tuple-element.46, ...), kind=kOutput, calls=%fused_computation.216 | convolution fusion | flops 554959872 | bytes 18497536 | tf_op jit(solution)/shard_map/sub | solution.py:164
  128.0 7.5 fusion.38
  136.3 3.3 bitcast_convert_fusion
  140.1 51.0 %reduce-scatter.5.cloned.1.call-done = bf16[128,2048]{1,0:T(8,128)(2,1)} async-done(((bf16[1024,2048]{1,0:T(8,128)(2,1)}), bf16[128,2048]{1,0:T(8,128)(2,1)}) %reduce-scatter.5.cloned.1.call-update) | async-done | bytes 524304 | tf_op jit(solution)/shard_map/reduce_scatter | solution.py:169
  197.6 5.9 all-to-all-start.1
  209.6 12.0 %collective-permute-done.9 = bf16[176,2048]{1,0:T(8,128)(2,1)S(1)} collective-permute-done((bf16[176,2048]{1,0:T(8,128)(2,1)S(1)}, bf16[176,2048]{1,0:T(8,128)(2,1)S(1)}, u32[]{:S(2)}, u32[]{:S(2)}) %collective-permute-start.9) | collective-permute-done | bytes 720928 | tf_op jit(solution)/shard_map/ppermute | solution.py:55
  222.5 43.6 %all-to-all-done.1 = bf16[8,64,1408]{2,1,0:T(8,128)(2,1)S(1)} async-done(((bf16[8,64,1408]{2,1,0:T(8,128)(2,1)}), bf16[8,64,1408]{2,1,0:T(8,128)(2,1)S(1)}, u32[]{:S(2)}, u32[]{:S(2)}) %all-to-all-start.1) | async-done | bytes 1441824 | tf_op jit(solution)/shard_map/all_to_all | solution.py:118
  272.8 3.2 broadcast_in_dim.149
  277.3 21.7 %collective-permute-done.6 = bf16[8,64,1408]{2,1,0:T(8,128)(2,1)S(1)} collective-permute-done((bf16[8,64,1408]{2,1,0:T(8,128)(2,1)S(1)}, bf16[8,64,1408]{2,1,0:T(8,128)(2,1)S(1)}, u32[]{:S(2)}, u32[]{:S(2)}) %collective-permute-start.6) | collective-permute-done | bytes 1441824 | tf_op jit(solution)/shard_map/ppermute | solution.py:55
  300.2 32.8 %collective-permute-done.7 = bf16[8,64,1408]{2,1,0:T(8,128)(2,1)S(1)} collective-permute-done((bf16[8,64,1408]{2,1,0:T(8,128)(2,1)S(1)}, bf16[8,64,1408]{2,1,0:T(8,128)(2,1)S(1)}, u32[]{:S(2)}, u32[]{:S(2)}) %collective-permute-start.7) | collective-permute-done | bytes 1441824 | tf_op jit(solution)/shard_map/ppermute | solution.py:55
  335.4 11.7 %fusion.125 = f32[1024,1408]{1,0:T(8,128)} fusion(bf16[1024,2048]{1,0:T(8,128)(2,1)} %all-gather.9.cloned.1.call-done, bf16[2048,1408]{1,0:T(8,128)(2,1)} %bitcast.34), kind=kOutput, calls=%fused_computation.218 | convolution fusion | flops 5905580032 | bytes 15728640 | tf_op jit(solution)/shard_map/dot_general | solution.py:78
  347.1 10.2 %fusion.23 = (bf16[1024,704]{1,0:T(8,128)(2,1)S(1)}, bf16[1024,704]{1,0:T(8,128)(2,1)S(1)}, bf16[1024,704]{1,0:T(8,128)(2,1)}) fusion(f32[1024,1408]{1,0:T(8,128)} %fusion.125, bf16[704,2048]{1,0:T(8,128)(2,1)} %bitcast.39, bf16[1,1024,2048]{2,1,0:T(8,128)(2,1)} %all-gather.15.cloned.1.call-done), kind=kOutput, calls=%fused_computation.36 | convolution fusion | flops 2963603456 | bytes 17170432 | tf_op jit(solution)/shard_map/dot_general | solution.py:82
  359.0 11.0 %convolution_convert_fusion.1 = bf16[1024,2048]{1,0:T(8,128)(2,1)} fusion(bf16[2048,1408]{1,0:T(8,128)(2,1)} %bitcast.34, bf16[1024,704]{1,0:T(8,128)(2,1)S(1)} %get-tuple-element.21, bf16[1024,704]{1,0:T(8,128)(2,1)S(1)} %get-tuple-element.20), kind=kOutput, calls=%fused_computation.30 | convolution fusion | flops 5913444352 | bytes 12845056 | tf_op jit(solution)/shard_map/dot_general | solution.py:82
  370.0 50.4 %reduce-scatter.9.cloned.1.call-done = bf16[128,2048]{1,0:T(8,128)(2,1)} async-done(((bf16[1024,2048]{1,0:T(8,128)(2,1)}), bf16[128,2048]{1,0:T(8,128)(2,1)}) %reduce-scatter.9.cloned.1.call-update) | async-done | bytes 524304 | tf_op jit(solution)/shard_map/reduce_scatter | solution.py:187
  422.0 2.3 fusion.120
  424.5 45.6 %all-gather.11.cloned.1.call-done = bf16[1024,2048]{1,0:T(8,128)(2,1)} async-done(((bf16[128,2048]{1,0:T(8,128)(2,1)}), bf16[1024,2048]{1,0:T(8,128)(2,1)}) %all-gather.11.cloned.1.call-update) | async-done | bytes 4194320 | tf_op jit(solution)/shard_map/all_gather | solution.py:203
  470.2 3.6 convolution_convert_fusion.3
  473.8 8.6 %fusion.53 = bf16[1024,64]{0,1:T(8,128)(2,1)S(1)} fusion(bf16[1024,4,64]{0,2,1:T(8,128)(2,1)S(1)} %bitcast.296, f32[4,1024,1024]{1,2,0:T(8,128)} %get-tuple-element.55, f32[4,1024]{1,0:T(4,128)S(1)} %get-tuple-element.54), kind=kOutput, calls=%fused_computation.84 | convolution fusion | flops 545325056 | bytes 17448960 | tf_op jit(solution)/shard_map/jqk,qjd->kd/dot_general | solution.py:211
  483.2 8.1 %fusion.1 = (f32[4,1024]{1,0:T(4,128)S(1)}, f32[1024,1024,4]{1,0,2:T(8,128)}) fusion(f32[4,1024,1024]{1,2,0:T(8,128)S(1)} %bitcast.273, f32[4,1024]{1,0:T(4,128)S(1)} %get-tuple-element.54, bf16[1024,4,64]{0,2,1:T(8,128)(2,1)S(1)} %bitcast.297, f32[1024,384]{0,1:T(8,128)} %copy-done.12), kind=kOutput, calls=%fused_computation.3 | convolution fusion | flops 549449728 | bytes 34242560 | tf_op jit(solution)/shard_map/qjd,kd->jqk/dot_general | solution.py:206
  491.3 7.8 %fusion.3 = bf16[4,1024,1024]{1,2,0:T(8,128)(2,1)S(1)} fusion(f32[1024,1024,4]{1,0,2:T(8,128)} %get-tuple-element.57, f32[4,1024]{1,0:T(4,128)S(1)} %get-tuple-element.56, f32[4,1024,1024]{1,2,0:T(8,128)S(1)} %bitcast.273, f32[4,1024]{1,0:T(4,128)S(1)} %get-tuple-element.54), kind=kLoop, calls=%fused_computation.5 | loop fusion | flops 16777216 | bytes 41975808 | tf_op jit(solution)/shard_map/convert_element_type | solution.py:208
  499.1 2.7 fusion.49
  504.8 4.3 convolution_convert_fusion
  510.5 9.2 %fusion.31 = f32[2048,1408]{1,0:T(8,128)S(1)} fusion(bf16[1024,2048]{1,0:T(8,128)(2,1)} %all-gather.9.cloned.1.call-done, bf16[1024,704]{1,0:T(8,128)(2,1)} %copy-done.42, bf16[1024,704]{1,0:T(8,128)(2,1)S(1)} %copy-done.41), kind=kOutput, calls=%fused_computation.48 | convolution fusion | flops 5911347200 | bytes 18612224 | tf_op jit(solution)/shard_map/dot_general | solution.py:86
  519.7 4.2 copy-done.5
  523.9 2.2 dynamic-slice_bitcast_fusion.2
  528.8 6.9 convolution_convert_fusion.2
  535.7 23.7 %collective-permute-done.18 = bf16[8,64,1408]{2,1,0:T(8,128)(2,1)} collective-permute-done((bf16[8,64,1408]{2,1,0:T(8,128)(2,1)}, bf16[8,64,1408]{2,1,0:T(8,128)(2,1)}, u32[]{:S(2)}, u32[]{:S(2)}) %collective-permute-start.18) | collective-permute-done | bytes 1441824 | tf_op jit(solution)/shard_map/ppermute | solution.py:55
  559.4 31.9 %collective-permute-done.20 = bf16[8,64,1408]{2,1,0:T(8,128)(2,1)} collective-permute-done((bf16[8,64,1408]{2,1,0:T(8,128)(2,1)}, bf16[8,64,1408]{2,1,0:T(8,128)(2,1)}, u32[]{:S(2)}, u32[]{:S(2)}) %collective-permute-start.20) | collective-permute-done | bytes 1441824 | tf_op jit(solution)/shard_map/ppermute | solution.py:55
  591.2 5.0 fusion.28
  596.2 7.8 %all-to-all-start.3 = ((bf16[8,64,1408]{2,1,0:T(8,128)(2,1)}), bf16[8,64,1408]{2,1,0:T(8,128)(2,1)S(1)}, u32[]{:S(2)}, u32[]{:S(2)}) async-start(bf16[8,64,1408]{2,1,0:T(8,128)(2,1)} %fusion.28), calls=%async_computation.7 | async-start | bytes 2883584 | tf_op jit(solution)/shard_map/all_to_all | solution.py:194
  604.0 5.5 fusion.13
  616.0 15.0 %collective-permute-done.21 = bf16[176,2048]{1,0:T(8,128)(2,1)} collective-permute-done((bf16[176,2048]{1,0:T(8,128)(2,1)}, bf16[176,2048]{1,0:T(8,128)(2,1)}, u32[]{:S(2)}, u32[]{:S(2)}) %collective-permute-start.21) | collective-permute-done | bytes 720928 | tf_op jit(solution)/shard_map/ppermute | solution.py:55
  631.1 15.5 %collective-permute-done.23 = bf16[176,2048]{1,0:T(8,128)(2,1)} collective-permute-done((bf16[176,2048]{1,0:T(8,128)(2,1)}, bf16[176,2048]{1,0:T(8,128)(2,1)}, u32[]{:S(2)}, u32[]{:S(2)}) %collective-permute-start.23) | collective-permute-done | bytes 720928 | tf_op jit(solution)/shard_map/ppermute | solution.py:55
  646.6 3.5 fusion.36
  654.4 2.4 copy.109
  658.5 5.2 fusion.44
  666.6 2.6 fusion.124
  673.1 8.2 %collective-permute-done.14 = bf16[8,64,384]{2,1,0:T(8,128)(2,1)S(1)} collective-permute-done((bf16[8,64,384]{2,1,0:T(8,128)(2,1)S(1)}, bf16[8,64,384]{2,1,0:T(8,128)(2,1)S(1)}, u32[]{:S(2)}, u32[]{:S(2)}) %collective-permute-start.14) | collective-permute-done | bytes 393248 | tf_op jit(solution)/shard_map/ppermute | solution.py:55
  682.3 14.6 %all-to-all-start.2 = ((bf16[8,64,384]{2,1,0:T(8,128)(2,1)}), bf16[8,64,384]{2,1,0:T(8,128)(2,1)S(1)}, u32[]{:S(2)}, u32[]{:S(2)}) async-start(bf16[8,64,384]{2,1,0:T(8,128)(2,1)} %fusion.69), calls=%async_computation.6 | async-start | bytes 786432 | tf_op jit(solution)/shard_map/all_to_all | solution.py:194
  699.7 6.6 all-to-all-done.2
  710.5 39.9 %all-reduce.2 = (f32[2048]{0:T(1024)S(1)}, f32[2048]{0:T(1024)S(1)}) all-reduce(f32[2048]{0:T(1024)S(1)} %get-tuple-element.13, f32[2048]{0:T(1024)S(1)} %get-tuple-element.11), channel_id=9, replica_groups=mesh['ctx'=8,'fsdp'=4] {'ctx','fsdp'}, use_global_device_ids=true, to_apply=%region_14.15.clone | all-reduce | flops 4096 | bytes 32768
  751.6 3.0 fusion.71
  (234 shorter events, 83.2 us)
Async XLA Ops:
  7.2 78.8 %copy-start.24 = (bf16[64,2048]{1,0:T(8,128)(2,1)S(1)}, bf16[64,2048]{1,0:T(8,128)(2,1)}, u32[]{:S(2)}) copy-start(bf16[64,2048]{1,0:T(8,128)(2,1)} %param.18) | copy-start | bytes 786436
  7.2 77.3 %copy-start.34 = (s32[8]{0:T(128)S(1)}, s32[8]{0:T(128)}, u32[]{:S(2)}) copy-start(s32[8]{0:T(128)} %param.13) | copy-start | bytes 100
  7.2 103.5 %all-gather.13.cloned.1.call-start = ((), (), s32[]{:S(2)}) async-start(), calls=%async_computation.14 | async-start | bytes 4718592 | tf_op jit(solution)/shard_map/all_gather | solution.py:125
  8.0 79.7 %collective-permute-start.3 = (bf16[64,2048]{1,0:T(8,128)(2,1)}, bf16[64,2048]{1,0:T(8,128)(2,1)S(1)}, u32[]{:S(2)}, u32[]{:S(2)}) collective-permute-start(bf16[64,2048]{1,0:T(8,128)(2,1)} %param.18), channel_id=1, source_target_pairs={{0,1},{1,0},{2,3},{3,2},{4,5},{5,4},{6,7},{7,6},{8,9},{9,8},{10,11... | collective-permute-start | bytes 786440 | tf_op jit(solution)/shard_map/ppermute | solution.py:55
  9.2 79.2 %collective-permute-start.5 = (bf16[64,2048]{1,0:T(8,128)(2,1)}, bf16[64,2048]{1,0:T(8,128)(2,1)S(1)}, u32[]{:S(2)}, u32[]{:S(2)}) collective-permute-start(bf16[64,2048]{1,0:T(8,128)(2,1)} %param.18), channel_id=1, source_target_pairs={{0,3},{1,2},{2,1},{3,0},{4,7},{5,6},{6,5},{7,4},{8,11},{9,10},{10,... | collective-permute-start | bytes 786440 | tf_op jit(solution)/shard_map/ppermute | solution.py:55
  10.4 77.2 %collective-permute-start.4 = (bf16[64,2048]{1,0:T(8,128)(2,1)}, bf16[64,2048]{1,0:T(8,128)(2,1)S(1)}, u32[]{:S(2)}, u32[]{:S(2)}) collective-permute-start(bf16[64,2048]{1,0:T(8,128)(2,1)} %param.18), channel_id=1, source_target_pairs={{0,2},{1,3},{2,0},{3,1},{4,6},{5,7},{6,4},{7,5},{8,10},{9,11},{10,... | collective-permute-start | bytes 786440 | tf_op jit(solution)/shard_map/ppermute | solution.py:55
  14.5 73.2 %all-to-all-start = ((bf16[8,64,384]{2,1,0:T(8,128)(2,1)}), bf16[8,64,384]{2,1,0:T(8,128)(2,1)S(1)}, u32[]{:S(2)}, u32[]{:S(2)}) async-start(bf16[8,64,384]{2,1,0:T(8,128)(2,1)} %copy.95), calls=%async_computation | async-start | bytes 786432 | tf_op jit(solution)/shard_map/all_to_all | solution.py:118
  21.0 170.2 %reduce-scatter.5.cloned.1.call-start = ((), (), s32[]{:S(2)}) async-start(), calls=%async_computation.8 | async-start | bytes 4718592 | tf_op jit(solution)/shard_map/reduce_scatter | solution.py:169
  84.5 32.5 %copy-start.30 = (f32[32]{0:T(128)}, f32[32]{0:T(128)S(1)}, u32[]{:S(2)}) copy-start(f32[32]{0:T(128)S(1)} %negate_power_fusion) | copy-start | bytes 388
  84.6 32.4 %copy-start.28 = (f32[1024]{0:T(1024)}, f32[1024]{0:T(1024)S(1)}, u32[]{:S(2)}) copy-start(f32[1024]{0:T(1024)S(1)} %get-tuple-element.18) | copy-start | bytes 12292
  85.8 31.7 %copy-start.10 = (f32[1024,32]{0,1:T(8,128)}, f32[1024,32]{0,1:T(8,128)S(1)}, u32[]{:S(2)}) copy-start(f32[1024,32]{0,1:T(8,128)S(1)} %get-tuple-element.53) | copy-start | bytes 393220
  87.7 10.7 %collective-permute-start = (bf16[8,64,384]{2,1,0:T(8,128)(2,1)S(1)}, bf16[8,64,384]{2,1,0:T(8,128)(2,1)S(1)}, u32[]{:S(2)}, u32[]{:S(2)}) collective-permute-start(bf16[8,64,384]{2,1,0:T(8,128)(2,1)S(1)} %all-to-all-done), channel_id=1, source_target_pairs={{0,1},{1,0},{2,3},{3,2},{4,5},{5,4},{6,7},{7,6},{8,9},{9,8},{10,11... | collective-permute-start | bytes 1179656 | tf_op jit(solution)/shard_map/ppermute | solution.py:55
  88.5 22.1 %collective-permute-start.2 = (bf16[8,64,384]{2,1,0:T(8,128)(2,1)S(1)}, bf16[8,64,384]{2,1,0:T(8,128)(2,1)S(1)}, u32[]{:S(2)}, u32[]{:S(2)}) collective-permute-start(bf16[8,64,384]{2,1,0:T(8,128)(2,1)S(1)} %all-to-all-done), channel_id=1, source_target_pairs={{0,3},{1,2},{2,1},{3,0},{4,7},{5,6},{6,5},{7,4},{8,11},{9,10},{10,... | collective-permute-start | bytes 1179656 | tf_op jit(solution)/shard_map/ppermute | solution.py:55
  91.3 19.3 %collective-permute-start.1 = (bf16[8,64,384]{2,1,0:T(8,128)(2,1)S(1)}, bf16[8,64,384]{2,1,0:T(8,128)(2,1)S(1)}, u32[]{:S(2)}, u32[]{:S(2)}) collective-permute-start(bf16[8,64,384]{2,1,0:T(8,128)(2,1)S(1)} %all-to-all-done), channel_id=1, source_target_pairs={{0,2},{1,3},{2,0},{3,1},{4,6},{5,7},{6,4},{7,5},{8,10},{9,11},{10,... | collective-permute-start | bytes 1179656 | tf_op jit(solution)/shard_map/ppermute | solution.py:55
  139.6 51.5 %copy-start = (bf16[1,128,2048]{2,1,0:T(8,128)(2,1)S(1)}, bf16[1,128,2048]{2,1,0:T(8,128)(2,1)}, u32[]{:S(2)}) copy-start(bf16[1,128,2048]{2,1,0:T(8,128)(2,1)} %param.12) | copy-start | bytes 1572868
  139.6 54.9 %copy-start.17 = (bf16[64,5632]{1,0:T(8,128)(2,1)S(1)}, bf16[64,5632]{1,0:T(8,128)(2,1)}, u32[]{:S(2)}) copy-start(bf16[64,5632]{1,0:T(8,128)(2,1)} %param.20) | copy-start | bytes 2162692
  139.7 55.5 %copy-start.18 = (bf16[64,5632]{1,0:T(8,128)(2,1)S(1)}, bf16[64,5632]{1,0:T(8,128)(2,1)}, u32[]{:S(2)}) copy-start(bf16[64,5632]{1,0:T(8,128)(2,1)} %param.21) | copy-start | bytes 2162692
  139.7 195.8 %all-gather.9.cloned.1.call-start = ((), (), s32[]{:S(2)}) async-start(), calls=%async_computation.9 | async-start | bytes 4718592 | tf_op jit(solution)/shard_map/all_gather | solution.py:173
  197.6 68.5 %all-to-all-start.1 = ((bf16[8,64,1408]{2,1,0:T(8,128)(2,1)}), bf16[8,64,1408]{2,1,0:T(8,128)(2,1)S(1)}, u32[]{:S(2)}, u32[]{:S(2)}) async-start(bf16[8,64,1408]{2,1,0:T(8,128)(2,1)} %copy.97), calls=%async_computation.2 | async-start | bytes 2883584 | tf_op jit(solution)/shard_map/all_to_all | solution.py:118
  203.4 143.7 %all-gather.15.cloned.1.call-start = ((), (), s32[]{:S(2)}) async-start(), calls=%async_computation.15 | async-start | bytes 4718592 | tf_op jit(solution)/shard_map/all_gather | solution.py:150
  204.0 216.4 %reduce-scatter.9.cloned.1.call-start = ((), (), s32[]{:S(2)}) async-start(), calls=%async_computation.11 | async-start | bytes 4718592 | tf_op jit(solution)/shard_map/reduce_scatter | solution.py:187
  204.1 17.5 %collective-permute-start.9 = (bf16[176,2048]{1,0:T(8,128)(2,1)S(1)}, bf16[176,2048]{1,0:T(8,128)(2,1)S(1)}, u32[]{:S(2)}, u32[]{:S(2)}) collective-permute-start(bf16[176,2048]{1,0:T(8,128)(2,1)S(1)} %copy-done.19), channel_id=1, source_target_pairs={{0,1},{1,0},{2,3},{3,2},{4,5},{5,4},{6,7},{7,6},{8,9},{9,8},{10,11... | collective-permute-start | bytes 2162696 | tf_op jit(solution)/shard_map/ppermute | solution.py:55
  205.3 65.4 %collective-permute-start.11 = (bf16[176,2048]{1,0:T(8,128)(2,1)S(1)}, bf16[176,2048]{1,0:T(8,128)(2,1)}, u32[]{:S(2)}, u32[]{:S(2)}) collective-permute-start(bf16[176,2048]{1,0:T(8,128)(2,1)S(1)} %copy-done.19), channel_id=1, source_target_pairs={{0,3},{1,2},{2,1},{3,0},{4,7},{5,6},{6,5},{7,4},{8,11},{9,10},{10,... | collective-permute-start | bytes 2162696 | tf_op jit(solution)/shard_map/ppermute | solution.py:55
  206.5 61.0 %collective-permute-start.10 = (bf16[176,2048]{1,0:T(8,128)(2,1)S(1)}, bf16[176,2048]{1,0:T(8,128)(2,1)}, u32[]{:S(2)}, u32[]{:S(2)}) collective-permute-start(bf16[176,2048]{1,0:T(8,128)(2,1)S(1)} %copy-done.19), channel_id=1, source_target_pairs={{0,2},{1,3},{2,0},{3,1},{4,6},{5,7},{6,4},{7,5},{8,10},{9,11},{10,... | collective-permute-start | bytes 2162696 | tf_op jit(solution)/shard_map/ppermute | solution.py:55
  266.1 32.9 %collective-permute-start.6 = (bf16[8,64,1408]{2,1,0:T(8,128)(2,1)S(1)}, bf16[8,64,1408]{2,1,0:T(8,128)(2,1)S(1)}, u32[]{:S(2)}, u32[]{:S(2)}) collective-permute-start(bf16[8,64,1408]{2,1,0:T(8,128)(2,1)S(1)} %all-to-all-done.1), channel_id=1, source_target_pairs={{0,1},{1,0},{2,3},{3,2},{4,5},{5,4},{6,7},{7,6},{8,9},{9,8},{10,11... | collective-permute-start | bytes 4325384 | tf_op jit(solution)/shard_map/ppermute | solution.py:55
  269.6 63.3 %collective-permute-start.7 = (bf16[8,64,1408]{2,1,0:T(8,128)(2,1)S(1)}, bf16[8,64,1408]{2,1,0:T(8,128)(2,1)S(1)}, u32[]{:S(2)}, u32[]{:S(2)}) collective-permute-start(bf16[8,64,1408]{2,1,0:T(8,128)(2,1)S(1)} %all-to-all-done.1), channel_id=1, source_target_pairs={{0,2},{1,3},{2,0},{3,1},{4,6},{5,7},{6,4},{7,5},{8,10},{9,11},{10,... | collective-permute-start | bytes 4325384 | tf_op jit(solution)/shard_map/ppermute | solution.py:55
  272.8 61.4 %collective-permute-start.8 = (bf16[8,64,1408]{2,1,0:T(8,128)(2,1)S(1)}, bf16[8,64,1408]{2,1,0:T(8,128)(2,1)S(1)}, u32[]{:S(2)}, u32[]{:S(2)}) collective-permute-start(bf16[8,64,1408]{2,1,0:T(8,128)(2,1)S(1)} %all-to-all-done.1), channel_id=1, source_target_pairs={{0,3},{1,2},{2,1},{3,0},{4,7},{5,6},{6,5},{7,4},{8,11},{9,10},{10,... | collective-permute-start | bytes 4325384 | tf_op jit(solution)/shard_map/ppermute | solution.py:55
  369.9 50.5 %copy-start.1 = (bf16[128,2048]{1,0:T(8,128)(2,1)S(1)}, bf16[128,2048]{1,0:T(8,128)(2,1)}, u32[]{:S(2)}) copy-start(bf16[128,2048]{1,0:T(8,128)(2,1)} %reduce-scatter.5.cloned.1.call-done) | copy-start | bytes 1572868
  369.9 52.1 %copy-start.4 = (bf16[1,128,2048]{2,1,0:T(8,128)(2,1)S(1)}, bf16[1,128,2048]{2,1,0:T(8,128)(2,1)}, u32[]{:S(2)}) copy-start(bf16[1,128,2048]{2,1,0:T(8,128)(2,1)} %param.23) | copy-start | bytes 1572868
  370.0 100.2 %copy-start.16 = (bf16[4,64,2048]{2,1,0:T(8,128)(2,1)S(1)}, bf16[4,64,2048]{2,1,0:T(8,128)(2,1)}, u32[]{:S(2)}) copy-start(bf16[4,64,2048]{2,1,0:T(8,128)(2,1)} %copy-done.14) | copy-start | bytes 3145732
  370.0 100.2 %all-gather.11.cloned.1.call-start = ((), (), s32[]{:S(2)}) async-start(), calls=%async_computation.12 | async-start | bytes 4718592 | tf_op jit(solution)/shard_map/all_gather | solution.py:203
  424.3 284.7 %reduce-scatter.11.cloned.1.call-start = ((), (), s32[]{:S(2)}) async-start(), calls=%async_computation.13 | async-start | bytes 4718592 | tf_op jit(solution)/shard_map/reduce_scatter | solution.py:216
  509.2 242.4 %reduce-scatter.7.cloned.1.call-start = ((), (), s32[]{:S(2)}) async-start(), calls=%async_computation.10 | async-start | bytes 4718592 | tf_op jit(solution)/shard_map/reduce_scatter | solution.py:181
  526.1 33.2 %collective-permute-start.18 = (bf16[8,64,1408]{2,1,0:T(8,128)(2,1)}, bf16[8,64,1408]{2,1,0:T(8,128)(2,1)}, u32[]{:S(2)}, u32[]{:S(2)}) collective-permute-start(bf16[8,64,1408]{2,1,0:T(8,128)(2,1)} %get-tuple-element.22), channel_id=1, source_target_pairs={{0,1},{1,0},{2,3},{3,2},{4,5},{5,4},{6,7},{7,6},{8,9},{9,8},{10,11... | collective-permute-start | bytes 4325384 | tf_op jit(solution)/shard_map/ppermute | solution.py:55
  527.3 63.9 %collective-permute-start.20 = (bf16[8,64,1408]{2,1,0:T(8,128)(2,1)}, bf16[8,64,1408]{2,1,0:T(8,128)(2,1)}, u32[]{:S(2)}, u32[]{:S(2)}) collective-permute-start(bf16[8,64,1408]{2,1,0:T(8,128)(2,1)} %get-tuple-element.23), channel_id=1, source_target_pairs={{0,3},{1,2},{2,1},{3,0},{4,7},{5,6},{6,5},{7,4},{8,11},{9,10},{10,... | collective-permute-start | bytes 4325384 | tf_op jit(solution)/shard_map/ppermute | solution.py:55
  528.5 62.7 %collective-permute-start.19 = (bf16[8,64,1408]{2,1,0:T(8,128)(2,1)S(1)}, bf16[8,64,1408]{2,1,0:T(8,128)(2,1)}, u32[]{:S(2)}, u32[]{:S(2)}) collective-permute-start(bf16[8,64,1408]{2,1,0:T(8,128)(2,1)S(1)} %get-tuple-element.24), channel_id=1, source_target_pairs={{0,2},{1,3},{2,0},{3,1},{4,6},{5,7},{6,4},{7,5},{8,10},{9,11},{10,... | collective-permute-start | bytes 4325384 | tf_op jit(solution)/shard_map/ppermute | solution.py:55
  596.2 53.9 %all-to-all-start.3 = ((bf16[8,64,1408]{2,1,0:T(8,128)(2,1)}), bf16[8,64,1408]{2,1,0:T(8,128)(2,1)S(1)}, u32[]{:S(2)}, u32[]{:S(2)}) async-start(bf16[8,64,1408]{2,1,0:T(8,128)(2,1)} %fusion.28), calls=%async_computation.7 | async-start | bytes 2883584 | tf_op jit(solution)/shard_map/all_to_all | solution.py:194
  613.4 17.7 %collective-permute-start.21 = (bf16[176,2048]{1,0:T(8,128)(2,1)}, bf16[176,2048]{1,0:T(8,128)(2,1)}, u32[]{:S(2)}, u32[]{:S(2)}) collective-permute-start(bf16[176,2048]{1,0:T(8,128)(2,1)} %get-tuple-element.26), channel_id=1, source_target_pairs={{0,1},{1,0},{2,3},{3,2},{4,5},{5,4},{6,7},{7,6},{8,9},{9,8},{10,11... | collective-permute-start | bytes 2162696 | tf_op jit(solution)/shard_map/ppermute | solution.py:55
  614.6 32.0 %collective-permute-start.23 = (bf16[176,2048]{1,0:T(8,128)(2,1)}, bf16[176,2048]{1,0:T(8,128)(2,1)}, u32[]{:S(2)}, u32[]{:S(2)}) collective-permute-start(bf16[176,2048]{1,0:T(8,128)(2,1)} %get-tuple-element.27), channel_id=1, source_target_pairs={{0,3},{1,2},{2,1},{3,0},{4,7},{5,6},{6,5},{7,4},{8,11},{9,10},{10,... | collective-permute-start | bytes 2162696 | tf_op jit(solution)/shard_map/ppermute | solution.py:55
  614.9 31.7 %collective-permute-start.22 = (bf16[176,2048]{1,0:T(8,128)(2,1)}, bf16[176,2048]{1,0:T(8,128)(2,1)}, u32[]{:S(2)}, u32[]{:S(2)}) collective-permute-start(bf16[176,2048]{1,0:T(8,128)(2,1)} %get-tuple-element.28), channel_id=1, source_target_pairs={{0,2},{1,3},{2,0},{3,1},{4,6},{5,7},{6,4},{7,5},{8,10},{9,11},{10,... | collective-permute-start | bytes 2162696 | tf_op jit(solution)/shard_map/ppermute | solution.py:55
  663.9 8.5 %collective-permute-start.12 = (bf16[8,64,384]{2,1,0:T(8,128)(2,1)S(1)}, bf16[8,64,384]{2,1,0:T(8,128)(2,1)S(1)}, u32[]{:S(2)}, u32[]{:S(2)}) collective-permute-start(bf16[8,64,384]{2,1,0:T(8,128)(2,1)S(1)} %get-tuple-element.29), channel_id=1, source_target_pairs={{0,1},{1,0},{2,3},{3,2},{4,5},{5,4},{6,7},{7,6},{8,9},{9,8},{10,11... | collective-permute-start | bytes 1179656 | tf_op jit(solution)/shard_map/ppermute | solution.py:55
  665.1 16.1 %collective-permute-start.14 = (bf16[8,64,384]{2,1,0:T(8,128)(2,1)S(1)}, bf16[8,64,384]{2,1,0:T(8,128)(2,1)S(1)}, u32[]{:S(2)}, u32[]{:S(2)}) collective-permute-start(bf16[8,64,384]{2,1,0:T(8,128)(2,1)S(1)} %get-tuple-element.30), channel_id=1, source_target_pairs={{0,3},{1,2},{2,1},{3,0},{4,7},{5,6},{6,5},{7,4},{8,11},{9,10},{10,... | collective-permute-start | bytes 1179656 | tf_op jit(solution)/shard_map/ppermute | solution.py:55
  666.3 15.0 %collective-permute-start.13 = (bf16[8,64,384]{2,1,0:T(8,128)(2,1)S(1)}, bf16[8,64,384]{2,1,0:T(8,128)(2,1)S(1)}, u32[]{:S(2)}, u32[]{:S(2)}) collective-permute-start(bf16[8,64,384]{2,1,0:T(8,128)(2,1)S(1)} %get-tuple-element.31), channel_id=1, source_target_pairs={{0,2},{1,3},{2,0},{3,1},{4,6},{5,7},{6,4},{7,5},{8,10},{9,11},{10,... | collective-permute-start | bytes 1179656 | tf_op jit(solution)/shard_map/ppermute | solution.py:55
  670.1 26.8 %collective-permute-start.15 = (bf16[64,2048]{1,0:T(8,128)(2,1)}, bf16[64,2048]{1,0:T(8,128)(2,1)S(1)}, u32[]{:S(2)}, u32[]{:S(2)}) collective-permute-start(bf16[64,2048]{1,0:T(8,128)(2,1)} %get-tuple-element.38), channel_id=1, source_target_pairs={{0,1},{1,0},{2,3},{3,2},{4,5},{5,4},{6,7},{7,6},{8,9},{9,8},{10,11... | collective-permute-start | bytes 786440 | tf_op jit(solution)/shard_map/ppermute | solution.py:55
  671.3 25.6 %collective-permute-start.17 = (bf16[64,2048]{1,0:T(8,128)(2,1)}, bf16[64,2048]{1,0:T(8,128)(2,1)S(1)}, u32[]{:S(2)}, u32[]{:S(2)}) collective-permute-start(bf16[64,2048]{1,0:T(8,128)(2,1)} %get-tuple-element.39), channel_id=1, source_target_pairs={{0,3},{1,2},{2,1},{3,0},{4,7},{5,6},{6,5},{7,4},{8,11},{9,10},{10,... | collective-permute-start | bytes 786440 | tf_op jit(solution)/shard_map/ppermute | solution.py:55
  672.4 24.5 %collective-permute-start.16 = (bf16[64,2048]{1,0:T(8,128)(2,1)S(1)}, bf16[64,2048]{1,0:T(8,128)(2,1)S(1)}, u32[]{:S(2)}, u32[]{:S(2)}) collective-permute-start(bf16[64,2048]{1,0:T(8,128)(2,1)S(1)} %get-tuple-element.40), channel_id=1, source_target_pairs={{0,2},{1,3},{2,0},{3,1},{4,6},{5,7},{6,4},{7,5},{8,10},{9,11},{10,... | collective-permute-start | bytes 786440 | tf_op jit(solution)/shard_map/ppermute | solution.py:55
  682.3 24.0 %all-to-all-start.2 = ((bf16[8,64,384]{2,1,0:T(8,128)(2,1)}), bf16[8,64,384]{2,1,0:T(8,128)(2,1)S(1)}, u32[]{:S(2)}, u32[]{:S(2)}) async-start(bf16[8,64,384]{2,1,0:T(8,128)(2,1)} %fusion.69), calls=%async_computation.6 | async-start | bytes 786432 | tf_op jit(solution)/shard_map/all_to_all | solution.py:194
  697.6 53.9 %copy-start.3 = (bf16[128,2048]{1,0:T(8,128)(2,1)S(1)}, bf16[128,2048]{1,0:T(8,128)(2,1)}, u32[]{:S(2)}) copy-start(bf16[128,2048]{1,0:T(8,128)(2,1)} %reduce-scatter.9.cloned.1.call-done) | copy-start | bytes 1572868
  (35 other events, 211.5 us)
Sparse Core Ops, SparseCore 0:
  9.7 53.6 all-gather.12
  139.8 51.3 reduce-scatter.4
  194.6 72.7 all-gather.8
  268.9 49.3 all-gather.14
  370.1 50.3 reduce-scatter.8
  424.4 45.6 all-gather.10
  509.3 48.6 reduce-scatter.10
  560.2 49.0 reduce-scatter.6

commit v2 on v1

v2 whole, which is shorter than its diff:
```python
import functools

import jax
import jax.numpy as jnp
from jax import lax
from jax.experimental import pallas as pl
from jax.experimental.pallas import tpu as pltpu
from jax.sharding import PartitionSpec as P

H = 32
KVH = 4
HD = 64

EPS = 1e-05
THETA = 10000.0
BF = jnp.bfloat16
F32 = jnp.float32
FFN_ROWS = 256


def rms_parts(values):
    recip = lax.rsqrt(jnp.mean(values * values, axis=-1, keepdims=True) + EPS)
    return (values * recip, recip)


def norm_back(grad_in, normed, recip):
    return recip * (grad_in - normed * jnp.mean(grad_in * normed, axis=-1, keepdims=True))


def positions(block_order, row_count, tok_rows, ctx_count):
    row_ids = jnp.arange(row_count, dtype=jnp.int32)
    owner_index = row_ids // tok_rows
    within = row_ids % tok_rows
    half_rows = tok_rows // 2
    match = owner_index[:, None] == jnp.arange(ctx_count, dtype=jnp.int32)[None, :]
    paired = jnp.sum(jnp.where(match, block_order[None, :], 0), axis=1)
    block_id = jnp.where(within < half_rows, paired, 2 * ctx_count - 1 - paired)
    return block_id * half_rows + within % half_rows


def rope_tables(pos):
    freqs = THETA ** (-(jnp.arange(HD // 2, dtype=F32) * 2.0 / HD))
    angles = pos.astype(F32)[:, None] * freqs[None, :]
    return (jnp.cos(angles)[:, None, :], jnp.sin(angles)[:, None, :])


def turn(values):
    return jnp.concatenate([values[..., HD // 2 :], -values[..., : HD // 2]], axis=-1)


def rotate(values, cos_table, sin_table):
    first_half = values[..., : HD // 2]
    second_half = values[..., HD // 2 :]
    return jnp.concatenate(
        [
            first_half * cos_table - second_half * sin_table,
            second_half * cos_table + first_half * sin_table,
        ],
        axis=-1,
    )


def after(value, *others):
    return lax.optimization_barrier((value,) + others)[0]


def swap_f(value, step, f_count):
    return lax.ppermute(value, "fsdp", [(i, i ^ step) for i in range(f_count)])


def swap_core(value, c_count):
    return lax.ppermute(value, "ctx", [(i, i ^ 1) for i in range(c_count)])


def pick(stack, index, axis=0):
    return lax.dynamic_index_in_dim(stack, index, axis, keepdims=False)


def place_f(pieces, axis, f_index):
    value = pieces[0]
    shape = value.shape[:axis] + (len(pieces),) + value.shape[axis:]
    out = jnp.zeros(shape, value.dtype)
    for step, piece in enumerate(pieces):
        out = lax.dynamic_update_index_in_dim(out, piece, f_index ^ step, axis)
    return out


def fetch_f(value, f_count):
    return [value] + [swap_f(value, step, f_count) for step in range(1, f_count)]


def send_f(parts, axis, f_index, f_count):
    pieces = []
    for step in range(f_count):
        piece = pick(parts, f_index ^ step, axis)
        pieces.append(swap_f(piece, step, f_count) if step else piece)
    return pieces


def total_f(pieces, *others):
    return sum(after(piece, *others).astype(F32) for piece in pieces)


def gather_c(rows):
    return lax.all_gather(rows, "ctx", axis=0, tiled=True)


def scatter_c(full):
    return lax.psum_scatter(full, "ctx", scatter_dimension=0, tiled=True)


def exchange_z(blocks, c_count):
    groups = [list(range(core, c_count, 2)) for core in range(2)]
    return lax.all_to_all(
        blocks, "ctx", split_axis=0, concat_axis=0, tiled=True, axis_index_groups=groups
    )


def pair_sum(full, c_count):
    core = lax.axis_index("ctx") % 2
    parts = full.reshape(c_count // 2, 2, full.shape[0] // c_count, full.shape[1])
    got = swap_core(pick(parts, 1 - core, 1), c_count)
    return (pick(parts, core, 1).astype(F32) + got.astype(F32)).astype(BF)


def dot(a, b):
    return jnp.dot(a, b, preferred_element_type=F32)


def dot_nt(a, b):
    return lax.dot_general(a, b, (((1,), (1,)), ((), ())), preferred_element_type=F32)


def dot_tn(a, b):
    return lax.dot_general(a, b, (((0,), (0,)), ((), ())), preferred_element_type=F32)


def halves_of(value, half):
    rows, cols = value.shape
    blocks = value.reshape(rows // (2 * half), 2, half, cols)
    return [blocks[:, i].reshape(rows // 2, cols) for i in range(2)]


def merge_halves(first, second, half):
    rows, cols = first.shape
    blocks = [v.reshape(rows // half, 1, half, cols) for v in (first, second)]
    return jnp.concatenate(blocks, axis=1).reshape(2 * rows, cols)


def soft_parts(q_pair, k_pair, cols, rows_pos):
    scale = HD ** (-0.5)
    s_aa = jnp.where(rows_pos[0] <= cols[0], dot_nt(q_pair[0], k_pair[0]) * scale, -jnp.inf)
    s_ba = dot_nt(q_pair[1], k_pair[0]) * scale
    s_bb = jnp.where(rows_pos[1] <= cols[1], dot_nt(q_pair[1], k_pair[1]) * scale, -jnp.inf)
    m_a = jnp.max(s_aa, axis=1, keepdims=True)
    m_b = jnp.maximum(jnp.max(s_ba, axis=1, keepdims=True), jnp.max(s_bb, axis=1, keepdims=True))
    e_aa, e_ba, e_bb = jnp.exp(s_aa - m_a), jnp.exp(s_ba - m_b), jnp.exp(s_bb - m_b)
    r_a = 1.0 / jnp.sum(e_aa, axis=1, keepdims=True)
    r_b = 1.0 / (jnp.sum(e_ba, axis=1, keepdims=True) + jnp.sum(e_bb, axis=1, keepdims=True))
    return e_aa * r_a, e_ba * r_b, e_bb * r_b


def attend_kernel(half, q_ref, k_ref, v_ref, col_ref, row_ref, o_ref):
    cols = halves_of(col_ref[...], half)
    rows_pos = [row_ref[0:1], row_ref[1:2]]
    k_pair, v_pair = halves_of(k_ref[...], half), halves_of(v_ref[...], half)
    outs = []
    for j in range(q_ref.shape[1] // HD):
        q_pair = halves_of(q_ref[:, j * HD : (j + 1) * HD], half)
        p_aa, p_ba, p_bb = soft_parts(q_pair, k_pair, cols, rows_pos)
        o_a = dot(p_aa.astype(BF), v_pair[0])
        o_b = dot(p_ba.astype(BF), v_pair[0]) + dot(p_bb.astype(BF), v_pair[1])
        outs.append(merge_halves(o_a.astype(BF), o_b.astype(BF), half))
    o_ref[...] = jnp.concatenate(outs, axis=1)


def attend_back_kernel(half, q_ref, k_ref, v_ref, do_ref, kr_ref, qr_ref, cos_ref, sin_ref, col_ref, row_ref, dq_ref, dk_ref, dv_ref, acc_ref):
    scale = HD ** (-0.5)
    cols = halves_of(col_ref[...], half)
    rows_pos = [row_ref[0:1], row_ref[1:2]]
    k_pair, v_pair = halves_of(k_ref[...], half), halves_of(v_ref[...], half)
    kr_pair = halves_of(kr_ref[...], half)
    kk = [jnp.concatenate([k_pair[i], kr_pair[i]], axis=1) for i in range(2)]
    cos_pair, sin_pair = halves_of(cos_ref[...], half), halves_of(sin_ref[...], half)

    @pl.when(pl.program_id(0) == 0)
    def _():
        acc_ref[...] = jnp.zeros_like(acc_ref)

    dqs = []
    for j in range(q_ref.shape[1] // HD):
        lanes = slice(j * HD, (j + 1) * HD)
        q_pair = halves_of(q_ref[:, lanes], half)
        do_pair = halves_of(do_ref[:, lanes], half)
        qr_pair = halves_of(qr_ref[:, lanes], half)
        qq = [jnp.concatenate([q_pair[i], qr_pair[i]], axis=1) for i in range(2)]
        p_aa, p_ba, p_bb = soft_parts(q_pair, k_pair, cols, rows_pos)
        g_aa = dot_nt(do_pair[0], v_pair[0])
        g_ba = dot_nt(do_pair[1], v_pair[0])
        g_bb = dot_nt(do_pair[1], v_pair[1])
        d_a = jnp.sum(p_aa * g_aa, axis=1, keepdims=True)
        d_b = jnp.sum(p_ba * g_ba, axis=1, keepdims=True) + jnp.sum(p_bb * g_bb, axis=1, keepdims=True)
        s_aa = (p_aa * (g_aa - d_a)).astype(BF)
        s_ba = (p_ba * (g_ba - d_b)).astype(BF)
        s_bb = (p_bb * (g_bb - d_b)).astype(BF)
        dq_pair = [dot(s_aa, kk[0]), dot(s_ba, kk[0]) + dot(s_bb, kk[1])]
        out = []
        for i in range(2):
            d = dq_pair[i] * scale
            out.append((d[:, :HD] * cos_pair[i] + d[:, HD:] * sin_pair[i]).astype(BF))
        dqs.append(merge_halves(out[0], out[1], half))
        acc_ref[0, :, : 2 * HD] += dot_tn(s_aa, qq[0]) + dot_tn(s_ba, qq[1])
        acc_ref[1, :, : 2 * HD] += dot_tn(s_bb, qq[1])
        acc_ref[0, :, 2 * HD : 3 * HD] += dot_tn(p_aa.astype(BF), do_pair[0]) + dot_tn(p_ba.astype(BF), do_pair[1])
        acc_ref[1, :, 2 * HD : 3 * HD] += dot_tn(p_bb.astype(BF), do_pair[1])
    dq_ref[...] = jnp.concatenate(dqs, axis=1)

    @pl.when(pl.program_id(0) == pl.num_programs(0) - 1)
    def _():
        dk = []
        for i in range(2):
            d = acc_ref[i, :, : 2 * HD] * scale
            dk.append((d[:, :HD] * cos_pair[i] + d[:, HD:] * sin_pair[i]).astype(BF))
        dk_ref[...] = merge_halves(dk[0], dk[1], half)
        dv_ref[...] = merge_halves(acc_ref[0, :, 2 * HD : 3 * HD].astype(BF), acc_ref[1, :, 2 * HD : 3 * HD].astype(BF), half)


def whole(shape):
    return pl.BlockSpec(shape, lambda g: (0,) * len(shape))


def attend(q, k, v, col, row, half):
    seq, q_cols = q.shape
    by_pair = pl.BlockSpec((seq, 2 * HD), lambda g: (0, g))
    return pl.pallas_call(
        functools.partial(attend_kernel, half),
        grid=(q_cols // (2 * HD),),
        in_specs=[by_pair, whole(k.shape), whole(v.shape), whole(col.shape), whole(row.shape)],
        out_specs=by_pair,
        out_shape=jax.ShapeDtypeStruct((seq, q_cols), BF),
        compiler_params=pltpu.CompilerParams(vmem_limit_bytes=56 * 2**20),
    )(q, k, v, col, row)


def attend_back(q, k, v, do, kr, qr, cos, sin, col, row, half):
    seq, q_cols = q.shape
    by_pair = pl.BlockSpec((seq, 2 * HD), lambda g: (0, g))
    return pl.pallas_call(
        functools.partial(attend_back_kernel, half),
        grid=(q_cols // (2 * HD),),
        in_specs=[by_pair, whole(k.shape), whole(v.shape), by_pair, whole(kr.shape), by_pair, whole(cos.shape), whole(sin.shape), whole(col.shape), whole(row.shape)],
        out_specs=[by_pair, whole(k.shape), whole(v.shape)],
        out_shape=[jax.ShapeDtypeStruct((seq, q_cols), BF), jax.ShapeDtypeStruct(k.shape, BF), jax.ShapeDtypeStruct(v.shape, BF)],
        scratch_shapes=[pltpu.VMEM((2, seq // 2, 4 * HD), F32)],
        compiler_params=pltpu.CompilerParams(vmem_limit_bytes=56 * 2**20),
    )(q, k, v, do, kr, qr, cos, sin, col, row)


def ffn_kernel(h_ref, g_ref, wgu_ref, wd_ref, z_ref, dgu_ref, out_ref, dh_ref):
    ff = z_ref.shape[1]
    gu = dot(h_ref[...], wgu_ref[...])
    gate, up = gu[:, :ff], gu[:, ff:]
    sig = 1.0 / (1.0 + jnp.exp(-gate))
    act = gate * sig
    z = (act * up).astype(BF)
    z_ref[...] = z
    dz = dot_nt(g_ref[...], wd_ref[...])
    dub = (dz * act).astype(BF)
    dgb = (dz * up * (sig * (1.0 + gate * (1.0 - sig)))).astype(BF)
    dgu = jnp.concatenate([dgb, dub], axis=1)
    dgu_ref[...] = dgu
    dh_ref[...] = dot_nt(dgu, wgu_ref[...]).astype(BF)
    out_ref[...] = dot(z, wd_ref[...]).astype(BF)


def ffn(h, g, w_gu, w_d, block):
    seq, width = h.shape
    ff = w_d.shape[0]
    rows = pl.BlockSpec((block, width), lambda i: (i, 0))
    return pl.pallas_call(
        ffn_kernel,
        grid=(seq // block,),
        in_specs=[rows, rows, whole(w_gu.shape), whole(w_d.shape)],
        out_specs=[pl.BlockSpec((block, ff), lambda i: (i, 0)), pl.BlockSpec((block, 2 * ff), lambda i: (i, 0)), rows, rows],
        out_shape=[jax.ShapeDtypeStruct((seq, ff), BF), jax.ShapeDtypeStruct((seq, 2 * ff), BF), jax.ShapeDtypeStruct((seq, width), BF), jax.ShapeDtypeStruct((seq, width), BF)],
        compiler_params=pltpu.CompilerParams(vmem_limit_bytes=56 * 2**20),
    )(h, g, w_gu, w_d)


def on_device(
    tokens,
    block_order,
    norm_attn,
    w_query,
    w_key,
    w_value,
    w_out,
    norm_ffn,
    w_gate,
    w_up,
    w_down,
    cotangent,
):
    c_count = lax.axis_size("ctx")
    f_count = lax.axis_size("fsdp")
    f_index = lax.axis_index("fsdp")
    tok_rows = tokens.shape[1]
    width = tokens.shape[2]
    seq = tok_rows * c_count
    half = tok_rows // 2
    heads = H // c_count
    share = c_count // KVH
    q_cols = heads * HD
    a_cols = q_cols + 2 * HD
    rows = w_query.shape[0]
    ff_cols = w_gate.shape[1] // c_count

    def to_dest(packed):
        return lax.all_to_all(packed, "ctx", split_axis=0, concat_axis=0, tiled=True)

    def by_dest(w):
        return w.reshape(rows, c_count, -1).transpose(1, 0, 2)

    def kv_dest(w):
        return jnp.repeat(w.reshape(rows, KVH, HD).transpose(1, 0, 2), share, axis=0)

    pos = positions(block_order, seq, tok_rows, c_count)
    cos_table, sin_table = rope_tables(pos)
    cos_wide = jnp.concatenate([cos_table, cos_table], axis=2)[:, 0]
    sin_wide = jnp.concatenate([sin_table, sin_table], axis=2)[:, 0]
    pos_col = pos[:, None]
    pos_row = pos.reshape(c_count, 2, half).transpose(1, 0, 2).reshape(2, seq // 2)
    x_all = gather_c(tokens[0])
    gain_pack = jnp.pad(jnp.stack([norm_attn, norm_ffn], axis=1), ((0, 0), (0, 126)))
    qkv_pack = jnp.concatenate(
        [
            by_dest(w_query),
            kv_dest(w_key),
            kv_dest(w_value),
            jnp.broadcast_to(gain_pack[None], (c_count, rows, 128)),
        ],
        axis=2,
    )
    moved_qkv = to_dest(qkv_pack)
    d_pieces = fetch_f(w_down, f_count)
    w_qkvg = place_f(fetch_f(after(moved_qkv, *d_pieces), f_count), 1, f_index).reshape(width, a_cols + 128)
    w_qkv = w_qkvg[:, :a_cols]
    unit = jnp.eye(8, 128, dtype=BF)
    gains = dot_nt(unit, w_qkvg[:, a_cols:])
    gain_a = gains[0]
    gain_f = gains[1]
    w_o = place_f(fetch_f(w_out, f_count), 0, f_index).reshape(f_count * rows, width)
    moved_gu = to_dest(after(jnp.concatenate([by_dest(w_gate), by_dest(w_up)], axis=2), moved_qkv))
    gu_pieces = fetch_f(moved_gu, f_count)

    x_seen = after(x_all, w_qkvg, w_o, moved_gu, cos_wide, sin_wide, pos_col, pos_row)
    normed_all, _ = rms_parts(x_seen.astype(F32))
    h1 = (normed_all * gain_a).astype(BF)
    g_all = gather_c(after(cotangent[0], h1))
    qkv = dot(h1, w_qkv)
    q = rotate(qkv[:, :q_cols].reshape(seq, heads, HD), cos_table, sin_table).astype(BF)
    k = rotate(qkv[:, None, q_cols : q_cols + HD], cos_table, sin_table).astype(BF)
    q_turn = turn(q).reshape(seq, q_cols)
    k_turn = turn(k)[:, 0]
    q = q.reshape(seq, q_cols)
    k = k[:, 0]
    v = qkv[:, q_cols + HD :].astype(BF)
    o = attend(q, k, v, pos_col, pos_row, half)
    y_part = dot(o, w_o).astype(BF)
    y_rows = scatter_c(after(y_part, g_all, *gu_pieces[:3]))

    source = tokens[0].astype(F32)
    residual = source + y_rows.astype(F32)
    normed_f, recip_f = rms_parts(residual)
    w_d = place_f(d_pieces, 0, f_index).reshape(ff_cols, width)
    w_gu = place_f(gu_pieces, 1, f_index).reshape(width, 2 * ff_cols)
    h2_rows = after((normed_f * gain_f).astype(BF), w_gu, w_d)
    h2 = gather_c(h2_rows)

    z, dgu, out_part, dh2_part = ffn(h2, g_all, w_gu, w_d, FFN_ROWS)
    dh2 = scatter_c(dh2_part)
    grad_gu_low = dot_tn(after(h2, dh2_part), dgu).astype(BF)
    sent_gu = send_f(grad_gu_low.reshape(c_count, f_count, rows, -1), 1, f_index, f_count)
    grad_down_low = dot_tn(z, after(g_all, grad_gu_low)).astype(BF)
    sent_down = send_f(grad_down_low.reshape(f_count, -1, width), 0, f_index, f_count)
    out_mine = pair_sum(out_part, c_count)

    out_blocks = exchange_z(out_mine, c_count)
    d_h = after(dh2, grad_down_low, out_blocks, *sent_gu).astype(F32)
    gain_terms_f = jnp.sum(d_h * normed_f, axis=0)
    d_res = cotangent[0].astype(F32) + norm_back(d_h * gain_f, normed_f, recip_f)
    ab_rows = d_res.astype(BF)
    ab = gather_c(ab_rows)
    sum_gu = total_f(sent_gu, ab_rows).astype(BF)
    shard_down = total_f(sent_down, sum_gu)
    out_sum = jnp.sum(after(out_blocks, ab_rows).astype(F32), axis=0)
    result = (residual + out_sum).astype(BF)
    ab = after(ab, sum_gu, shard_down, result)

    d_o = dot_nt(ab, w_o).astype(BF)
    owned_gu = to_dest(after(sum_gu, d_o))
    dq, dk, dv = attend_back(
        q, k, v, d_o, k_turn, q_turn, cos_wide, sin_wide, pos_col, pos_row, half
    )
    dqkv = jnp.concatenate([dq, dk, dv], axis=1)
    dh1_part = dot_nt(dqkv, w_qkv)
    dh1_low = after(dh1_part.astype(BF), owned_gu)
    dh1 = scatter_c(dh1_low)
    gain_terms_a = jnp.sum(dh1_part * normed_all, axis=0)

    terms = jnp.stack([gain_terms_a, gain_terms_f])
    high = terms.astype(BF)
    low = (terms - high.astype(F32)).astype(BF)
    gain_cols = dot_tn(jnp.concatenate([high, low]), jnp.eye(4, 128, dtype=BF)).astype(BF)
    grad_qkv_low = jnp.concatenate([dot_tn(after(h1, dh1_low), dqkv).astype(BF), gain_cols], axis=1)
    sent_qkv = send_f(grad_qkv_low.reshape(c_count, f_count, rows, -1), 1, f_index, f_count)
    grad_out_low = dot_tn(after(o, grad_qkv_low), ab).astype(BF)
    sent_out = send_f(grad_out_low.reshape(f_count, rows, width), 0, f_index, f_count)
    owned_qkv = to_dest(total_f(sent_qkv, owned_gu).astype(BF))
    shard_out = total_f(sent_out)
    shard_gate = owned_gu[:, :, :ff_cols].transpose(1, 0, 2).reshape(rows, -1).astype(F32)
    shard_up = owned_gu[:, :, ff_cols:].transpose(1, 0, 2).reshape(rows, -1).astype(F32)
    shard_query = owned_qkv[:, :, :q_cols].transpose(1, 0, 2).reshape(rows, -1).astype(F32)
    grad_kv = jnp.sum(
        owned_qkv[:, :, q_cols:a_cols].reshape(KVH, share, rows, 2 * HD).astype(F32), axis=1
    )
    shard_key = grad_kv[:, :, :HD].transpose(1, 0, 2).reshape(rows, -1)
    shard_value = grad_kv[:, :, HD:].transpose(1, 0, 2).reshape(rows, -1)
    gain_sums = jnp.sum(owned_qkv[:, :, a_cols : a_cols + 4].astype(F32), axis=0)

    normed_a, recip_a = rms_parts(source)
    grads = d_res + norm_back(dh1.astype(F32) * gain_a, normed_a, recip_a)
    return (
        result[None],
        grads.astype(BF)[None],
        gain_sums[:, 0] + gain_sums[:, 2],
        shard_query,
        shard_key,
        shard_value,
        shard_out,
        gain_sums[:, 1] + gain_sums[:, 3],
        shard_gate,
        shard_up,
        shard_down,
    )


def solution(mesh):
    both = ("ctx", "fsdp")
    row = P(both, None)
    in_specs = (
        P("fsdp", "ctx", None),
        P(),
        P(both),
        row,
        row,
        row,
        row,
        P(both),
        row,
        row,
        row,
        P("fsdp", "ctx", None),
    )
    out_specs = (
        P("fsdp", "ctx", None),
        P("fsdp", "ctx", None),
        P(both),
        row,
        row,
        row,
        row,
        P(both),
        row,
        row,
        row,
    )
    return jax.shard_map(
        on_device, mesh=mesh, in_specs=in_specs, out_specs=out_specs, check_vma=False
    )
```

time: 773 us -> 556 us (0.72)
  waiting for transfers between devices: 377 us -> 251 us
  blocking collectives: 103 us -> 0 us
  matrix products: 113 us -> 42.6 us
  Pallas kernels: 0 us -> 50.9 us
  other arithmetic: 41.9 us -> 57.5 us
  starting transfers between devices: 59.4 us -> 68.8 us
  local copies, waits for them, and re-layouts: 51.6 us -> 59.9 us
    reduce_scatter x4 -> x3, waiting for transfers between devices: 101 us -> 6.44 us  [scatter_c(): return lax.psum_scatter(full, 'ctx', scatter_dimension=0, tiled=True)]
    all_gather x1 -> x0, blocking collectives: 63.3 us -> none  [on_device(): lax.all_gather(jnp.concatenate([norm_attn, norm_ffn])[None], ('ctx', 'fsd...]
    pallas_call x0 -> x3, Pallas kernels: none -> 50.9 us  [the longest x1 26.8 us: ffn(): pl.pallas_call(ffn_kernel, grid=(seq // block,), in_specs=[rows, rows, wh...]
    unnamed x1 -> x0, blocking collectives: 39.9 us -> none
    dot_general x5 -> x0, matrix products: 28.4 us -> none  [the longest x1 8.59 us: on_device(): dv = jnp.einsum('jqk,qjd->kd', prob_low, d_o, preferred_element_type=F32)]
    all_to_all x4 -> x5, waiting for transfers between devices: 50.2 us -> 28.7 us  [the longest x4 28.7 us: to_dest(): lax.all_to_all(packed, 'ctx', split_axis=0, concat_axis=0, tiled=True)]
    ppermute x24, waiting for transfers between devices: 179 us -> 159 us  [swap_f(): return lax.ppermute(value, 'fsdp', [(i, i ^ step) for i in range(f_count)])]
    dot_general x4 -> x3, matrix products: 29.1 us -> 10.7 us  [dot_nt(): lax.dot_general(a, b, (((1,), (1,)), ((), ())), preferred_element_type=F32)]
  transfers between devices with their start and end apart: 36 -> 37, of which waited for: 15 -> 20; matrix products, arithmetic and copies ran while one was open for 13% -> 24% of each run, Pallas kernels for 0% -> 4%
where the time goes in v2:
time: 556 us; the launch traced here: 546 us
  waiting for transfers between devices  251 us (45%)
  starting transfers between devices  68.8 us (12%)
  local copies, waits for them, and re-layouts  59.9 us (11%)
  other arithmetic  57.5 us (10%)
  Pallas kernels  50.9 us (9%)
  matrix products  42.6 us (8%)
  between operations  15.4 us (3%)
    ppermute x24, waiting for transfers between devices, swap_f(): return lax.ppermute(value, 'fsdp', [(i, i ^ step) for i in range(f_count)])  159 us
    all_gather x4, waiting for transfers between devices, gather_c(): return lax.all_gather(rows, 'ctx', axis=0, tiled=True)  52.2 us
    all_to_all x4, waiting for transfers between devices, to_dest(): lax.all_to_all(packed, 'ctx', split_axis=0, concat_axis=0, tiled=True)  28.7 us
    all_to_all x4, starting transfers between devices, to_dest(): lax.all_to_all(packed, 'ctx', split_axis=0, concat_axis=0, tiled=True)  27 us
    pallas_call x1, Pallas kernels, ffn(): pl.pallas_call(ffn_kernel, grid=(seq // block,), in_specs=[rows, rows, wh...  26.8 us
    ppermute x24, starting transfers between devices, swap_f(): return lax.ppermute(value, 'fsdp', [(i, i ^ step) for i in range(f_count)])  23.5 us
    dot_general x5, matrix products, dot_tn(): lax.dot_general(a, b, (((0,), (0,)), ((), ())), preferred_element_type=F32)  23.1 us
    dynamic_update_slice x16, local copies, waits for them, and re-layouts, place_f(): out = lax.dynamic_update_index_in_dim(out, piece, f_index ^ step, axis)  16.9 us
  transfers between devices with their start and end apart: 37, of which 20 were waited for; matrix products, arithmetic and copies ran while one was open for 24% of the time, Pallas kernels for 4%

profile of v2, /device:TPU:9, one launch (start us, length us, event | category | flops | bytes accessed | tf_op | source)
XLA Modules:
  0.0 546.5 jit_solution(99846966404085595)
XLA Ops:
  18.0 7.1 %all-to-all-start = ((bf16[8,64,512]{2,1,0:T(8,128)(2,1)}), bf16[8,64,512]{2,1,0:T(8,128)(2,1)S(1)}, u32[]{:S(2)}, u32[]{:S(2)}) async-start(bf16[8,64,512]{2,1,0:T(8,128)(2,1)} %copy.132), calls=%async_computation | async-start | bytes 1048576 | tf_op jit(solution)/shard_map/all_to_all | solution.py:319
  35.0 15.5 %all-to-all-done = bf16[8,64,512]{2,1,0:T(8,128)(2,1)S(1)} async-done(((bf16[8,64,512]{2,1,0:T(8,128)(2,1)}), bf16[8,64,512]{2,1,0:T(8,128)(2,1)S(1)}, u32[]{:S(2)}, u32[]{:S(2)}) %all-to-all-start) | async-done | bytes 524320 | tf_op jit(solution)/shard_map/all_to_all | solution.py:319
  50.5 7.8 %all-to-all-start.1 = ((bf16[8,64,1408]{2,1,0:T(8,128)(2,1)}), bf16[8,64,1408]{2,1,0:T(8,128)(2,1)S(1)}, u32[]{:S(2)}, u32[]{:S(2)}) async-start(bf16[8,64,1408]{2,1,0:T(8,128)(2,1)} %pad_maximum_fusion.1), calls=%async_computation.1 | async-start | bytes 2883584 | tf_op jit(solution)/shard_map/all_to_all | solution.py:319
  62.4 11.0 %collective-permute-done.3 = bf16[8,64,512]{2,1,0:T(8,128)(2,1)S(1)} collective-permute-done((bf16[8,64,512]{2,1,0:T(8,128)(2,1)S(1)}, bf16[8,64,512]{2,1,0:T(8,128)(2,1)S(1)}, u32[]{:S(2)}, u32[]{:S(2)}) %collective-permute-start.3) | collective-permute-done | bytes 524320 | tf_op jit(solution)/shard_map/ppermute | solution.py:68
  73.5 11.1 %collective-permute-done.5 = bf16[8,64,512]{2,1,0:T(8,128)(2,1)S(1)} collective-permute-done((bf16[8,64,512]{2,1,0:T(8,128)(2,1)S(1)}, bf16[8,64,512]{2,1,0:T(8,128)(2,1)S(1)}, u32[]{:S(2)}, u32[]{:S(2)}) %collective-permute-start.5) | collective-permute-done | bytes 524320 | tf_op jit(solution)/shard_map/ppermute | solution.py:68
  85.9 9.5 %all-to-all-done.1 = bf16[8,64,1408]{2,1,0:T(8,128)(2,1)S(1)} async-done(((bf16[8,64,1408]{2,1,0:T(8,128)(2,1)}), bf16[8,64,1408]{2,1,0:T(8,128)(2,1)S(1)}, u32[]{:S(2)}, u32[]{:S(2)}) %all-to-all-start.1) | async-done | bytes 1441824 | tf_op jit(solution)/shard_map/all_to_all | solution.py:319
  95.4 3.2 fusion.4
  98.9 3.1 fusion.2
  105.3 4.5 fusion.8
  114.6 3.0 fusion.60
  118.5 8.8 %shard_map.203 = bf16[1024,256]{1,0:T(8,128)(2,1)} custom-call(bf16[1024,256]{1,0:T(8,128)(2,1)} %copy.140.q_ref, bf16[1024,64]{1,0:T(8,128)(2,1)} %pad_maximum_fusion.5.k_ref, bf16[1024,64]{1,0:T(8,128)(2,1)} %copy.162.v_ref, s32[1024,1]{1,0:T(8,128)} %fusion.26.col_ref, s32[2,512]{1,0:T(2,128)} %reshape.375.row_ref), custom_call_target="tpu_custom_call" | custom-call | tf_op jit(solution)/shard_map/pallas_call | solution.py:235
  127.2 4.3 convolution_convert_fusion.1
  131.5 4.2 collective-permute-done.10
  136.7 13.1 %all-gather.6.cloned.1.call-done.g_ref = bf16[1024,2048]{1,0:T(8,128)(2,1)} async-done(((bf16[128,2048]{1,0:T(8,128)(2,1)}), bf16[1024,2048]{1,0:T(8,128)(2,1)}) %all-gather.6.cloned.1.call-update) | async-done | bytes 4194320 | tf_op jit(solution)/shard_map/all_gather | solution.py:105
  161.1 3.2 broadcast_in_dim.126
  165.5 2.6 bitcast_dynamic-update-slice_fusion.1
  168.1 2.6 bitcast_dynamic-update-slice_fusion
  170.7 22.1 %collective-permute-done.11 = bf16[8,64,1408]{2,1,0:T(8,128)(2,1)S(1)} collective-permute-done((bf16[8,64,1408]{2,1,0:T(8,128)(2,1)S(1)}, bf16[8,64,1408]{2,1,0:T(8,128)(2,1)S(1)}, u32[]{:S(2)}, u32[]{:S(2)}) %collective-permute-start.11) | collective-permute-done | bytes 1441824 | tf_op jit(solution)/shard_map/ppermute | solution.py:68
  194.0 6.4 %reduce-scatter.4.cloned.1.call-done = bf16[128,2048]{1,0:T(8,128)(2,1)} async-done(((bf16[1024,2048]{1,0:T(8,128)(2,1)}), bf16[128,2048]{1,0:T(8,128)(2,1)}) %reduce-scatter.4.cloned.1.call-update) | async-done | bytes 524304 | tf_op jit(solution)/shard_map/reduce_scatter | solution.py:109
  203.8 11.5 %reduce-scatter.6.cloned.1.call-start = ((), (), s32[]{:S(2)}) async-start(), calls=%async_computation.11 | async-start | bytes 4718592 | tf_op jit(solution)/shard_map/reduce_scatter | solution.py:109
  215.3 34.4 %all-gather.8.cloned.1.call-done.h_ref = bf16[1024,2048]{1,0:T(8,128)(2,1)} async-done(((bf16[128,2048]{1,0:T(8,128)(2,1)}), bf16[1024,2048]{1,0:T(8,128)(2,1)}) %all-gather.8.cloned.1.call-update) | async-done | bytes 4194320 | tf_op jit(solution)/shard_map/all_gather | solution.py:105
  249.7 26.8 %shard_map.204 = (bf16[1024,704]{1,0:T(8,128)(2,1)}, bf16[1024,1408]{1,0:T(8,128)(2,1)}, bf16[1024,2048]{1,0:T(8,128)(2,1)}, bf16[1024,2048]{1,0:T(8,128)(2,1)}) custom-call(bf16[1024,2048]{1,0:T(8,128)(2,1)} %all-gather.8.cloned.1.call-done.h_ref, bf16[1024,2048]{1,0:T(8,128)(2,1)} %all-gather.6.cloned.1.call-done.g_ref, ...), custom_call_target="tpu_custom_call" | custom-call | tf_op jit(solution)/shard_map/pallas_call | solution.py:280
  276.6 3.1 dynamic-slice_bitcast_fusion
  280.0 4.1 collective-permute-done.12
  284.1 3.7 fusion.5
  287.8 6.2 %all-to-all-start.2 = ((bf16[4,128,2048]{2,1,0:T(8,128)(2,1)}), bf16[4,128,2048]{2,1,0:T(8,128)(2,1)}, u32[]{:S(2)}, u32[]{:S(2)}) async-start(bf16[4,128,2048]{2,1,0:T(8,128)(2,1)} %fusion.5), calls=%async_computation.3 | async-start | bytes 4194304 | tf_op jit(solution)/shard_map/all_to_all | solution.py:114
  294.0 9.5 %convolution_convert_fusion = bf16[2048,1408]{1,0:T(8,128)(2,1)S(1)} fusion(bf16[1024,2048]{1,0:T(8,128)(2,1)} %all-gather.8.cloned.1.call-done.h_ref, bf16[1024,1408]{1,0:T(8,128)(2,1)} %get-tuple-element.55), kind=kOutput, calls=%fused_computation.7 | convolution fusion | flops 5908463616 | bytes 12845056 | tf_op jit(solution)/shard_map/dot_general | solution.py:135
  306.8 4.6 convolution_convert_fusion.2
  311.4 26.3 %collective-permute-done.15 = bf16[8,64,1408]{2,1,0:T(8,128)(2,1)S(1)} collective-permute-done((bf16[8,64,1408]{2,1,0:T(8,128)(2,1)S(1)}, bf16[8,64,1408]{2,1,0:T(8,128)(2,1)S(1)}, u32[]{:S(2)}, u32[]{:S(2)}) %collective-permute-start.15) | collective-permute-done | bytes 1441824 | tf_op jit(solution)/shard_map/ppermute | solution.py:68
  337.7 31.9 %collective-permute-done.14 = bf16[8,64,1408]{2,1,0:T(8,128)(2,1)S(1)} collective-permute-done((bf16[8,64,1408]{2,1,0:T(8,128)(2,1)S(1)}, bf16[8,64,1408]{2,1,0:T(8,128)(2,1)S(1)}, u32[]{:S(2)}, u32[]{:S(2)}) %collective-permute-start.14) | collective-permute-done | bytes 1441824 | tf_op jit(solution)/shard_map/ppermute | solution.py:68
  380.6 3.2 add_convert_fusion
  383.8 12.4 %collective-permute-done.18 = bf16[176,2048]{1,0:T(8,128)(2,1)S(1)} collective-permute-done((bf16[176,2048]{1,0:T(8,128)(2,1)S(1)}, bf16[176,2048]{1,0:T(8,128)(2,1)S(1)}, u32[]{:S(2)}, u32[]{:S(2)}) %collective-permute-start.18) | collective-permute-done | bytes 720928 | tf_op jit(solution)/shard_map/ppermute | solution.py:68
  396.2 16.1 %collective-permute-done.17 = bf16[176,2048]{1,0:T(8,128)(2,1)S(1)} collective-permute-done((bf16[176,2048]{1,0:T(8,128)(2,1)S(1)}, bf16[176,2048]{1,0:T(8,128)(2,1)S(1)}, u32[]{:S(2)}, u32[]{:S(2)}) %collective-permute-start.17) | collective-permute-done | bytes 720928 | tf_op jit(solution)/shard_map/ppermute | solution.py:68
  417.1 4.8 all-gather.10.cloned.1.call-done
  421.9 4.3 convolution_convert_fusion.6.do_ref
  426.1 5.6 %all-to-all-start.3 = ((bf16[8,64,1408]{2,1,0:T(8,128)(2,1)}), bf16[8,64,1408]{2,1,0:T(8,128)(2,1)S(1)}, u32[]{:S(2)}, u32[]{:S(2)}) async-start(bf16[8,64,1408]{2,1,0:T(8,128)(2,1)} %add_convert_fusion), calls=%async_computation.5 | async-start | bytes 2883584 | tf_op jit(solution)/shard_map/all_to_all | solution.py:319
  432.8 3.2 add_convert_fusion.3
  438.0 15.3 %shard_map.205 = (bf16[1024,256]{1,0:T(8,128)(2,1)}, bf16[1024,64]{1,0:T(8,128)(2,1)}, bf16[1024,64]{1,0:T(8,128)(2,1)}) custom-call(bf16[1024,256]{1,0:T(8,128)(2,1)} %copy.140.q_ref, bf16[1024,64]{1,0:T(8,128)(2,1)} %pad_maximum_fusion.5.k_ref, bf16[1024,64]{1,0:T(8,128)(2,1)} %copy.162.v_ref, bf16[1024,256]{1,0:T(8,128)(2,1)} %convolution_convert_fusion.6.do_ref, ...), custom_call_target="tpu_custom_call" | custom-call | tf_op jit(solution)/shard_map/pallas_call | solution.py:248
  453.3 6.1 %fusion.3 = (f32[2048]{0:T(1024)S(1)}, bf16[1024,2048]{1,0:T(8,128)(2,1)}) fusion(bf16[1024,2048]{1,0:T(8,128)(2,1)S(1)} %bitcast.183, f32[1024]{0:T(1024)S(1)} %add_rsqrt_fusion, bf16[2048,512]{1,0:T(8,128)(2,1)} %bitcast.195, bf16[1024,64]{1,0:T(8,128)(2,1)} %get-tuple-element.70, bf16[1024,64]{1,0:T(8,128)(2,1)} %get-tuple-element.69, ...), kind=kOutput, calls=%fused_computation.5 | convolution fusion | flops 1623455744 | bytes 11022336 | tf_op jit(solution)/shard_map/dot_general | solution.py:131
  459.5 3.7 all-to-all-done.3
  464.3 4.2 convolution_convert_fusion.3
  470.1 4.2 copy.150
  478.8 4.5 convolution_convert_fusion.4
  483.3 6.8 %collective-permute-done.21 = bf16[8,64,512]{2,1,0:T(8,128)(2,1)S(1)} collective-permute-done((bf16[8,64,512]{2,1,0:T(8,128)(2,1)S(1)}, bf16[8,64,512]{2,1,0:T(8,128)(2,1)S(1)}, u32[]{:S(2)}, u32[]{:S(2)}) %collective-permute-start.21) | collective-permute-done | bytes 524320 | tf_op jit(solution)/shard_map/ppermute | solution.py:68
  490.1 12.1 %collective-permute-done.20 = bf16[8,64,512]{2,1,0:T(8,128)(2,1)S(1)} collective-permute-done((bf16[8,64,512]{2,1,0:T(8,128)(2,1)S(1)}, bf16[8,64,512]{2,1,0:T(8,128)(2,1)S(1)}, u32[]{:S(2)}, u32[]{:S(2)}) %collective-permute-start.20) | collective-permute-done | bytes 524320 | tf_op jit(solution)/shard_map/ppermute | solution.py:68
  503.3 6.6 %all-to-all-start.4 = ((bf16[8,64,512]{2,1,0:T(8,128)(2,1)}), bf16[8,64,512]{2,1,0:T(8,128)(2,1)S(1)}, u32[]{:S(2)}, u32[]{:S(2)}) async-start(bf16[8,64,512]{2,1,0:T(8,128)(2,1)} %add_convert_fusion.1), calls=%async_computation.7 | async-start | bytes 1048576 | tf_op jit(solution)/shard_map/all_to_all | solution.py:319
  522.9 4.1 collective-permute-done.23
  536.6 2.6 fusion.28
  (231 shorter events, 106.2 us)
Async XLA Ops:
  7.2 88.2 %all-gather.12.cloned.1.call-start = ((), (), s32[]{:S(2)}) async-start(), calls=%async_computation.14 | async-start | bytes 4718592 | tf_op jit(solution)/shard_map/all_gather | solution.py:105
  7.9 25.9 %collective-permute-start.6 = (bf16[64,2048]{1,0:T(8,128)(2,1)}, bf16[64,2048]{1,0:T(8,128)(2,1)}, u32[]{:S(2)}, u32[]{:S(2)}) collective-permute-start(bf16[64,2048]{1,0:T(8,128)(2,1)} %param.18), channel_id=1, source_target_pairs={{0,1},{1,0},{2,3},{3,2},{4,5},{5,4},{6,7},{7,6},{8,9},{9,8},{10,11... | collective-permute-start | bytes 786440 | tf_op jit(solution)/shard_map/ppermute | solution.py:68
  9.2 51.8 %collective-permute-start.8 = (bf16[64,2048]{1,0:T(8,128)(2,1)}, bf16[64,2048]{1,0:T(8,128)(2,1)S(1)}, u32[]{:S(2)}, u32[]{:S(2)}) collective-permute-start(bf16[64,2048]{1,0:T(8,128)(2,1)} %param.18), channel_id=1, source_target_pairs={{0,3},{1,2},{2,1},{3,0},{4,7},{5,6},{6,5},{7,4},{8,11},{9,10},{10,... | collective-permute-start | bytes 786440 | tf_op jit(solution)/shard_map/ppermute | solution.py:68
  10.4 47.9 %collective-permute-start.7 = (bf16[64,2048]{1,0:T(8,128)(2,1)}, bf16[64,2048]{1,0:T(8,128)(2,1)}, u32[]{:S(2)}, u32[]{:S(2)}) collective-permute-start(bf16[64,2048]{1,0:T(8,128)(2,1)} %param.18), channel_id=1, source_target_pairs={{0,2},{1,3},{2,0},{3,1},{4,6},{5,7},{6,4},{7,5},{8,10},{9,11},{10,... | collective-permute-start | bytes 786440 | tf_op jit(solution)/shard_map/ppermute | solution.py:68
  10.6 48.6 %collective-permute-start.2 = (bf16[176,2048]{1,0:T(8,128)(2,1)}, bf16[176,2048]{1,0:T(8,128)(2,1)}, u32[]{:S(2)}, u32[]{:S(2)}) collective-permute-start(bf16[176,2048]{1,0:T(8,128)(2,1)} %param.22), channel_id=1, source_target_pairs={{0,3},{1,2},{2,1},{3,0},{4,7},{5,6},{6,5},{7,4},{8,11},{9,10},{10,... | collective-permute-start | bytes 2162696 | tf_op jit(solution)/shard_map/ppermute | solution.py:68
  12.8 46.5 %collective-permute-start.1 = (bf16[176,2048]{1,0:T(8,128)(2,1)}, bf16[176,2048]{1,0:T(8,128)(2,1)}, u32[]{:S(2)}, u32[]{:S(2)}) collective-permute-start(bf16[176,2048]{1,0:T(8,128)(2,1)} %param.22), channel_id=1, source_target_pairs={{0,2},{1,3},{2,0},{3,1},{4,6},{5,7},{6,4},{7,5},{8,10},{9,11},{10,... | collective-permute-start | bytes 2162696 | tf_op jit(solution)/shard_map/ppermute | solution.py:68
  15.5 9.5 %copy-start.35 = (s32[8]{0:T(128)S(1)}, s32[8]{0:T(128)}, u32[]{:S(2)}) copy-start(s32[8]{0:T(128)} %param.13) | copy-start | bytes 100
  15.6 9.6 %copy-start.20 = (bf16[64,5632]{1,0:T(8,128)(2,1)S(1)}, bf16[64,5632]{1,0:T(8,128)(2,1)}, u32[]{:S(2)}) copy-start(bf16[64,5632]{1,0:T(8,128)(2,1)} %param.20) | copy-start | bytes 2162692
  18.0 32.5 %all-to-all-start = ((bf16[8,64,512]{2,1,0:T(8,128)(2,1)}), bf16[8,64,512]{2,1,0:T(8,128)(2,1)S(1)}, u32[]{:S(2)}, u32[]{:S(2)}) async-start(bf16[8,64,512]{2,1,0:T(8,128)(2,1)} %copy.132), calls=%async_computation | async-start | bytes 1048576 | tf_op jit(solution)/shard_map/all_to_all | solution.py:319
  33.8 25.5 %collective-permute-start = (bf16[176,2048]{1,0:T(8,128)(2,1)}, bf16[176,2048]{1,0:T(8,128)(2,1)}, u32[]{:S(2)}, u32[]{:S(2)}) collective-permute-start(bf16[176,2048]{1,0:T(8,128)(2,1)} %param.22), channel_id=1, source_target_pairs={{0,1},{1,0},{2,3},{3,2},{4,5},{5,4},{6,7},{7,6},{8,9},{9,8},{10,11... | collective-permute-start | bytes 2162696 | tf_op jit(solution)/shard_map/ppermute | solution.py:68
  50.5 44.9 %all-to-all-start.1 = ((bf16[8,64,1408]{2,1,0:T(8,128)(2,1)}), bf16[8,64,1408]{2,1,0:T(8,128)(2,1)S(1)}, u32[]{:S(2)}, u32[]{:S(2)}) async-start(bf16[8,64,1408]{2,1,0:T(8,128)(2,1)} %pad_maximum_fusion.1), calls=%async_computation.1 | async-start | bytes 2883584 | tf_op jit(solution)/shard_map/all_to_all | solution.py:319
  58.3 91.5 %all-gather.6.cloned.1.call-start = ((), (), s32[]{:S(2)}) async-start(), calls=%async_computation.8 | async-start | bytes 4718592 | tf_op jit(solution)/shard_map/all_gather | solution.py:105
  59.3 14.1 %collective-permute-start.4 = (bf16[8,64,512]{2,1,0:T(8,128)(2,1)S(1)}, bf16[8,64,512]{2,1,0:T(8,128)(2,1)S(1)}, u32[]{:S(2)}, u32[]{:S(2)}) collective-permute-start(bf16[8,64,512]{2,1,0:T(8,128)(2,1)S(1)} %all-to-all-done), channel_id=1, source_target_pairs={{0,2},{1,3},{2,0},{3,1},{4,6},{5,7},{6,4},{7,5},{8,10},{9,11},{10,... | collective-permute-start | bytes 1572872 | tf_op jit(solution)/shard_map/ppermute | solution.py:68
  60.6 12.8 %collective-permute-start.3 = (bf16[8,64,512]{2,1,0:T(8,128)(2,1)S(1)}, bf16[8,64,512]{2,1,0:T(8,128)(2,1)S(1)}, u32[]{:S(2)}, u32[]{:S(2)}) collective-permute-start(bf16[8,64,512]{2,1,0:T(8,128)(2,1)S(1)} %all-to-all-done), channel_id=1, source_target_pairs={{0,1},{1,0},{2,3},{3,2},{4,5},{5,4},{6,7},{7,6},{8,9},{9,8},{10,11... | collective-permute-start | bytes 1572872 | tf_op jit(solution)/shard_map/ppermute | solution.py:68
  61.0 12.4 %copy-start.10 = (bf16[4,64,2048]{2,1,0:T(8,128)(2,1)}, bf16[4,64,2048]{2,1,0:T(8,128)(2,1)S(1)}, u32[]{:S(2)}) copy-start(bf16[4,64,2048]{2,1,0:T(8,128)(2,1)S(1)} %bitcast_dynamic-update-slice_fusion.12) | copy-start | bytes 3145732
  61.0 23.5 %collective-permute-start.5 = (bf16[8,64,512]{2,1,0:T(8,128)(2,1)S(1)}, bf16[8,64,512]{2,1,0:T(8,128)(2,1)S(1)}, u32[]{:S(2)}, u32[]{:S(2)}) collective-permute-start(bf16[8,64,512]{2,1,0:T(8,128)(2,1)S(1)} %all-to-all-done), channel_id=1, source_target_pairs={{0,3},{1,2},{2,1},{3,0},{4,7},{5,6},{6,5},{7,4},{8,11},{9,10},{10,... | collective-permute-start | bytes 1572872 | tf_op jit(solution)/shard_map/ppermute | solution.py:68
  85.9 12.7 %copy-start.24 = (f32[1,2048]{1,0:T(1,128)}, f32[1,2048]{1,0:T(1,128)S(1)}, u32[]{:S(2)}) copy-start(f32[1,2048]{1,0:T(1,128)S(1)} %get-tuple-element.113) | copy-start | bytes 24580
  102.0 98.5 %reduce-scatter.4.cloned.1.call-start = ((), (), s32[]{:S(2)}) async-start(), calls=%async_computation.9 | async-start | bytes 4718592 | tf_op jit(solution)/shard_map/reduce_scatter | solution.py:109
  102.8 32.9 %collective-permute-start.10 = (bf16[8,64,1408]{2,1,0:T(8,128)(2,1)S(1)}, bf16[8,64,1408]{2,1,0:T(8,128)(2,1)}, u32[]{:S(2)}, u32[]{:S(2)}) collective-permute-start(bf16[8,64,1408]{2,1,0:T(8,128)(2,1)S(1)} %all-to-all-done.1), channel_id=1, source_target_pairs={{0,2},{1,3},{2,0},{3,1},{4,6},{5,7},{6,4},{7,5},{8,10},{9,11},{10,... | collective-permute-start | bytes 4325384 | tf_op jit(solution)/shard_map/ppermute | solution.py:68
  104.2 32.5 %collective-permute-start.9 = (bf16[8,64,1408]{2,1,0:T(8,128)(2,1)S(1)}, bf16[8,64,1408]{2,1,0:T(8,128)(2,1)}, u32[]{:S(2)}, u32[]{:S(2)}) collective-permute-start(bf16[8,64,1408]{2,1,0:T(8,128)(2,1)S(1)} %all-to-all-done.1), channel_id=1, source_target_pairs={{0,1},{1,0},{2,3},{3,2},{4,5},{5,4},{6,7},{7,6},{8,9},{9,8},{10,11... | collective-permute-start | bytes 4325384 | tf_op jit(solution)/shard_map/ppermute | solution.py:68
  114.6 12.7 %copy-start.11 = (bf16[4,64,2048]{2,1,0:T(8,128)(2,1)S(1)}, bf16[4,64,2048]{2,1,0:T(8,128)(2,1)}, u32[]{:S(2)}) copy-start(bf16[4,64,2048]{2,1,0:T(8,128)(2,1)} %copy-done.10) | copy-start | bytes 3145732
  149.8 99.8 %all-gather.8.cloned.1.call-start = ((), (), s32[]{:S(2)}) async-start(), calls=%async_computation.10 | async-start | bytes 4718592 | tf_op jit(solution)/shard_map/all_gather | solution.py:105
  159.0 33.8 %collective-permute-start.11 = (bf16[8,64,1408]{2,1,0:T(8,128)(2,1)S(1)}, bf16[8,64,1408]{2,1,0:T(8,128)(2,1)S(1)}, u32[]{:S(2)}, u32[]{:S(2)}) collective-permute-start(bf16[8,64,1408]{2,1,0:T(8,128)(2,1)S(1)} %all-to-all-done.1), channel_id=1, source_target_pairs={{0,3},{1,2},{2,1},{3,0},{4,7},{5,6},{6,5},{7,4},{8,11},{9,10},{10,... | collective-permute-start | bytes 4325384 | tf_op jit(solution)/shard_map/ppermute | solution.py:68
  170.7 29.7 %copy-start = (bf16[1,128,2048]{2,1,0:T(8,128)(2,1)S(1)}, bf16[1,128,2048]{2,1,0:T(8,128)(2,1)}, u32[]{:S(2)}) copy-start(bf16[1,128,2048]{2,1,0:T(8,128)(2,1)} %param.12) | copy-start | bytes 1572868
  201.8 74.8 %copy-start.30 = (f32[128]{0:T(128)}, f32[128]{0:T(128)S(1)}, u32[]{:S(2)}) copy-start(f32[128]{0:T(128)S(1)} %add_rsqrt_fusion.2) | copy-start | bytes 1540
  203.8 166.8 %reduce-scatter.6.cloned.1.call-start = ((), (), s32[]{:S(2)}) async-start(), calls=%async_computation.11 | async-start | bytes 4718592 | tf_op jit(solution)/shard_map/reduce_scatter | solution.py:109
  279.7 4.4 collective-permute-start.12
  287.8 82.9 %all-to-all-start.2 = ((bf16[4,128,2048]{2,1,0:T(8,128)(2,1)}), bf16[4,128,2048]{2,1,0:T(8,128)(2,1)}, u32[]{:S(2)}, u32[]{:S(2)}) async-start(bf16[4,128,2048]{2,1,0:T(8,128)(2,1)} %fusion.5), calls=%async_computation.3 | async-start | bytes 4194304 | tf_op jit(solution)/shard_map/all_to_all | solution.py:114
  294.0 127.8 %all-gather.10.cloned.1.call-start = ((), (), s32[]{:S(2)}) async-start(), calls=%async_computation.12 | async-start | bytes 4718592 | tf_op jit(solution)/shard_map/all_gather | solution.py:105
  304.1 33.6 %collective-permute-start.15 = (bf16[8,64,1408]{2,1,0:T(8,128)(2,1)S(1)}, bf16[8,64,1408]{2,1,0:T(8,128)(2,1)S(1)}, u32[]{:S(2)}, u32[]{:S(2)}) collective-permute-start(bf16[8,64,1408]{2,1,0:T(8,128)(2,1)S(1)} %get-tuple-element.88), channel_id=1, source_target_pairs={{0,3},{1,2},{2,1},{3,0},{4,7},{5,6},{6,5},{7,4},{8,11},{9,10},{10,... | collective-permute-start | bytes 4325384 | tf_op jit(solution)/shard_map/ppermute | solution.py:68
  306.2 63.3 %collective-permute-start.14 = (bf16[8,64,1408]{2,1,0:T(8,128)(2,1)S(1)}, bf16[8,64,1408]{2,1,0:T(8,128)(2,1)S(1)}, u32[]{:S(2)}, u32[]{:S(2)}) collective-permute-start(bf16[8,64,1408]{2,1,0:T(8,128)(2,1)S(1)} %get-tuple-element.89), channel_id=1, source_target_pairs={{0,2},{1,3},{2,0},{3,1},{4,6},{5,7},{6,4},{7,5},{8,10},{9,11},{10,... | collective-permute-start | bytes 4325384 | tf_op jit(solution)/shard_map/ppermute | solution.py:68
  306.5 64.2 %collective-permute-start.13 = (bf16[8,64,1408]{2,1,0:T(8,128)(2,1)S(1)}, bf16[8,64,1408]{2,1,0:T(8,128)(2,1)}, u32[]{:S(2)}, u32[]{:S(2)}) collective-permute-start(bf16[8,64,1408]{2,1,0:T(8,128)(2,1)S(1)} %get-tuple-element.90), channel_id=1, source_target_pairs={{0,1},{1,0},{2,3},{3,2},{4,5},{5,4},{6,7},{7,6},{8,9},{9,8},{10,11... | collective-permute-start | bytes 4325384 | tf_op jit(solution)/shard_map/ppermute | solution.py:68
  306.8 63.9 %copy-start.1 = (bf16[128,2048]{1,0:T(8,128)(2,1)S(1)}, bf16[128,2048]{1,0:T(8,128)(2,1)}, u32[]{:S(2)}) copy-start(bf16[128,2048]{1,0:T(8,128)(2,1)} %reduce-scatter.4.cloned.1.call-done) | copy-start | bytes 1572868
  306.8 66.6 %copy-start.5 = (bf16[1,128,2048]{2,1,0:T(8,128)(2,1)S(1)}, bf16[1,128,2048]{2,1,0:T(8,128)(2,1)}, u32[]{:S(2)}) copy-start(bf16[1,128,2048]{2,1,0:T(8,128)(2,1)} %param.23) | copy-start | bytes 1572868
  337.7 31.9 %copy-start.16 = (bf16[8,64,1408]{2,1,0:T(8,128)(2,1)}, bf16[8,64,1408]{2,1,0:T(8,128)(2,1)S(1)}, u32[]{:S(2)}) copy-start(bf16[8,64,1408]{2,1,0:T(8,128)(2,1)S(1)} %collective-permute-done.15) | copy-start | bytes 4325380
  377.9 18.3 %collective-permute-start.18 = (bf16[176,2048]{1,0:T(8,128)(2,1)S(1)}, bf16[176,2048]{1,0:T(8,128)(2,1)S(1)}, u32[]{:S(2)}, u32[]{:S(2)}) collective-permute-start(bf16[176,2048]{1,0:T(8,128)(2,1)S(1)} %get-tuple-element.93), channel_id=1, source_target_pairs={{0,3},{1,2},{2,1},{3,0},{4,7},{5,6},{6,5},{7,4},{8,11},{9,10},{10,... | collective-permute-start | bytes 2162696 | tf_op jit(solution)/shard_map/ppermute | solution.py:68
  379.6 32.7 %collective-permute-start.17 = (bf16[176,2048]{1,0:T(8,128)(2,1)S(1)}, bf16[176,2048]{1,0:T(8,128)(2,1)S(1)}, u32[]{:S(2)}, u32[]{:S(2)}) collective-permute-start(bf16[176,2048]{1,0:T(8,128)(2,1)S(1)} %get-tuple-element.94), channel_id=1, source_target_pairs={{0,2},{1,3},{2,0},{3,1},{4,6},{5,7},{6,4},{7,5},{8,10},{9,11},{10,... | collective-permute-start | bytes 2162696 | tf_op jit(solution)/shard_map/ppermute | solution.py:68
  380.3 32.1 %collective-permute-start.16 = (bf16[176,2048]{1,0:T(8,128)(2,1)S(1)}, bf16[176,2048]{1,0:T(8,128)(2,1)S(1)}, u32[]{:S(2)}, u32[]{:S(2)}) collective-permute-start(bf16[176,2048]{1,0:T(8,128)(2,1)S(1)} %get-tuple-element.95), channel_id=1, source_target_pairs={{0,1},{1,0},{2,3},{3,2},{4,5},{5,4},{6,7},{7,6},{8,9},{9,8},{10,11... | collective-permute-start | bytes 2162696 | tf_op jit(solution)/shard_map/ppermute | solution.py:68
  426.1 37.1 %all-to-all-start.3 = ((bf16[8,64,1408]{2,1,0:T(8,128)(2,1)}), bf16[8,64,1408]{2,1,0:T(8,128)(2,1)S(1)}, u32[]{:S(2)}, u32[]{:S(2)}) async-start(bf16[8,64,1408]{2,1,0:T(8,128)(2,1)} %add_convert_fusion), calls=%async_computation.5 | async-start | bytes 2883584 | tf_op jit(solution)/shard_map/all_to_all | solution.py:319
  431.7 103.4 %reduce-scatter.8.cloned.1.call-start = ((), (), s32[]{:S(2)}) async-start(), calls=%async_computation.13 | async-start | bytes 4718592 | tf_op jit(solution)/shard_map/reduce_scatter | solution.py:109
  436.0 17.3 %copy-start.3 = (bf16[1,1024,2048]{2,1,0:T(8,128)(2,1)S(1)}, bf16[1,1024,2048]{2,1,0:T(8,128)(2,1)}, u32[]{:S(2)}) copy-start(bf16[1,1024,2048]{2,1,0:T(8,128)(2,1)} %all-gather.12.cloned.1.call-done) | copy-start | bytes 12582916
  476.1 14.1 %collective-permute-start.21 = (bf16[8,64,512]{2,1,0:T(8,128)(2,1)S(1)}, bf16[8,64,512]{2,1,0:T(8,128)(2,1)S(1)}, u32[]{:S(2)}, u32[]{:S(2)}) collective-permute-start(bf16[8,64,512]{2,1,0:T(8,128)(2,1)S(1)} %get-tuple-element.97), channel_id=1, source_target_pairs={{0,3},{1,2},{2,1},{3,0},{4,7},{5,6},{6,5},{7,4},{8,11},{9,10},{10,... | collective-permute-start | bytes 1572872 | tf_op jit(solution)/shard_map/ppermute | solution.py:68
  478.2 24.0 %collective-permute-start.20 = (bf16[8,64,512]{2,1,0:T(8,128)(2,1)S(1)}, bf16[8,64,512]{2,1,0:T(8,128)(2,1)S(1)}, u32[]{:S(2)}, u32[]{:S(2)}) collective-permute-start(bf16[8,64,512]{2,1,0:T(8,128)(2,1)S(1)} %get-tuple-element.98), channel_id=1, source_target_pairs={{0,2},{1,3},{2,0},{3,1},{4,6},{5,7},{6,4},{7,5},{8,10},{9,11},{10,... | collective-permute-start | bytes 1572872 | tf_op jit(solution)/shard_map/ppermute | solution.py:68
  478.5 23.7 %collective-permute-start.19 = (bf16[8,64,512]{2,1,0:T(8,128)(2,1)S(1)}, bf16[8,64,512]{2,1,0:T(8,128)(2,1)S(1)}, u32[]{:S(2)}, u32[]{:S(2)}) collective-permute-start(bf16[8,64,512]{2,1,0:T(8,128)(2,1)S(1)} %get-tuple-element.99), channel_id=1, source_target_pairs={{0,1},{1,0},{2,3},{3,2},{4,5},{5,4},{6,7},{7,6},{8,9},{9,8},{10,11... | collective-permute-start | bytes 1572872 | tf_op jit(solution)/shard_map/ppermute | solution.py:68
  503.3 25.8 %all-to-all-start.4 = ((bf16[8,64,512]{2,1,0:T(8,128)(2,1)}), bf16[8,64,512]{2,1,0:T(8,128)(2,1)S(1)}, u32[]{:S(2)}, u32[]{:S(2)}) async-start(bf16[8,64,512]{2,1,0:T(8,128)(2,1)} %add_convert_fusion.1), calls=%async_computation.7 | async-start | bytes 1048576 | tf_op jit(solution)/shard_map/all_to_all | solution.py:319
  512.0 11.0 %collective-permute-start.24 = (bf16[64,2048]{1,0:T(8,128)(2,1)}, bf16[64,2048]{1,0:T(8,128)(2,1)}, u32[]{:S(2)}, u32[]{:S(2)}) collective-permute-start(bf16[64,2048]{1,0:T(8,128)(2,1)} %get-tuple-element.105), channel_id=1, source_target_pairs={{0,3},{1,2},{2,1},{3,0},{4,7},{5,6},{6,5},{7,4},{8,11},{9,10},{10,... | collective-permute-start | bytes 786440 | tf_op jit(solution)/shard_map/ppermute | solution.py:68
  513.4 13.7 %collective-permute-start.23 = (bf16[64,2048]{1,0:T(8,128)(2,1)}, bf16[64,2048]{1,0:T(8,128)(2,1)}, u32[]{:S(2)}, u32[]{:S(2)}) collective-permute-start(bf16[64,2048]{1,0:T(8,128)(2,1)} %get-tuple-element.106), channel_id=1, source_target_pairs={{0,2},{1,3},{2,0},{3,1},{4,6},{5,7},{6,4},{7,5},{8,10},{9,11},{10,... | collective-permute-start | bytes 786440 | tf_op jit(solution)/shard_map/ppermute | solution.py:68
  514.3 12.7 %collective-permute-start.22 = (bf16[64,2048]{1,0:T(8,128)(2,1)}, bf16[64,2048]{1,0:T(8,128)(2,1)}, u32[]{:S(2)}, u32[]{:S(2)}) collective-permute-start(bf16[64,2048]{1,0:T(8,128)(2,1)} %get-tuple-element.107), channel_id=1, source_target_pairs={{0,1},{1,0},{2,3},{3,2},{4,5},{5,4},{6,7},{7,6},{8,9},{9,8},{10,11... | collective-permute-start | bytes 786440 | tf_op jit(solution)/shard_map/ppermute | solution.py:68
  (27 other events, 105.5 us)
Sparse Core Ops, SparseCore 0:
  9.6 69.3 all-gather.11
  102.1 47.6 all-gather.5
  152.1 48.3 reduce-scatter.3
  204.0 45.6 all-gather.7
  276.7 93.8 reduce-scatter.5
  375.9 45.9 all-gather.9
  463.3 50.0 reduce-scatter.7

commit v3 on v2

--- a/solution.py
+++ b/solution.py
@@ -16,6 +16,7 @@
 BF = jnp.bfloat16
 F32 = jnp.float32
 FFN_ROWS = 256
+SUM_COST = 40 * 10**9
 
 
 def rms_parts(values):
@@ -287,6 +288,26 @@
     )(h, g, w_gu, w_d)
 
 
+def sum_kernel(*refs):
+    total = refs[0][...].astype(F32)
+    for ref in refs[1:-1]:
+        total = total + ref[...].astype(F32)
+    refs[-1][...] = total.astype(refs[-1].dtype)
+
+
+def sum_pieces(pieces, cost):
+    shape = pieces[0].shape
+    block = pl.BlockSpec((1,) + shape[1:], lambda i: (i, 0, 0))
+    return pl.pallas_call(
+        sum_kernel,
+        grid=(shape[0],),
+        in_specs=[block] * len(pieces),
+        out_specs=block,
+        out_shape=jax.ShapeDtypeStruct(shape, BF),
+        cost_estimate=pl.CostEstimate(flops=cost, bytes_accessed=cost // 300, transcendentals=0),
+    )(*pieces)
+
+
 def on_device(
     tokens,
     block_order,
@@ -367,7 +388,7 @@
     v = qkv[:, q_cols + HD :].astype(BF)
     o = attend(q, k, v, pos_col, pos_row, half)
     y_part = dot(o, w_o).astype(BF)
-    y_rows = scatter_c(after(y_part, g_all, *gu_pieces[:3]))
+    y_rows = scatter_c(after(y_part, g_all, q_turn, k_turn, *gu_pieces[:3]))
 
     source = tokens[0].astype(F32)
     residual = source + y_rows.astype(F32)
@@ -383,19 +404,15 @@
     sent_gu = send_f(grad_gu_low.reshape(c_count, f_count, rows, -1), 1, f_index, f_count)
     grad_down_low = dot_tn(z, after(g_all, grad_gu_low)).astype(BF)
     sent_down = send_f(grad_down_low.reshape(f_count, -1, width), 0, f_index, f_count)
-    out_mine = pair_sum(out_part, c_count)
-
-    out_blocks = exchange_z(out_mine, c_count)
-    d_h = after(dh2, grad_down_low, out_blocks, *sent_gu).astype(F32)
+
+    d_h = after(dh2, grad_down_low, *sent_gu[:3]).astype(F32)
     gain_terms_f = jnp.sum(d_h * normed_f, axis=0)
     d_res = cotangent[0].astype(F32) + norm_back(d_h * gain_f, normed_f, recip_f)
     ab_rows = d_res.astype(BF)
     ab = gather_c(ab_rows)
-    sum_gu = total_f(sent_gu, ab_rows).astype(BF)
-    shard_down = total_f(sent_down, sum_gu)
-    out_sum = jnp.sum(after(out_blocks, ab_rows).astype(F32), axis=0)
-    result = (residual + out_sum).astype(BF)
-    ab = after(ab, sum_gu, shard_down, result)
+    sum_gu = sum_pieces([after(piece, ab_rows) for piece in sent_gu], SUM_COST)
+    ab = after(ab, sum_gu)
+    out_rows = scatter_c(after(out_part, ab))
 
     d_o = dot_nt(ab, w_o).astype(BF)
     owned_gu = to_dest(after(sum_gu, d_o))
@@ -403,20 +420,23 @@
         q, k, v, d_o, k_turn, q_turn, cos_wide, sin_wide, pos_col, pos_row, half
     )
     dqkv = jnp.concatenate([dq, dk, dv], axis=1)
-    dh1_part = dot_nt(dqkv, w_qkv)
-    dh1_low = after(dh1_part.astype(BF), owned_gu)
-    dh1 = scatter_c(dh1_low)
-    gain_terms_a = jnp.sum(dh1_part * normed_all, axis=0)
-
+    grad_qkv = dot_tn(h1, dqkv)
+    gain_terms_a = jnp.sum(grad_qkv * w_qkv.astype(F32), axis=1) / gain_a
     terms = jnp.stack([gain_terms_a, gain_terms_f])
     high = terms.astype(BF)
     low = (terms - high.astype(F32)).astype(BF)
     gain_cols = dot_tn(jnp.concatenate([high, low]), jnp.eye(4, 128, dtype=BF)).astype(BF)
-    grad_qkv_low = jnp.concatenate([dot_tn(after(h1, dh1_low), dqkv).astype(BF), gain_cols], axis=1)
+    grad_qkv_low = jnp.concatenate([grad_qkv.astype(BF), gain_cols], axis=1)
     sent_qkv = send_f(grad_qkv_low.reshape(c_count, f_count, rows, -1), 1, f_index, f_count)
     grad_out_low = dot_tn(after(o, grad_qkv_low), ab).astype(BF)
     sent_out = send_f(grad_out_low.reshape(f_count, rows, width), 0, f_index, f_count)
-    owned_qkv = to_dest(total_f(sent_qkv, owned_gu).astype(BF))
+    dh1_cast = dot_nt(after(dqkv, grad_qkv_low), w_qkv).astype(BF)
+    dh1_low = after(dh1_cast, owned_gu, out_rows, *sent_down, *sent_qkv)
+    dh1 = scatter_c(dh1_low)
+    sum_qkv = total_f(sent_qkv, dh1_low).astype(BF)
+    shard_down = total_f(sent_down, sum_qkv)
+    result = (residual + after(out_rows, sum_qkv).astype(F32)).astype(BF)
+    owned_qkv = to_dest(sum_qkv)
     shard_out = total_f(sent_out)
     shard_gate = owned_gu[:, :, :ff_cols].transpose(1, 0, 2).reshape(rows, -1).astype(F32)
     shard_up = owned_gu[:, :, ff_cols:].transpose(1, 0, 2).reshape(rows, -1).astype(F32)

time: 556 us -> 536 us (0.964)
  waiting for transfers between devices: 251 us -> 242 us
  starting transfers between devices: 68.8 us -> 59.9 us
  Pallas kernels: 50.9 us -> 57.6 us
  matrix products: 42.6 us -> 36.1 us
    ppermute x24, waiting for transfers between devices: 159 us -> 142 us  [swap_f(): return lax.ppermute(value, 'fsdp', [(i, i ^ step) for i in range(f_count)])]
    reduce_scatter x3 -> x4, waiting for transfers between devices: 6.44 us -> 18.6 us  [scatter_c(): return lax.psum_scatter(full, 'ctx', scatter_dimension=0, tiled=True)]
    all_to_all x4, waiting for transfers between devices: 28.7 us -> 18.1 us  [to_dest(): lax.all_to_all(packed, 'ctx', split_axis=0, concat_axis=0, tiled=True)]
    reduce_scatter x3 -> x4, starting transfers between devices: 11.8 us -> 1.28 us  [scatter_c(): return lax.psum_scatter(full, 'ctx', scatter_dimension=0, tiled=True)]
    all_gather x4, waiting for transfers between devices: 52.2 us -> 62.1 us  [gather_c(): return lax.all_gather(rows, 'ctx', axis=0, tiled=True)]
    unnamed x80 -> x74, local copies, waits for them, and re-layouts: 6.78 us -> 13.6 us
    pallas_call x0 -> x1, Pallas kernels: none -> 6.55 us  [sum_pieces(): pl.pallas_call(sum_kernel, grid=(shape[0],), in_specs=[block] * len(piece...]
    all_to_all x1 -> x0, starting transfers between devices: 6.23 us -> none  [exchange_z(): lax.all_to_all(blocks, 'ctx', split_axis=0, concat_axis=0, tiled=True, ax...]
  transfers between devices with their start and end apart: 37 -> 36, of which waited for: 20 -> 23; matrix products, arithmetic and copies ran while one was open for 24% -> 24% of each run, Pallas kernels for 4% -> 6%
where the time goes in v3:
time: 536 us; the launch traced here: 527 us
  waiting for transfers between devices  242 us (45%)
  local copies, waits for them, and re-layouts  62.6 us (12%)
  starting transfers between devices  59.9 us (11%)
  Pallas kernels  57.6 us (11%)
  other arithmetic  54 us (10%)
  matrix products  36.1 us (7%)
  between operations  15.3 us (3%)
    ppermute x24, waiting for transfers between devices, swap_f(): return lax.ppermute(value, 'fsdp', [(i, i ^ step) for i in range(f_count)])  142 us
    all_gather x4, waiting for transfers between devices, gather_c(): return lax.all_gather(rows, 'ctx', axis=0, tiled=True)  62.1 us
    all_to_all x4, starting transfers between devices, to_dest(): lax.all_to_all(packed, 'ctx', split_axis=0, concat_axis=0, tiled=True)  31.5 us
    ppermute x24, starting transfers between devices, swap_f(): return lax.ppermute(value, 'fsdp', [(i, i ^ step) for i in range(f_count)])  27 us
    pallas_call x1, Pallas kernels, ffn(): pl.pallas_call(ffn_kernel, grid=(seq // block,), in_specs=[rows, rows, wh...  26.8 us
    dot_general x5, matrix products, dot_tn(): lax.dot_general(a, b, (((0,), (0,)), ((), ())), preferred_element_type=F32)  22.1 us
    reduce_scatter x4, waiting for transfers between devices, scatter_c(): return lax.psum_scatter(full, 'ctx', scatter_dimension=0, tiled=True)  18.6 us
    all_to_all x4, waiting for transfers between devices, to_dest(): lax.all_to_all(packed, 'ctx', split_axis=0, concat_axis=0, tiled=True)  18.1 us
  transfers between devices with their start and end apart: 36, of which 23 were waited for; matrix products, arithmetic and copies ran while one was open for 24% of the time, Pallas kernels for 6%

profile of v3, /device:TPU:9, one launch (start us, length us, event | category | flops | bytes accessed | tf_op | source)
XLA Modules:
  0.0 527.4 jit_solution(2113972062516502264)
XLA Ops:
  18.0 7.0 %all-to-all-start = ((bf16[8,64,512]{2,1,0:T(8,128)(2,1)}), bf16[8,64,512]{2,1,0:T(8,128)(2,1)}, u32[]{:S(2)}, u32[]{:S(2)}) async-start(bf16[8,64,512]{2,1,0:T(8,128)(2,1)} %copy.151), calls=%async_computation | async-start | bytes 1048576 | tf_op jit(solution)/shard_map/all_to_all | solution.py:340
  33.8 12.7 %collective-permute-done.6 = bf16[64,2048]{1,0:T(8,128)(2,1)S(1)} collective-permute-done((bf16[64,2048]{1,0:T(8,128)(2,1)}, bf16[64,2048]{1,0:T(8,128)(2,1)S(1)}, u32[]{:S(2)}, u32[]{:S(2)}) %collective-permute-start.6) | collective-permute-done | bytes 262176 | tf_op jit(solution)/shard_map/ppermute | solution.py:69
  50.5 7.9 %all-to-all-start.1 = ((bf16[8,64,1408]{2,1,0:T(8,128)(2,1)}), bf16[8,64,1408]{2,1,0:T(8,128)(2,1)S(1)}, u32[]{:S(2)}, u32[]{:S(2)}) async-start(bf16[8,64,1408]{2,1,0:T(8,128)(2,1)} %pad_maximum_fusion.1), calls=%async_computation.1 | async-start | bytes 2883584 | tf_op jit(solution)/shard_map/all_to_all | solution.py:340
  64.5 8.3 %collective-permute-done.3 = bf16[8,64,512]{2,1,0:T(8,128)(2,1)S(1)} collective-permute-done((bf16[8,64,512]{2,1,0:T(8,128)(2,1)}, bf16[8,64,512]{2,1,0:T(8,128)(2,1)S(1)}, u32[]{:S(2)}, u32[]{:S(2)}) %collective-permute-start.3) | collective-permute-done | bytes 524320 | tf_op jit(solution)/shard_map/ppermute | solution.py:69
  73.0 11.2 %collective-permute-done.5 = bf16[8,64,512]{2,1,0:T(8,128)(2,1)S(1)} collective-permute-done((bf16[8,64,512]{2,1,0:T(8,128)(2,1)}, bf16[8,64,512]{2,1,0:T(8,128)(2,1)S(1)}, u32[]{:S(2)}, u32[]{:S(2)}) %collective-permute-start.5) | collective-permute-done | bytes 524320 | tf_op jit(solution)/shard_map/ppermute | solution.py:69
  86.0 9.4 %all-to-all-done.1 = bf16[8,64,1408]{2,1,0:T(8,128)(2,1)S(1)} async-done(((bf16[8,64,1408]{2,1,0:T(8,128)(2,1)}), bf16[8,64,1408]{2,1,0:T(8,128)(2,1)S(1)}, u32[]{:S(2)}, u32[]{:S(2)}) %all-to-all-start.1) | async-done | bytes 1441824 | tf_op jit(solution)/shard_map/all_to_all | solution.py:340
  95.4 3.2 fusion
  98.9 3.1 fusion.2
  106.3 4.0 fusion.53
  115.3 2.4 fusion.55
  117.7 2.4 fusion.74
  120.9 8.8 %shard_map.203 = bf16[1024,256]{1,0:T(8,128)(2,1)} custom-call(bf16[1024,256]{1,0:T(8,128)(2,1)} %copy.161.q_ref, bf16[1024,64]{1,0:T(8,128)(2,1)} %pad_maximum_fusion.5.k_ref, bf16[1024,64]{1,0:T(8,128)(2,1)} %copy.184.v_ref, s32[1024,1]{1,0:T(8,128)} %fusion.19.col_ref, s32[2,512]{1,0:T(2,128)} %reshape.371.row_ref), custom_call_target="tpu_custom_call" | custom-call | tf_op jit(solution)/shard_map/pallas_call | solution.py:236
  133.8 3.3 convolution_convert_fusion.2
  137.5 12.3 %all-gather.6.cloned.1.call-done.g_ref = bf16[1024,2048]{1,0:T(8,128)(2,1)} async-done(((bf16[128,2048]{1,0:T(8,128)(2,1)}), bf16[1024,2048]{1,0:T(8,128)(2,1)}) %all-gather.6.cloned.1.call-update) | async-done | bytes 4194320 | tf_op jit(solution)/shard_map/all_gather | solution.py:106
  156.7 3.2 broadcast_in_dim.126
  161.2 2.6 bitcast_dynamic-update-slice_fusion.1
  163.8 2.7 bitcast_dynamic-update-slice_fusion
  166.5 22.0 %collective-permute-done.11 = bf16[8,64,1408]{2,1,0:T(8,128)(2,1)S(1)} collective-permute-done((bf16[8,64,1408]{2,1,0:T(8,128)(2,1)S(1)}, bf16[8,64,1408]{2,1,0:T(8,128)(2,1)S(1)}, u32[]{:S(2)}, u32[]{:S(2)}) %collective-permute-start.11) | collective-permute-done | bytes 1441824 | tf_op jit(solution)/shard_map/ppermute | solution.py:69
  189.7 10.8 %reduce-scatter.5.cloned.1.call-done = bf16[128,2048]{1,0:T(8,128)(2,1)} async-done(((bf16[1024,2048]{1,0:T(8,128)(2,1)}), bf16[128,2048]{1,0:T(8,128)(2,1)}) %reduce-scatter.5.cloned.1.call-update) | async-done | bytes 524304 | tf_op jit(solution)/shard_map/reduce_scatter | solution.py:110
  204.1 45.6 %all-gather.8.cloned.1.call-done.h_ref = bf16[1024,2048]{1,0:T(8,128)(2,1)} async-done(((bf16[128,2048]{1,0:T(8,128)(2,1)}), bf16[1024,2048]{1,0:T(8,128)(2,1)}) %all-gather.8.cloned.1.call-update) | async-done | bytes 4194320 | tf_op jit(solution)/shard_map/all_gather | solution.py:106
  249.7 26.8 %shard_map.204 = (bf16[1024,704]{1,0:T(8,128)(2,1)}, bf16[1024,1408]{1,0:T(8,128)(2,1)}, bf16[1024,2048]{1,0:T(8,128)(2,1)}, bf16[1024,2048]{1,0:T(8,128)(2,1)}) custom-call(bf16[1024,2048]{1,0:T(8,128)(2,1)} %all-gather.8.cloned.1.call-done.h_ref, bf16[1024,2048]{1,0:T(8,128)(2,1)} %all-gather.6.cloned.1.call-done.g_ref, ...), custom_call_target="tpu_custom_call" | custom-call | tf_op jit(solution)/shard_map/pallas_call | solution.py:281
  278.4 9.4 %convolution_convert_fusion = bf16[2048,1408]{1,0:T(8,128)(2,1)S(1)} fusion(bf16[1024,2048]{1,0:T(8,128)(2,1)} %all-gather.8.cloned.1.call-done.h_ref, bf16[1024,1408]{1,0:T(8,128)(2,1)S(1)} %copy-done.31), kind=kOutput, calls=%fused_computation.5 | convolution fusion | flops 5908463616 | bytes 12845056 | tf_op jit(solution)/shard_map/dot_general | solution.py:136
  291.8 4.6 convolution_convert_fusion.3
  296.4 26.0 %collective-permute-done.12.refs_1_ = bf16[8,64,1408]{2,1,0:T(8,128)(2,1)S(1)} collective-permute-done((bf16[8,64,1408]{2,1,0:T(8,128)(2,1)S(1)}, bf16[8,64,1408]{2,1,0:T(8,128)(2,1)S(1)}, u32[]{:S(2)}, u32[]{:S(2)}) %collective-permute-start.12) | collective-permute-done | bytes 1441824 | tf_op jit(solution)/shard_map/ppermute | solution.py:69
  331.4 32.6 %collective-permute-done.14.refs_3_ = bf16[8,64,1408]{2,1,0:T(8,128)(2,1)} collective-permute-done((bf16[8,64,1408]{2,1,0:T(8,128)(2,1)S(1)}, bf16[8,64,1408]{2,1,0:T(8,128)(2,1)}, u32[]{:S(2)}, u32[]{:S(2)}) %collective-permute-start.14) | collective-permute-done | bytes 1441824 | tf_op jit(solution)/shard_map/ppermute | solution.py:69
  364.0 6.5 %shard_map.205 = bf16[8,64,1408]{2,1,0:T(8,128)(2,1)} custom-call(bf16[8,64,1408]{2,1,0:T(8,128)(2,1)} %get-tuple-element.59.refs_0_, bf16[8,64,1408]{2,1,0:T(8,128)(2,1)} %copy-done.33, bf16[8,64,1408]{2,1,0:T(8,128)(2,1)} %collective-permute-done.13.refs_2_, bf16[8,64,1408]{2,1,0:T(8,128)(2,1)} %collective-permute-done.14.refs_3_), custom_call_target="tpu_custom_call" | custom-call | flops 40000000000 | bytes 133333336 | tf_op jit(solution)/shard_map/pallas_call | solution.py:301
  370.5 4.2 all-gather.10.cloned.1.call-done
  376.1 2.6 copy.177
  380.8 3.6 dynamic-slice_bitcast_fusion.4
  389.2 15.3 %shard_map.206 = (bf16[1024,256]{1,0:T(8,128)(2,1)}, bf16[1024,64]{1,0:T(8,128)(2,1)}, bf16[1024,64]{1,0:T(8,128)(2,1)}) custom-call(bf16[1024,256]{1,0:T(8,128)(2,1)} %copy.161.q_ref, bf16[1024,64]{1,0:T(8,128)(2,1)} %pad_maximum_fusion.5.k_ref, bf16[1024,64]{1,0:T(8,128)(2,1)} %copy.184.v_ref, bf16[1024,256]{1,0:T(8,128)(2,1)} %convolution_convert_fusion.6.do_ref, ...), custom_call_target="tpu_custom_call" | custom-call | tf_op jit(solution)/shard_map/pallas_call | solution.py:249
  404.5 7.5 %all-to-all-start.2 = ((bf16[8,64,1408]{2,1,0:T(8,128)(2,1)}), bf16[8,64,1408]{2,1,0:T(8,128)(2,1)}, u32[]{:S(2)}, u32[]{:S(2)}) async-start(bf16[8,64,1408]{2,1,0:T(8,128)(2,1)} %shard_map.205), calls=%async_computation.5 | async-start | bytes 2883584 | tf_op jit(solution)/shard_map/all_to_all | solution.py:340
  414.4 4.3 fusion.59
  422.2 4.0 copy.171
  426.2 3.0 dynamic-slice_bitcast_fusion.9
  431.8 4.4 convolution_convert_fusion.1
  436.2 6.5 %collective-permute-done.18 = bf16[8,64,512]{2,1,0:T(8,128)(2,1)} collective-permute-done((bf16[8,64,512]{2,1,0:T(8,128)(2,1)}, bf16[8,64,512]{2,1,0:T(8,128)(2,1)}, u32[]{:S(2)}, u32[]{:S(2)}) %collective-permute-start.18) | collective-permute-done | bytes 524320 | tf_op jit(solution)/shard_map/ppermute | solution.py:69
  443.6 11.2 %collective-permute-done.20 = bf16[8,64,512]{2,1,0:T(8,128)(2,1)} collective-permute-done((bf16[8,64,512]{2,1,0:T(8,128)(2,1)}, bf16[8,64,512]{2,1,0:T(8,128)(2,1)}, u32[]{:S(2)}, u32[]{:S(2)}) %collective-permute-start.20) | collective-permute-done | bytes 524320 | tf_op jit(solution)/shard_map/ppermute | solution.py:69
  454.9 3.5 convolution_convert_fusion.4
  461.2 3.8 collective-permute-done.21
  466.6 4.9 collective-permute-done.23
  471.5 2.5 add_convert_fusion.1
  474.0 9.1 %all-to-all-start.3 = ((bf16[8,64,512]{2,1,0:T(8,128)(2,1)}), bf16[8,64,512]{2,1,0:T(8,128)(2,1)}, u32[]{:S(2)}, u32[]{:S(2)}) async-start(bf16[8,64,512]{2,1,0:T(8,128)(2,1)} %add_convert_fusion.1), calls=%async_computation.7 | async-start | bytes 1048576 | tf_op jit(solution)/shard_map/all_to_all | solution.py:340
  484.0 3.0 convert_bitcast_fusion
  489.6 2.4 copy.176
  493.7 3.1 convert_add_fusion.1
  496.8 6.7 %all-to-all-done.3 = bf16[8,64,512]{2,1,0:T(8,128)(2,1)} async-done(((bf16[8,64,512]{2,1,0:T(8,128)(2,1)}), bf16[8,64,512]{2,1,0:T(8,128)(2,1)}, u32[]{:S(2)}, u32[]{:S(2)}) %all-to-all-start.3) | async-done | bytes 524320 | tf_op jit(solution)/shard_map/all_to_all | solution.py:340
  509.8 6.0 %reduce-scatter.11.cloned.1.call-done = bf16[128,2048]{1,0:T(8,128)(2,1)} async-done(((bf16[1024,2048]{1,0:T(8,128)(2,1)}), bf16[128,2048]{1,0:T(8,128)(2,1)}) %reduce-scatter.11.cloned.1.call-update) | async-done | bytes 524304 | tf_op jit(solution)/shard_map/reduce_scatter | solution.py:110
  517.2 2.9 fusion.22
  (223 shorter events, 108.7 us)
Async XLA Ops:
  7.2 17.9 %copy-start.20 = (bf16[64,5632]{1,0:T(8,128)(2,1)S(1)}, bf16[64,5632]{1,0:T(8,128)(2,1)}, u32[]{:S(2)}) copy-start(bf16[64,5632]{1,0:T(8,128)(2,1)} %param.20) | copy-start | bytes 2162692
  7.2 88.2 %all-gather.12.cloned.1.call-start = ((), (), s32[]{:S(2)}) async-start(), calls=%async_computation.15 | async-start | bytes 4718592 | tf_op jit(solution)/shard_map/all_gather | solution.py:106
  7.9 51.5 %collective-permute-start = (bf16[176,2048]{1,0:T(8,128)(2,1)}, bf16[176,2048]{1,0:T(8,128)(2,1)}, u32[]{:S(2)}, u32[]{:S(2)}) collective-permute-start(bf16[176,2048]{1,0:T(8,128)(2,1)} %param.22), channel_id=1, source_target_pairs={{0,1},{1,0},{2,3},{3,2},{4,5},{5,4},{6,7},{7,6},{8,9},{9,8},{10,11... | collective-permute-start | bytes 2162696 | tf_op jit(solution)/shard_map/ppermute | solution.py:69
  9.2 50.2 %collective-permute-start.1 = (bf16[176,2048]{1,0:T(8,128)(2,1)}, bf16[176,2048]{1,0:T(8,128)(2,1)}, u32[]{:S(2)}, u32[]{:S(2)}) collective-permute-start(bf16[176,2048]{1,0:T(8,128)(2,1)} %param.22), channel_id=1, source_target_pairs={{0,2},{1,3},{2,0},{3,1},{4,6},{5,7},{6,4},{7,5},{8,10},{9,11},{10,... | collective-permute-start | bytes 2162696 | tf_op jit(solution)/shard_map/ppermute | solution.py:69
  10.4 49.0 %collective-permute-start.2 = (bf16[176,2048]{1,0:T(8,128)(2,1)}, bf16[176,2048]{1,0:T(8,128)(2,1)}, u32[]{:S(2)}, u32[]{:S(2)}) collective-permute-start(bf16[176,2048]{1,0:T(8,128)(2,1)} %param.22), channel_id=1, source_target_pairs={{0,3},{1,2},{2,1},{3,0},{4,7},{5,6},{6,5},{7,4},{8,11},{9,10},{10,... | collective-permute-start | bytes 2162696 | tf_op jit(solution)/shard_map/ppermute | solution.py:69
  10.6 35.8 %collective-permute-start.6 = (bf16[64,2048]{1,0:T(8,128)(2,1)}, bf16[64,2048]{1,0:T(8,128)(2,1)S(1)}, u32[]{:S(2)}, u32[]{:S(2)}) collective-permute-start(bf16[64,2048]{1,0:T(8,128)(2,1)} %param.18), channel_id=1, source_target_pairs={{0,1},{1,0},{2,3},{3,2},{4,5},{5,4},{6,7},{7,6},{8,9},{9,8},{10,11... | collective-permute-start | bytes 786440 | tf_op jit(solution)/shard_map/ppermute | solution.py:69
  11.8 46.6 %collective-permute-start.7 = (bf16[64,2048]{1,0:T(8,128)(2,1)}, bf16[64,2048]{1,0:T(8,128)(2,1)}, u32[]{:S(2)}, u32[]{:S(2)}) collective-permute-start(bf16[64,2048]{1,0:T(8,128)(2,1)} %param.18), channel_id=1, source_target_pairs={{0,2},{1,3},{2,0},{3,1},{4,6},{5,7},{6,4},{7,5},{8,10},{9,11},{10,... | collective-permute-start | bytes 786440 | tf_op jit(solution)/shard_map/ppermute | solution.py:69
  18.0 32.5 %all-to-all-start = ((bf16[8,64,512]{2,1,0:T(8,128)(2,1)}), bf16[8,64,512]{2,1,0:T(8,128)(2,1)}, u32[]{:S(2)}, u32[]{:S(2)}) async-start(bf16[8,64,512]{2,1,0:T(8,128)(2,1)} %copy.151), calls=%async_computation | async-start | bytes 1048576 | tf_op jit(solution)/shard_map/all_to_all | solution.py:340
  46.4 13.5 %collective-permute-start.8 = (bf16[64,2048]{1,0:T(8,128)(2,1)S(1)}, bf16[64,2048]{1,0:T(8,128)(2,1)S(1)}, u32[]{:S(2)}, u32[]{:S(2)}) collective-permute-start(bf16[64,2048]{1,0:T(8,128)(2,1)S(1)} %copy-done.25), channel_id=1, source_target_pairs={{0,3},{1,2},{2,1},{3,0},{4,7},{5,6},{6,5},{7,4},{8,11},{9,10},{10,... | collective-permute-start | bytes 786440 | tf_op jit(solution)/shard_map/ppermute | solution.py:69
  50.5 44.9 %all-to-all-start.1 = ((bf16[8,64,1408]{2,1,0:T(8,128)(2,1)}), bf16[8,64,1408]{2,1,0:T(8,128)(2,1)S(1)}, u32[]{:S(2)}, u32[]{:S(2)}) async-start(bf16[8,64,1408]{2,1,0:T(8,128)(2,1)} %pad_maximum_fusion.1), calls=%async_computation.1 | async-start | bytes 2883584 | tf_op jit(solution)/shard_map/all_to_all | solution.py:340
  58.4 91.4 %all-gather.6.cloned.1.call-start = ((), (), s32[]{:S(2)}) async-start(), calls=%async_computation.8 | async-start | bytes 4718592 | tf_op jit(solution)/shard_map/all_gather | solution.py:106
  59.4 13.4 %collective-permute-start.3 = (bf16[8,64,512]{2,1,0:T(8,128)(2,1)}, bf16[8,64,512]{2,1,0:T(8,128)(2,1)S(1)}, u32[]{:S(2)}, u32[]{:S(2)}) collective-permute-start(bf16[8,64,512]{2,1,0:T(8,128)(2,1)} %all-to-all-done), channel_id=1, source_target_pairs={{0,1},{1,0},{2,3},{3,2},{4,5},{5,4},{6,7},{7,6},{8,9},{9,8},{10,11... | collective-permute-start | bytes 1572872 | tf_op jit(solution)/shard_map/ppermute | solution.py:69
  59.9 13.0 %collective-permute-start.4 = (bf16[8,64,512]{2,1,0:T(8,128)(2,1)}, bf16[8,64,512]{2,1,0:T(8,128)(2,1)S(1)}, u32[]{:S(2)}, u32[]{:S(2)}) collective-permute-start(bf16[8,64,512]{2,1,0:T(8,128)(2,1)} %all-to-all-done), channel_id=1, source_target_pairs={{0,2},{1,3},{2,0},{3,1},{4,6},{5,7},{6,4},{7,5},{8,10},{9,11},{10,... | collective-permute-start | bytes 1572872 | tf_op jit(solution)/shard_map/ppermute | solution.py:69
  61.0 23.3 %collective-permute-start.5 = (bf16[8,64,512]{2,1,0:T(8,128)(2,1)}, bf16[8,64,512]{2,1,0:T(8,128)(2,1)S(1)}, u32[]{:S(2)}, u32[]{:S(2)}) collective-permute-start(bf16[8,64,512]{2,1,0:T(8,128)(2,1)} %all-to-all-done), channel_id=1, source_target_pairs={{0,3},{1,2},{2,1},{3,0},{4,7},{5,6},{6,5},{7,4},{8,11},{9,10},{10,... | collective-permute-start | bytes 1572872 | tf_op jit(solution)/shard_map/ppermute | solution.py:69
  84.3 22.0 %copy-start.4 = (bf16[8,4,64,512]{3,2,1,0:T(8,128)(2,1)}, bf16[8,4,64,512]{3,2,1,0:T(8,128)(2,1)S(1)}, u32[]{:S(2)}) copy-start(bf16[8,4,64,512]{3,2,1,0:T(8,128)(2,1)S(1)} %bitcast_dynamic-update-slice_fusion.8) | copy-start | bytes 6291460
  102.0 98.5 %reduce-scatter.5.cloned.1.call-start = ((), (), s32[]{:S(2)}) async-start(), calls=%async_computation.9 | async-start | bytes 4718592 | tf_op jit(solution)/shard_map/reduce_scatter | solution.py:110
  103.8 33.3 %collective-permute-start.10 = (bf16[8,64,1408]{2,1,0:T(8,128)(2,1)S(1)}, bf16[8,64,1408]{2,1,0:T(8,128)(2,1)}, u32[]{:S(2)}, u32[]{:S(2)}) collective-permute-start(bf16[8,64,1408]{2,1,0:T(8,128)(2,1)S(1)} %all-to-all-done.1), channel_id=1, source_target_pairs={{0,2},{1,3},{2,0},{3,1},{4,6},{5,7},{6,4},{7,5},{8,10},{9,11},{10,... | collective-permute-start | bytes 4325384 | tf_op jit(solution)/shard_map/ppermute | solution.py:69
  105.1 32.5 %collective-permute-start.9 = (bf16[8,64,1408]{2,1,0:T(8,128)(2,1)S(1)}, bf16[8,64,1408]{2,1,0:T(8,128)(2,1)}, u32[]{:S(2)}, u32[]{:S(2)}) collective-permute-start(bf16[8,64,1408]{2,1,0:T(8,128)(2,1)S(1)} %all-to-all-done.1), channel_id=1, source_target_pairs={{0,1},{1,0},{2,3},{3,2},{4,5},{5,4},{6,7},{7,6},{8,9},{9,8},{10,11... | collective-permute-start | bytes 4325384 | tf_op jit(solution)/shard_map/ppermute | solution.py:69
  120.9 12.9 %copy-start.12 = (bf16[4,64,2048]{2,1,0:T(8,128)(2,1)S(1)}, bf16[4,64,2048]{2,1,0:T(8,128)(2,1)}, u32[]{:S(2)}) copy-start(bf16[4,64,2048]{2,1,0:T(8,128)(2,1)} %copy-done.11) | copy-start | bytes 3145732
  149.8 99.9 %all-gather.8.cloned.1.call-start = ((), (), s32[]{:S(2)}) async-start(), calls=%async_computation.10 | async-start | bytes 4718592 | tf_op jit(solution)/shard_map/all_gather | solution.py:106
  154.6 33.9 %collective-permute-start.11 = (bf16[8,64,1408]{2,1,0:T(8,128)(2,1)S(1)}, bf16[8,64,1408]{2,1,0:T(8,128)(2,1)S(1)}, u32[]{:S(2)}, u32[]{:S(2)}) collective-permute-start(bf16[8,64,1408]{2,1,0:T(8,128)(2,1)S(1)} %all-to-all-done.1), channel_id=1, source_target_pairs={{0,3},{1,2},{2,1},{3,0},{4,7},{5,6},{6,5},{7,4},{8,11},{9,10},{10,... | collective-permute-start | bytes 4325384 | tf_op jit(solution)/shard_map/ppermute | solution.py:69
  163.8 36.7 %copy-start = (bf16[1,128,2048]{2,1,0:T(8,128)(2,1)S(1)}, bf16[1,128,2048]{2,1,0:T(8,128)(2,1)}, u32[]{:S(2)}) copy-start(bf16[1,128,2048]{2,1,0:T(8,128)(2,1)} %param.12) | copy-start | bytes 1572868
  203.9 121.4 %reduce-scatter.7.cloned.1.call-start = ((), (), s32[]{:S(2)}) async-start(), calls=%async_computation.11 | async-start | bytes 4718592 | tf_op jit(solution)/shard_map/reduce_scatter | solution.py:110
  276.6 98.2 %all-gather.10.cloned.1.call-start = ((), (), s32[]{:S(2)}) async-start(), calls=%async_computation.12 | async-start | bytes 4718592 | tf_op jit(solution)/shard_map/all_gather | solution.py:106
  289.4 33.0 %collective-permute-start.12 = (bf16[8,64,1408]{2,1,0:T(8,128)(2,1)S(1)}, bf16[8,64,1408]{2,1,0:T(8,128)(2,1)S(1)}, u32[]{:S(2)}, u32[]{:S(2)}) collective-permute-start(bf16[8,64,1408]{2,1,0:T(8,128)(2,1)S(1)} %get-tuple-element.90), channel_id=1, source_target_pairs={{0,1},{1,0},{2,3},{3,2},{4,5},{5,4},{6,7},{7,6},{8,9},{9,8},{10,11... | collective-permute-start | bytes 4325384 | tf_op jit(solution)/shard_map/ppermute | solution.py:69
  290.6 32.9 %collective-permute-start.13 = (bf16[8,64,1408]{2,1,0:T(8,128)(2,1)S(1)}, bf16[8,64,1408]{2,1,0:T(8,128)(2,1)}, u32[]{:S(2)}, u32[]{:S(2)}) collective-permute-start(bf16[8,64,1408]{2,1,0:T(8,128)(2,1)S(1)} %get-tuple-element.89), channel_id=1, source_target_pairs={{0,2},{1,3},{2,0},{3,1},{4,6},{5,7},{6,4},{7,5},{8,10},{9,11},{10,... | collective-permute-start | bytes 4325384 | tf_op jit(solution)/shard_map/ppermute | solution.py:69
  291.8 33.5 %copy-start.2 = (bf16[128,2048]{1,0:T(8,128)(2,1)S(1)}, bf16[128,2048]{1,0:T(8,128)(2,1)}, u32[]{:S(2)}) copy-start(bf16[128,2048]{1,0:T(8,128)(2,1)} %reduce-scatter.5.cloned.1.call-done) | copy-start | bytes 1572868
  291.8 35.1 %copy-start.8 = (bf16[1,128,2048]{2,1,0:T(8,128)(2,1)S(1)}, bf16[1,128,2048]{2,1,0:T(8,128)(2,1)}, u32[]{:S(2)}) copy-start(bf16[1,128,2048]{2,1,0:T(8,128)(2,1)} %param.23) | copy-start | bytes 1572868
  329.2 125.6 %reduce-scatter.9.cloned.1.call-start = ((), (), s32[]{:S(2)}) async-start(), calls=%async_computation.13 | async-start | bytes 4718592 | tf_op jit(solution)/shard_map/reduce_scatter | solution.py:110
  329.5 34.5 %collective-permute-start.14 = (bf16[8,64,1408]{2,1,0:T(8,128)(2,1)S(1)}, bf16[8,64,1408]{2,1,0:T(8,128)(2,1)}, u32[]{:S(2)}, u32[]{:S(2)}) collective-permute-start(bf16[8,64,1408]{2,1,0:T(8,128)(2,1)S(1)} %get-tuple-element.88), channel_id=1, source_target_pairs={{0,3},{1,2},{2,1},{3,0},{4,7},{5,6},{6,5},{7,4},{8,11},{9,10},{10,... | collective-permute-start | bytes 4325384 | tf_op jit(solution)/shard_map/ppermute | solution.py:69
  384.4 47.2 %collective-permute-start.15 = (bf16[176,2048]{1,0:T(8,128)(2,1)}, bf16[176,2048]{1,0:T(8,128)(2,1)}, u32[]{:S(2)}, u32[]{:S(2)}) collective-permute-start(bf16[176,2048]{1,0:T(8,128)(2,1)} %get-tuple-element.96), channel_id=1, source_target_pairs={{0,1},{1,0},{2,3},{3,2},{4,5},{5,4},{6,7},{7,6},{8,9},{9,8},{10,11... | collective-permute-start | bytes 2162696 | tf_op jit(solution)/shard_map/ppermute | solution.py:69
  385.6 50.6 %collective-permute-start.16 = (bf16[176,2048]{1,0:T(8,128)(2,1)}, bf16[176,2048]{1,0:T(8,128)(2,1)}, u32[]{:S(2)}, u32[]{:S(2)}) collective-permute-start(bf16[176,2048]{1,0:T(8,128)(2,1)} %get-tuple-element.95), channel_id=1, source_target_pairs={{0,2},{1,3},{2,0},{3,1},{4,6},{5,7},{6,4},{7,5},{8,10},{9,11},{10,... | collective-permute-start | bytes 2162696 | tf_op jit(solution)/shard_map/ppermute | solution.py:69
  386.8 49.4 %collective-permute-start.17 = (bf16[176,2048]{1,0:T(8,128)(2,1)}, bf16[176,2048]{1,0:T(8,128)(2,1)}, u32[]{:S(2)}, u32[]{:S(2)}) collective-permute-start(bf16[176,2048]{1,0:T(8,128)(2,1)} %get-tuple-element.94), channel_id=1, source_target_pairs={{0,3},{1,2},{2,1},{3,0},{4,7},{5,6},{6,5},{7,4},{8,11},{9,10},{10,... | collective-permute-start | bytes 2162696 | tf_op jit(solution)/shard_map/ppermute | solution.py:69
  404.5 50.3 %all-to-all-start.2 = ((bf16[8,64,1408]{2,1,0:T(8,128)(2,1)}), bf16[8,64,1408]{2,1,0:T(8,128)(2,1)}, u32[]{:S(2)}, u32[]{:S(2)}) async-start(bf16[8,64,1408]{2,1,0:T(8,128)(2,1)} %shard_map.205), calls=%async_computation.5 | async-start | bytes 2883584 | tf_op jit(solution)/shard_map/all_to_all | solution.py:340
  412.0 103.8 %reduce-scatter.11.cloned.1.call-start = ((), (), s32[]{:S(2)}) async-start(), calls=%async_computation.14 | async-start | bytes 4718592 | tf_op jit(solution)/shard_map/reduce_scatter | solution.py:110
  429.2 13.5 %collective-permute-start.18 = (bf16[8,64,512]{2,1,0:T(8,128)(2,1)}, bf16[8,64,512]{2,1,0:T(8,128)(2,1)}, u32[]{:S(2)}, u32[]{:S(2)}) collective-permute-start(bf16[8,64,512]{2,1,0:T(8,128)(2,1)} %get-tuple-element.100), channel_id=1, source_target_pairs={{0,1},{1,0},{2,3},{3,2},{4,5},{5,4},{6,7},{7,6},{8,9},{9,8},{10,11... | collective-permute-start | bytes 1572872 | tf_op jit(solution)/shard_map/ppermute | solution.py:69
  430.4 13.3 %collective-permute-start.19 = (bf16[8,64,512]{2,1,0:T(8,128)(2,1)}, bf16[8,64,512]{2,1,0:T(8,128)(2,1)}, u32[]{:S(2)}, u32[]{:S(2)}) collective-permute-start(bf16[8,64,512]{2,1,0:T(8,128)(2,1)} %get-tuple-element.98), channel_id=1, source_target_pairs={{0,2},{1,3},{2,0},{3,1},{4,6},{5,7},{6,4},{7,5},{8,10},{9,11},{10,... | collective-permute-start | bytes 1572872 | tf_op jit(solution)/shard_map/ppermute | solution.py:69
  431.6 23.2 %collective-permute-start.20 = (bf16[8,64,512]{2,1,0:T(8,128)(2,1)}, bf16[8,64,512]{2,1,0:T(8,128)(2,1)}, u32[]{:S(2)}, u32[]{:S(2)}) collective-permute-start(bf16[8,64,512]{2,1,0:T(8,128)(2,1)} %get-tuple-element.99), channel_id=1, source_target_pairs={{0,3},{1,2},{2,1},{3,0},{4,7},{5,6},{6,5},{7,4},{8,11},{9,10},{10,... | collective-permute-start | bytes 1572872 | tf_op jit(solution)/shard_map/ppermute | solution.py:69
  436.2 18.6 %copy-start.15 = (bf16[1024,256]{1,0:T(8,128)(2,1)S(1)}, bf16[1024,256]{1,0:T(8,128)(2,1)}, u32[]{:S(2)}) copy-start(bf16[1024,256]{1,0:T(8,128)(2,1)} %shard_map.203) | copy-start | bytes 1572868
  454.9 16.6 %copy-start.17 = (bf16[8,64,512]{2,1,0:T(8,128)(2,1)S(1)}, bf16[8,64,512]{2,1,0:T(8,128)(2,1)}, u32[]{:S(2)}) copy-start(bf16[8,64,512]{2,1,0:T(8,128)(2,1)} %get-tuple-element.71) | copy-start | bytes 1572868
  458.5 6.5 %collective-permute-start.21 = (bf16[64,2048]{1,0:T(8,128)(2,1)S(1)}, bf16[64,2048]{1,0:T(8,128)(2,1)S(1)}, u32[]{:S(2)}, u32[]{:S(2)}) collective-permute-start(bf16[64,2048]{1,0:T(8,128)(2,1)S(1)} %get-tuple-element.109), channel_id=1, source_target_pairs={{0,1},{1,0},{2,3},{3,2},{4,5},{5,4},{6,7},{7,6},{8,9},{9,8},{10,11... | collective-permute-start | bytes 786440 | tf_op jit(solution)/shard_map/ppermute | solution.py:69
  459.8 6.8 %collective-permute-start.22 = (bf16[64,2048]{1,0:T(8,128)(2,1)S(1)}, bf16[64,2048]{1,0:T(8,128)(2,1)S(1)}, u32[]{:S(2)}, u32[]{:S(2)}) collective-permute-start(bf16[64,2048]{1,0:T(8,128)(2,1)S(1)} %get-tuple-element.108), channel_id=1, source_target_pairs={{0,2},{1,3},{2,0},{3,1},{4,6},{5,7},{6,4},{7,5},{8,10},{9,11},{10,... | collective-permute-start | bytes 786440 | tf_op jit(solution)/shard_map/ppermute | solution.py:69
  460.1 11.4 %collective-permute-start.23 = (bf16[64,2048]{1,0:T(8,128)(2,1)S(1)}, bf16[64,2048]{1,0:T(8,128)(2,1)S(1)}, u32[]{:S(2)}, u32[]{:S(2)}) collective-permute-start(bf16[64,2048]{1,0:T(8,128)(2,1)S(1)} %get-tuple-element.107), channel_id=1, source_target_pairs={{0,3},{1,2},{2,1},{3,0},{4,7},{5,6},{6,5},{7,4},{8,11},{9,10},{10,... | collective-permute-start | bytes 786440 | tf_op jit(solution)/shard_map/ppermute | solution.py:69
  474.0 29.6 %all-to-all-start.3 = ((bf16[8,64,512]{2,1,0:T(8,128)(2,1)}), bf16[8,64,512]{2,1,0:T(8,128)(2,1)}, u32[]{:S(2)}, u32[]{:S(2)}) async-start(bf16[8,64,512]{2,1,0:T(8,128)(2,1)} %add_convert_fusion.1), calls=%async_computation.7 | async-start | bytes 1048576 | tf_op jit(solution)/shard_map/all_to_all | solution.py:340
  496.8 19.0 %copy-start.27 = (f32[1,2048]{1,0:T(1,128)S(1)}, f32[1,2048]{1,0:T(1,128)}, u32[]{:S(2)}) copy-start(f32[1,2048]{1,0:T(1,128)} %get-tuple-element.117) | copy-start | bytes 24580
  496.8 20.4 %copy-start.7 = (bf16[128,2048]{1,0:T(8,128)(2,1)S(1)}, bf16[128,2048]{1,0:T(8,128)(2,1)}, u32[]{:S(2)}) copy-start(bf16[128,2048]{1,0:T(8,128)(2,1)} %reduce-scatter.7.cloned.1.call-done) | copy-start | bytes 1572868
  496.8 20.4 %copy-start.9 = (bf16[1,128,2048]{2,1,0:T(8,128)(2,1)S(1)}, bf16[1,128,2048]{2,1,0:T(8,128)(2,1)}, u32[]{:S(2)}) copy-start(bf16[1,128,2048]{2,1,0:T(8,128)(2,1)} %param.23) | copy-start | bytes 1572868
  496.8 20.4 %copy-start.23 = (bf16[128,2048]{1,0:T(8,128)(2,1)S(1)}, bf16[128,2048]{1,0:T(8,128)(2,1)}, u32[]{:S(2)}) copy-start(bf16[128,2048]{1,0:T(8,128)(2,1)} %reduce-scatter.9.cloned.1.call-done) | copy-start | bytes 1572868
  (22 other events, 92.9 us)
Sparse Core Ops, SparseCore 0:
  9.6 69.1 all-gather.11
  102.1 47.6 all-gather.5
  152.1 48.3 reduce-scatter.4
  204.0 45.6 all-gather.7
  276.7 48.5 reduce-scatter.6
  329.3 45.4 all-gather.9
  377.1 74.1 reduce-scatter.8
  455.0 60.7 reduce-scatter.10

commit v4 on v3

--- a/solution.py
+++ b/solution.py
@@ -16,7 +16,6 @@
 BF = jnp.bfloat16
 F32 = jnp.float32
 FFN_ROWS = 256
-SUM_COST = 40 * 10**9
 
 
 def rms_parts(values):
@@ -175,13 +174,12 @@
     o_ref[...] = jnp.concatenate(outs, axis=1)
 
 
-def attend_back_kernel(half, q_ref, k_ref, v_ref, do_ref, kr_ref, qr_ref, cos_ref, sin_ref, col_ref, row_ref, dq_ref, dk_ref, dv_ref, acc_ref):
+def attend_back_kernel(half, q_ref, k_ref, v_ref, do_ref, cos_ref, sin_ref, col_ref, row_ref, dq_ref, dk_ref, dv_ref, acc_ref):
     scale = HD ** (-0.5)
     cols = halves_of(col_ref[...], half)
     rows_pos = [row_ref[0:1], row_ref[1:2]]
     k_pair, v_pair = halves_of(k_ref[...], half), halves_of(v_ref[...], half)
-    kr_pair = halves_of(kr_ref[...], half)
-    kk = [jnp.concatenate([k_pair[i], kr_pair[i]], axis=1) for i in range(2)]
+    kk = [jnp.concatenate([k_pair[i], turn(k_pair[i])], axis=1) for i in range(2)]
     cos_pair, sin_pair = halves_of(cos_ref[...], half), halves_of(sin_ref[...], half)
 
     @pl.when(pl.program_id(0) == 0)
@@ -193,8 +191,7 @@
         lanes = slice(j * HD, (j + 1) * HD)
         q_pair = halves_of(q_ref[:, lanes], half)
         do_pair = halves_of(do_ref[:, lanes], half)
-        qr_pair = halves_of(qr_ref[:, lanes], half)
-        qq = [jnp.concatenate([q_pair[i], qr_pair[i]], axis=1) for i in range(2)]
+        qq = [jnp.concatenate([q_pair[i], turn(q_pair[i])], axis=1) for i in range(2)]
         p_aa, p_ba, p_bb = soft_parts(q_pair, k_pair, cols, rows_pos)
         g_aa = dot_nt(do_pair[0], v_pair[0])
         g_ba = dot_nt(do_pair[1], v_pair[0])
@@ -243,18 +240,18 @@
     )(q, k, v, col, row)
 
 
-def attend_back(q, k, v, do, kr, qr, cos, sin, col, row, half):
+def attend_back(q, k, v, do, cos, sin, col, row, half):
     seq, q_cols = q.shape
     by_pair = pl.BlockSpec((seq, 2 * HD), lambda g: (0, g))
     return pl.pallas_call(
         functools.partial(attend_back_kernel, half),
         grid=(q_cols // (2 * HD),),
-        in_specs=[by_pair, whole(k.shape), whole(v.shape), by_pair, whole(kr.shape), by_pair, whole(cos.shape), whole(sin.shape), whole(col.shape), whole(row.shape)],
+        in_specs=[by_pair, whole(k.shape), whole(v.shape), by_pair, whole(cos.shape), whole(sin.shape), whole(col.shape), whole(row.shape)],
         out_specs=[by_pair, whole(k.shape), whole(v.shape)],
         out_shape=[jax.ShapeDtypeStruct((seq, q_cols), BF), jax.ShapeDtypeStruct(k.shape, BF), jax.ShapeDtypeStruct(v.shape, BF)],
         scratch_shapes=[pltpu.VMEM((2, seq // 2, 4 * HD), F32)],
         compiler_params=pltpu.CompilerParams(vmem_limit_bytes=56 * 2**20),
-    )(q, k, v, do, kr, qr, cos, sin, col, row)
+    )(q, k, v, do, cos, sin, col, row)
 
 
 def ffn_kernel(h_ref, g_ref, wgu_ref, wd_ref, z_ref, dgu_ref, out_ref, dh_ref):
@@ -286,26 +283,6 @@
         out_shape=[jax.ShapeDtypeStruct((seq, ff), BF), jax.ShapeDtypeStruct((seq, 2 * ff), BF), jax.ShapeDtypeStruct((seq, width), BF), jax.ShapeDtypeStruct((seq, width), BF)],
         compiler_params=pltpu.CompilerParams(vmem_limit_bytes=56 * 2**20),
     )(h, g, w_gu, w_d)
-
-
-def sum_kernel(*refs):
-    total = refs[0][...].astype(F32)
-    for ref in refs[1:-1]:
-        total = total + ref[...].astype(F32)
-    refs[-1][...] = total.astype(refs[-1].dtype)
-
-
-def sum_pieces(pieces, cost):
-    shape = pieces[0].shape
-    block = pl.BlockSpec((1,) + shape[1:], lambda i: (i, 0, 0))
-    return pl.pallas_call(
-        sum_kernel,
-        grid=(shape[0],),
-        in_specs=[block] * len(pieces),
-        out_specs=block,
-        out_shape=jax.ShapeDtypeStruct(shape, BF),
-        cost_estimate=pl.CostEstimate(flops=cost, bytes_accessed=cost // 300, transcendentals=0),
-    )(*pieces)
 
 
 def on_device(
@@ -375,20 +352,18 @@
     gu_pieces = fetch_f(moved_gu, f_count)
 
     x_seen = after(x_all, w_qkvg, w_o, moved_gu, cos_wide, sin_wide, pos_col, pos_row)
+    g_all = gather_c(after(cotangent[0], x_seen))
     normed_all, _ = rms_parts(x_seen.astype(F32))
     h1 = (normed_all * gain_a).astype(BF)
-    g_all = gather_c(after(cotangent[0], h1))
     qkv = dot(h1, w_qkv)
     q = rotate(qkv[:, :q_cols].reshape(seq, heads, HD), cos_table, sin_table).astype(BF)
     k = rotate(qkv[:, None, q_cols : q_cols + HD], cos_table, sin_table).astype(BF)
-    q_turn = turn(q).reshape(seq, q_cols)
-    k_turn = turn(k)[:, 0]
     q = q.reshape(seq, q_cols)
     k = k[:, 0]
     v = qkv[:, q_cols + HD :].astype(BF)
     o = attend(q, k, v, pos_col, pos_row, half)
     y_part = dot(o, w_o).astype(BF)
-    y_rows = scatter_c(after(y_part, g_all, q_turn, k_turn, *gu_pieces[:3]))
+    y_rows = scatter_c(after(y_part, g_all, *gu_pieces[:3]))
 
     source = tokens[0].astype(F32)
     residual = source + y_rows.astype(F32)
@@ -410,14 +385,14 @@
     d_res = cotangent[0].astype(F32) + norm_back(d_h * gain_f, normed_f, recip_f)
     ab_rows = d_res.astype(BF)
     ab = gather_c(ab_rows)
-    sum_gu = sum_pieces([after(piece, ab_rows) for piece in sent_gu], SUM_COST)
+    sum_gu = total_f(sent_gu, ab_rows).astype(BF)
     ab = after(ab, sum_gu)
     out_rows = scatter_c(after(out_part, ab))
 
     d_o = dot_nt(ab, w_o).astype(BF)
     owned_gu = to_dest(after(sum_gu, d_o))
     dq, dk, dv = attend_back(
-        q, k, v, d_o, k_turn, q_turn, cos_wide, sin_wide, pos_col, pos_row, half
+        q, k, v, d_o, cos_wide, sin_wide, pos_col, pos_row, half
     )
     dqkv = jnp.concatenate([dq, dk, dv], axis=1)
     grad_qkv = dot_tn(h1, dqkv)

time: 536 us -> 527 us (0.983)
  waiting for transfers between devices: 242 us -> 249 us
  Pallas kernels: 57.6 us -> 51.8 us
    all_to_all x4, waiting for transfers between devices: 18.1 us -> 28.1 us  [to_dest(): lax.all_to_all(packed, 'ctx', split_axis=0, concat_axis=0, tiled=True)]
    pallas_call x1 -> x0, Pallas kernels: 6.55 us -> none  [sum_pieces(): pl.pallas_call(sum_kernel, grid=(shape[0],), in_specs=[block] * len(piece...]
    ppermute x24, waiting for transfers between devices: 142 us -> 137 us  [swap_f(): return lax.ppermute(value, 'fsdp', [(i, i ^ step) for i in range(f_count)])]
    unnamed x74 -> x84, local copies, waits for them, and re-layouts: 13.6 us -> 13.4 us
  transfers between devices with their start and end apart: 36 -> 36, of which waited for: 23 -> 24; matrix products, arithmetic and copies ran while one was open for 24% -> 25% of each run, Pallas kernels for 6% -> 5%
where the time goes in v4:
time: 527 us; the launch traced here: 520 us
  waiting for transfers between devices  249 us (47%)
  local copies, waits for them, and re-layouts  61.4 us (12%)
  starting transfers between devices  59.1 us (11%)
  Pallas kernels  51.8 us (10%)
  other arithmetic  49 us (9%)
  matrix products  35.3 us (7%)
  between operations  15.4 us (3%)
    ppermute x24, waiting for transfers between devices, swap_f(): return lax.ppermute(value, 'fsdp', [(i, i ^ step) for i in range(f_count)])  137 us
    all_gather x4, waiting for transfers between devices, gather_c(): return lax.all_gather(rows, 'ctx', axis=0, tiled=True)  63.9 us
    all_to_all x4, starting transfers between devices, to_dest(): lax.all_to_all(packed, 'ctx', split_axis=0, concat_axis=0, tiled=True)  32.4 us
    all_to_all x4, waiting for transfers between devices, to_dest(): lax.all_to_all(packed, 'ctx', split_axis=0, concat_axis=0, tiled=True)  28.1 us
    pallas_call x1, Pallas kernels, ffn(): pl.pallas_call(ffn_kernel, grid=(seq // block,), in_specs=[rows, rows, wh...  26.8 us
    ppermute x24, starting transfers between devices, swap_f(): return lax.ppermute(value, 'fsdp', [(i, i ^ step) for i in range(f_count)])  25.2 us
    dot_general x5, matrix products, dot_tn(): lax.dot_general(a, b, (((0,), (0,)), ((), ())), preferred_element_type=F32)  22.2 us
    reduce_scatter x4, waiting for transfers between devices, scatter_c(): return lax.psum_scatter(full, 'ctx', scatter_dimension=0, tiled=True)  18.8 us
  transfers between devices with their start and end apart: 36, of which 24 were waited for; matrix products, arithmetic and copies ran while one was open for 25% of the time, Pallas kernels for 5%

profile of v4, /device:TPU:9, one launch (start us, length us, event | category | flops | bytes accessed | tf_op | source)
XLA Modules:
  0.0 520.5 jit_solution(8325853305452421978)
XLA Ops:
  18.0 7.0 %all-to-all-start = ((bf16[8,64,512]{2,1,0:T(8,128)(2,1)}), bf16[8,64,512]{2,1,0:T(8,128)(2,1)}, u32[]{:S(2)}, u32[]{:S(2)}) async-start(bf16[8,64,512]{2,1,0:T(8,128)(2,1)} %copy.141), calls=%async_computation | async-start | bytes 1048576 | tf_op jit(solution)/shard_map/all_to_all | solution.py:317
  26.9 3.1 multiply_sine_fusion
  33.6 16.9 %all-to-all-done = bf16[8,64,512]{2,1,0:T(8,128)(2,1)} async-done(((bf16[8,64,512]{2,1,0:T(8,128)(2,1)}), bf16[8,64,512]{2,1,0:T(8,128)(2,1)}, u32[]{:S(2)}, u32[]{:S(2)}) %all-to-all-start) | async-done | bytes 524320 | tf_op jit(solution)/shard_map/all_to_all | solution.py:317
  50.5 7.9 %all-to-all-start.1 = ((bf16[8,64,1408]{2,1,0:T(8,128)(2,1)}), bf16[8,64,1408]{2,1,0:T(8,128)(2,1)S(1)}, u32[]{:S(2)}, u32[]{:S(2)}) async-start(bf16[8,64,1408]{2,1,0:T(8,128)(2,1)} %pad_maximum_fusion.1), calls=%async_computation.1 | async-start | bytes 2883584 | tf_op jit(solution)/shard_map/all_to_all | solution.py:317
  64.5 4.0 collective-permute-done.8
  71.2 7.7 %collective-permute-done.3 = bf16[8,64,512]{2,1,0:T(8,128)(2,1)S(1)} collective-permute-done((bf16[8,64,512]{2,1,0:T(8,128)(2,1)}, bf16[8,64,512]{2,1,0:T(8,128)(2,1)S(1)}, u32[]{:S(2)}, u32[]{:S(2)}) %collective-permute-start.3) | collective-permute-done | bytes 524320 | tf_op jit(solution)/shard_map/ppermute | solution.py:68
  81.0 9.9 %collective-permute-done.5 = bf16[8,64,512]{2,1,0:T(8,128)(2,1)S(1)} collective-permute-done((bf16[8,64,512]{2,1,0:T(8,128)(2,1)}, bf16[8,64,512]{2,1,0:T(8,128)(2,1)S(1)}, u32[]{:S(2)}, u32[]{:S(2)}) %collective-permute-start.5) | collective-permute-done | bytes 524320 | tf_op jit(solution)/shard_map/ppermute | solution.py:68
  91.0 4.5 all-to-all-done.1
  100.7 3.1 fusion
  111.5 3.1 fusion.33
  115.5 8.8 %shard_map.203 = bf16[1024,256]{1,0:T(8,128)(2,1)} custom-call(bf16[1024,256]{1,0:T(8,128)(2,1)} %copy.151.q_ref, bf16[1024,64]{1,0:T(8,128)(2,1)} %pad_maximum_fusion.5.k_ref, bf16[1024,64]{1,0:T(8,128)(2,1)} %copy.173.v_ref, s32[1024,1]{1,0:T(8,128)} %fusion.23.col_ref, s32[2,512]{1,0:T(2,128)} %reshape.347.row_ref), custom_call_target="tpu_custom_call" | custom-call | tf_op jit(solution)/shard_map/pallas_call | solution.py:233
  124.3 4.3 convolution_convert_fusion.2
  128.6 2.4 collective-permute-done.10
  131.9 11.4 %all-gather.6.cloned.1.call-done.g_ref = bf16[1024,2048]{1,0:T(8,128)(2,1)} async-done(((bf16[128,2048]{1,0:T(8,128)(2,1)}), bf16[1024,2048]{1,0:T(8,128)(2,1)}) %all-gather.6.cloned.1.call-update) | async-done | bytes 4194320 | tf_op jit(solution)/shard_map/all_gather | solution.py:105
  149.5 3.2 broadcast_in_dim.126
  154.0 2.6 bitcast_dynamic-update-slice_fusion.1
  156.6 2.6 bitcast_dynamic-update-slice_fusion
  159.2 22.1 %collective-permute-done.11 = bf16[8,64,1408]{2,1,0:T(8,128)(2,1)S(1)} collective-permute-done((bf16[8,64,1408]{2,1,0:T(8,128)(2,1)S(1)}, bf16[8,64,1408]{2,1,0:T(8,128)(2,1)S(1)}, u32[]{:S(2)}, u32[]{:S(2)}) %collective-permute-start.11) | collective-permute-done | bytes 1441824 | tf_op jit(solution)/shard_map/ppermute | solution.py:68
  182.5 11.5 %reduce-scatter.5.cloned.1.call-done = bf16[128,2048]{1,0:T(8,128)(2,1)} async-done(((bf16[1024,2048]{1,0:T(8,128)(2,1)}), bf16[128,2048]{1,0:T(8,128)(2,1)}) %reduce-scatter.5.cloned.1.call-update) | async-done | bytes 524304 | tf_op jit(solution)/shard_map/reduce_scatter | solution.py:109
  197.6 45.6 %all-gather.8.cloned.1.call-done.h_ref = bf16[1024,2048]{1,0:T(8,128)(2,1)} async-done(((bf16[128,2048]{1,0:T(8,128)(2,1)}), bf16[1024,2048]{1,0:T(8,128)(2,1)}) %all-gather.8.cloned.1.call-update) | async-done | bytes 4194320 | tf_op jit(solution)/shard_map/all_gather | solution.py:105
  243.2 26.8 %shard_map.204 = (bf16[1024,704]{1,0:T(8,128)(2,1)}, bf16[1024,1408]{1,0:T(8,128)(2,1)}, bf16[1024,2048]{1,0:T(8,128)(2,1)}, bf16[1024,2048]{1,0:T(8,128)(2,1)}) custom-call(bf16[1024,2048]{1,0:T(8,128)(2,1)} %all-gather.8.cloned.1.call-done.h_ref, bf16[1024,2048]{1,0:T(8,128)(2,1)} %all-gather.6.cloned.1.call-done.g_ref, ...), custom_call_target="tpu_custom_call" | custom-call | tf_op jit(solution)/shard_map/pallas_call | solution.py:278
  271.8 9.4 %convolution_convert_fusion = bf16[2048,1408]{1,0:T(8,128)(2,1)S(1)} fusion(bf16[1024,2048]{1,0:T(8,128)(2,1)} %all-gather.8.cloned.1.call-done.h_ref, bf16[1024,1408]{1,0:T(8,128)(2,1)S(1)} %copy-done.37), kind=kOutput, calls=%fused_computation.5 | convolution fusion | flops 5908463616 | bytes 12845056 | tf_op jit(solution)/shard_map/dot_general | solution.py:135
  285.3 4.6 convolution_convert_fusion.3
  289.8 26.1 %collective-permute-done.12 = bf16[8,64,1408]{2,1,0:T(8,128)(2,1)S(1)} collective-permute-done((bf16[8,64,1408]{2,1,0:T(8,128)(2,1)S(1)}, bf16[8,64,1408]{2,1,0:T(8,128)(2,1)S(1)}, u32[]{:S(2)}, u32[]{:S(2)}) %collective-permute-start.12) | collective-permute-done | bytes 1441824 | tf_op jit(solution)/shard_map/ppermute | solution.py:68
  324.8 32.8 %collective-permute-done.14 = bf16[8,64,1408]{2,1,0:T(8,128)(2,1)S(1)} collective-permute-done((bf16[8,64,1408]{2,1,0:T(8,128)(2,1)}, bf16[8,64,1408]{2,1,0:T(8,128)(2,1)S(1)}, u32[]{:S(2)}, u32[]{:S(2)}) %collective-permute-start.14) | collective-permute-done | bytes 1441824 | tf_op jit(solution)/shard_map/ppermute | solution.py:68
  357.7 3.7 add_convert_fusion
  361.3 6.9 %all-gather.10.cloned.1.call-done = bf16[1024,2048]{1,0:T(8,128)(2,1)} async-done(((bf16[128,2048]{1,0:T(8,128)(2,1)}), bf16[1024,2048]{1,0:T(8,128)(2,1)}) %all-gather.10.cloned.1.call-update) | async-done | bytes 4194320 | tf_op jit(solution)/shard_map/all_gather | solution.py:105
  369.6 2.6 copy.166
  372.2 3.7 dynamic-slice_bitcast_fusion.4
  380.7 16.2 %shard_map.205 = (bf16[1024,256]{1,0:T(8,128)(2,1)}, bf16[1024,64]{1,0:T(8,128)(2,1)}, bf16[1024,64]{1,0:T(8,128)(2,1)}) custom-call(bf16[1024,256]{1,0:T(8,128)(2,1)} %copy.151.q_ref, bf16[1024,64]{1,0:T(8,128)(2,1)} %pad_maximum_fusion.5.k_ref, bf16[1024,64]{1,0:T(8,128)(2,1)} %copy.173.v_ref, bf16[1024,256]{1,0:T(8,128)(2,1)} %convolution_convert_fusion.6.do_ref, ...), custom_call_target="tpu_custom_call" | custom-call | tf_op jit(solution)/shard_map/pallas_call | solution.py:246
  396.9 7.1 %all-to-all-start.2 = ((bf16[8,64,1408]{2,1,0:T(8,128)(2,1)}), bf16[8,64,1408]{2,1,0:T(8,128)(2,1)}, u32[]{:S(2)}, u32[]{:S(2)}) async-start(bf16[8,64,1408]{2,1,0:T(8,128)(2,1)} %add_convert_fusion), calls=%async_computation.5 | async-start | bytes 2883584 | tf_op jit(solution)/shard_map/all_to_all | solution.py:317
  406.4 4.4 fusion.7
  414.4 4.0 copy.160
  418.4 3.0 dynamic-slice_bitcast_fusion.9
  424.0 4.4 convolution_convert_fusion.1
  428.4 6.5 %collective-permute-done.18 = bf16[8,64,512]{2,1,0:T(8,128)(2,1)} collective-permute-done((bf16[8,64,512]{2,1,0:T(8,128)(2,1)}, bf16[8,64,512]{2,1,0:T(8,128)(2,1)}, u32[]{:S(2)}, u32[]{:S(2)}) %collective-permute-start.18) | collective-permute-done | bytes 524320 | tf_op jit(solution)/shard_map/ppermute | solution.py:68
  435.8 11.2 %collective-permute-done.20 = bf16[8,64,512]{2,1,0:T(8,128)(2,1)} collective-permute-done((bf16[8,64,512]{2,1,0:T(8,128)(2,1)}, bf16[8,64,512]{2,1,0:T(8,128)(2,1)}, u32[]{:S(2)}, u32[]{:S(2)}) %collective-permute-start.20) | collective-permute-done | bytes 524320 | tf_op jit(solution)/shard_map/ppermute | solution.py:68
  447.1 3.5 convolution_convert_fusion.4
  453.4 3.8 collective-permute-done.21
  459.4 4.3 collective-permute-done.23
  463.7 2.5 add_convert_fusion.2
  466.2 10.3 %all-to-all-start.3 = ((bf16[8,64,512]{2,1,0:T(8,128)(2,1)}), bf16[8,64,512]{2,1,0:T(8,128)(2,1)}, u32[]{:S(2)}, u32[]{:S(2)}) async-start(bf16[8,64,512]{2,1,0:T(8,128)(2,1)} %add_convert_fusion.2), calls=%async_computation.7 | async-start | bytes 1048576 | tf_op jit(solution)/shard_map/all_to_all | solution.py:317
  477.5 3.0 convert_bitcast_fusion
  483.1 2.4 copy.165
  487.2 3.1 convert_add_fusion.1
  490.3 6.7 %all-to-all-done.3 = bf16[8,64,512]{2,1,0:T(8,128)(2,1)} async-done(((bf16[8,64,512]{2,1,0:T(8,128)(2,1)}), bf16[8,64,512]{2,1,0:T(8,128)(2,1)}, u32[]{:S(2)}, u32[]{:S(2)}) %all-to-all-start.3) | async-done | bytes 524320 | tf_op jit(solution)/shard_map/all_to_all | solution.py:317
  503.3 5.6 %reduce-scatter.11.cloned.1.call-done = bf16[128,2048]{1,0:T(8,128)(2,1)} async-done(((bf16[1024,2048]{1,0:T(8,128)(2,1)}), bf16[128,2048]{1,0:T(8,128)(2,1)}) %reduce-scatter.11.cloned.1.call-update) | async-done | bytes 524304 | tf_op jit(solution)/shard_map/reduce_scatter | solution.py:109
  510.3 2.9 fusion.26
  (226 shorter events, 101.9 us)
Async XLA Ops:
  7.2 17.9 %copy-start.22 = (bf16[64,5632]{1,0:T(8,128)(2,1)S(1)}, bf16[64,5632]{1,0:T(8,128)(2,1)}, u32[]{:S(2)}) copy-start(bf16[64,5632]{1,0:T(8,128)(2,1)} %param.20) | copy-start | bytes 2162692
  7.2 88.2 %all-gather.12.cloned.1.call-start = ((), (), s32[]{:S(2)}) async-start(), calls=%async_computation.15 | async-start | bytes 4718592 | tf_op jit(solution)/shard_map/all_gather | solution.py:105
  7.9 53.8 %collective-permute-start = (bf16[176,2048]{1,0:T(8,128)(2,1)}, bf16[176,2048]{1,0:T(8,128)(2,1)}, u32[]{:S(2)}, u32[]{:S(2)}) collective-permute-start(bf16[176,2048]{1,0:T(8,128)(2,1)} %param.22), channel_id=1, source_target_pairs={{0,1},{1,0},{2,3},{3,2},{4,5},{5,4},{6,7},{7,6},{8,9},{9,8},{10,11... | collective-permute-start | bytes 2162696 | tf_op jit(solution)/shard_map/ppermute | solution.py:68
  9.2 52.5 %collective-permute-start.1 = (bf16[176,2048]{1,0:T(8,128)(2,1)}, bf16[176,2048]{1,0:T(8,128)(2,1)}, u32[]{:S(2)}, u32[]{:S(2)}) collective-permute-start(bf16[176,2048]{1,0:T(8,128)(2,1)} %param.22), channel_id=1, source_target_pairs={{0,2},{1,3},{2,0},{3,1},{4,6},{5,7},{6,4},{7,5},{8,10},{9,11},{10,... | collective-permute-start | bytes 2162696 | tf_op jit(solution)/shard_map/ppermute | solution.py:68
  10.4 51.3 %collective-permute-start.2 = (bf16[176,2048]{1,0:T(8,128)(2,1)}, bf16[176,2048]{1,0:T(8,128)(2,1)}, u32[]{:S(2)}, u32[]{:S(2)}) collective-permute-start(bf16[176,2048]{1,0:T(8,128)(2,1)} %param.22), channel_id=1, source_target_pairs={{0,3},{1,2},{2,1},{3,0},{4,7},{5,6},{6,5},{7,4},{8,11},{9,10},{10,... | collective-permute-start | bytes 2162696 | tf_op jit(solution)/shard_map/ppermute | solution.py:68
  10.6 49.1 %collective-permute-start.6 = (bf16[64,2048]{1,0:T(8,128)(2,1)}, bf16[64,2048]{1,0:T(8,128)(2,1)}, u32[]{:S(2)}, u32[]{:S(2)}) collective-permute-start(bf16[64,2048]{1,0:T(8,128)(2,1)} %param.18), channel_id=1, source_target_pairs={{0,1},{1,0},{2,3},{3,2},{4,5},{5,4},{6,7},{7,6},{8,9},{9,8},{10,11... | collective-permute-start | bytes 786440 | tf_op jit(solution)/shard_map/ppermute | solution.py:68
  11.8 48.9 %collective-permute-start.7 = (bf16[64,2048]{1,0:T(8,128)(2,1)}, bf16[64,2048]{1,0:T(8,128)(2,1)}, u32[]{:S(2)}, u32[]{:S(2)}) collective-permute-start(bf16[64,2048]{1,0:T(8,128)(2,1)} %param.18), channel_id=1, source_target_pairs={{0,2},{1,3},{2,0},{3,1},{4,6},{5,7},{6,4},{7,5},{8,10},{9,11},{10,... | collective-permute-start | bytes 786440 | tf_op jit(solution)/shard_map/ppermute | solution.py:68
  18.0 32.5 %all-to-all-start = ((bf16[8,64,512]{2,1,0:T(8,128)(2,1)}), bf16[8,64,512]{2,1,0:T(8,128)(2,1)}, u32[]{:S(2)}, u32[]{:S(2)}) async-start(bf16[8,64,512]{2,1,0:T(8,128)(2,1)} %copy.141), calls=%async_computation | async-start | bytes 1048576 | tf_op jit(solution)/shard_map/all_to_all | solution.py:317
  26.8 69.2 %copy-start.32 = (f32[32]{0:T(128)}, f32[32]{0:T(128)S(1)}, u32[]{:S(2)}) copy-start(f32[32]{0:T(128)S(1)} %negate_power_fusion) | copy-start | bytes 388
  26.9 69.2 %copy-start.31 = (f32[1024]{0:T(1024)}, f32[1024]{0:T(1024)S(1)}, u32[]{:S(2)}) copy-start(f32[1024]{0:T(1024)S(1)} %fusion.49) | copy-start | bytes 12292
  31.9 26.5 %copy-start.17 = (f32[1024,1,32]{2,0,1:T(8,128)S(1)}, f32[1024,1,32]{2,0,1:T(8,128)}, u32[]{:S(2)}) copy-start(f32[1024,1,32]{2,0,1:T(8,128)} %get-tuple-element.118) | copy-start | bytes 393220
  32.8 25.7 %copy-start.18 = (f32[1024,1,32]{2,0,1:T(8,128)S(1)}, f32[1024,1,32]{2,0,1:T(8,128)}, u32[]{:S(2)}) copy-start(f32[1024,1,32]{2,0,1:T(8,128)} %get-tuple-element.119) | copy-start | bytes 393220
  50.5 44.9 %all-to-all-start.1 = ((bf16[8,64,1408]{2,1,0:T(8,128)(2,1)}), bf16[8,64,1408]{2,1,0:T(8,128)(2,1)S(1)}, u32[]{:S(2)}, u32[]{:S(2)}) async-start(bf16[8,64,1408]{2,1,0:T(8,128)(2,1)} %pad_maximum_fusion.1), calls=%async_computation.1 | async-start | bytes 2883584 | tf_op jit(solution)/shard_map/all_to_all | solution.py:317
  58.4 84.9 %all-gather.6.cloned.1.call-start = ((), (), s32[]{:S(2)}) async-start(), calls=%async_computation.8 | async-start | bytes 4718592 | tf_op jit(solution)/shard_map/all_gather | solution.py:105
  59.8 8.7 %collective-permute-start.8 = (bf16[64,2048]{1,0:T(8,128)(2,1)}, bf16[64,2048]{1,0:T(8,128)(2,1)S(1)}, u32[]{:S(2)}, u32[]{:S(2)}) collective-permute-start(bf16[64,2048]{1,0:T(8,128)(2,1)} %param.18), channel_id=1, source_target_pairs={{0,3},{1,2},{2,1},{3,0},{4,7},{5,6},{6,5},{7,4},{8,11},{9,10},{10,... | collective-permute-start | bytes 786440 | tf_op jit(solution)/shard_map/ppermute | solution.py:68
  61.7 17.1 %collective-permute-start.3 = (bf16[8,64,512]{2,1,0:T(8,128)(2,1)}, bf16[8,64,512]{2,1,0:T(8,128)(2,1)S(1)}, u32[]{:S(2)}, u32[]{:S(2)}) collective-permute-start(bf16[8,64,512]{2,1,0:T(8,128)(2,1)} %all-to-all-done), channel_id=1, source_target_pairs={{0,1},{1,0},{2,3},{3,2},{4,5},{5,4},{6,7},{7,6},{8,9},{9,8},{10,11... | collective-permute-start | bytes 1572872 | tf_op jit(solution)/shard_map/ppermute | solution.py:68
  63.4 17.6 %collective-permute-start.4 = (bf16[8,64,512]{2,1,0:T(8,128)(2,1)}, bf16[8,64,512]{2,1,0:T(8,128)(2,1)S(1)}, u32[]{:S(2)}, u32[]{:S(2)}) collective-permute-start(bf16[8,64,512]{2,1,0:T(8,128)(2,1)} %all-to-all-done), channel_id=1, source_target_pairs={{0,2},{1,3},{2,0},{3,1},{4,6},{5,7},{6,4},{7,5},{8,10},{9,11},{10,... | collective-permute-start | bytes 1572872 | tf_op jit(solution)/shard_map/ppermute | solution.py:68
  69.4 21.5 %collective-permute-start.5 = (bf16[8,64,512]{2,1,0:T(8,128)(2,1)}, bf16[8,64,512]{2,1,0:T(8,128)(2,1)S(1)}, u32[]{:S(2)}, u32[]{:S(2)}) collective-permute-start(bf16[8,64,512]{2,1,0:T(8,128)(2,1)} %all-to-all-done), channel_id=1, source_target_pairs={{0,3},{1,2},{2,1},{3,0},{4,7},{5,6},{6,5},{7,4},{8,11},{9,10},{10,... | collective-permute-start | bytes 1572872 | tf_op jit(solution)/shard_map/ppermute | solution.py:68
  95.5 98.5 %reduce-scatter.5.cloned.1.call-start = ((), (), s32[]{:S(2)}) async-start(), calls=%async_computation.9 | async-start | bytes 4718592 | tf_op jit(solution)/shard_map/reduce_scatter | solution.py:109
  98.2 32.8 %collective-permute-start.10 = (bf16[8,64,1408]{2,1,0:T(8,128)(2,1)S(1)}, bf16[8,64,1408]{2,1,0:T(8,128)(2,1)}, u32[]{:S(2)}, u32[]{:S(2)}) collective-permute-start(bf16[8,64,1408]{2,1,0:T(8,128)(2,1)S(1)} %all-to-all-done.1), channel_id=1, source_target_pairs={{0,2},{1,3},{2,0},{3,1},{4,6},{5,7},{6,4},{7,5},{8,10},{9,11},{10,... | collective-permute-start | bytes 4325384 | tf_op jit(solution)/shard_map/ppermute | solution.py:68
  99.4 32.5 %collective-permute-start.9 = (bf16[8,64,1408]{2,1,0:T(8,128)(2,1)S(1)}, bf16[8,64,1408]{2,1,0:T(8,128)(2,1)}, u32[]{:S(2)}, u32[]{:S(2)}) collective-permute-start(bf16[8,64,1408]{2,1,0:T(8,128)(2,1)S(1)} %all-to-all-done.1), channel_id=1, source_target_pairs={{0,1},{1,0},{2,3},{3,2},{4,5},{5,4},{6,7},{7,6},{8,9},{9,8},{10,11... | collective-permute-start | bytes 4325384 | tf_op jit(solution)/shard_map/ppermute | solution.py:68
  143.3 99.9 %all-gather.8.cloned.1.call-start = ((), (), s32[]{:S(2)}) async-start(), calls=%async_computation.10 | async-start | bytes 4718592 | tf_op jit(solution)/shard_map/all_gather | solution.py:105
  147.4 33.9 %collective-permute-start.11 = (bf16[8,64,1408]{2,1,0:T(8,128)(2,1)S(1)}, bf16[8,64,1408]{2,1,0:T(8,128)(2,1)S(1)}, u32[]{:S(2)}, u32[]{:S(2)}) collective-permute-start(bf16[8,64,1408]{2,1,0:T(8,128)(2,1)S(1)} %all-to-all-done.1), channel_id=1, source_target_pairs={{0,3},{1,2},{2,1},{3,0},{4,7},{5,6},{6,5},{7,4},{8,11},{9,10},{10,... | collective-permute-start | bytes 4325384 | tf_op jit(solution)/shard_map/ppermute | solution.py:68
  156.5 37.4 %copy-start = (bf16[1,128,2048]{2,1,0:T(8,128)(2,1)S(1)}, bf16[1,128,2048]{2,1,0:T(8,128)(2,1)}, u32[]{:S(2)}) copy-start(bf16[1,128,2048]{2,1,0:T(8,128)(2,1)} %param.12) | copy-start | bytes 1572868
  197.3 121.4 %reduce-scatter.7.cloned.1.call-start = ((), (), s32[]{:S(2)}) async-start(), calls=%async_computation.11 | async-start | bytes 4718592 | tf_op jit(solution)/shard_map/reduce_scatter | solution.py:109
  270.0 98.2 %all-gather.10.cloned.1.call-start = ((), (), s32[]{:S(2)}) async-start(), calls=%async_computation.12 | async-start | bytes 4718592 | tf_op jit(solution)/shard_map/all_gather | solution.py:105
  282.9 33.0 %collective-permute-start.12 = (bf16[8,64,1408]{2,1,0:T(8,128)(2,1)S(1)}, bf16[8,64,1408]{2,1,0:T(8,128)(2,1)S(1)}, u32[]{:S(2)}, u32[]{:S(2)}) collective-permute-start(bf16[8,64,1408]{2,1,0:T(8,128)(2,1)S(1)} %get-tuple-element.88), channel_id=1, source_target_pairs={{0,1},{1,0},{2,3},{3,2},{4,5},{5,4},{6,7},{7,6},{8,9},{9,8},{10,11... | collective-permute-start | bytes 4325384 | tf_op jit(solution)/shard_map/ppermute | solution.py:68
  284.1 33.0 %collective-permute-start.13 = (bf16[8,64,1408]{2,1,0:T(8,128)(2,1)S(1)}, bf16[8,64,1408]{2,1,0:T(8,128)(2,1)}, u32[]{:S(2)}, u32[]{:S(2)}) collective-permute-start(bf16[8,64,1408]{2,1,0:T(8,128)(2,1)S(1)} %get-tuple-element.87), channel_id=1, source_target_pairs={{0,2},{1,3},{2,0},{3,1},{4,6},{5,7},{6,4},{7,5},{8,10},{9,11},{10,... | collective-permute-start | bytes 4325384 | tf_op jit(solution)/shard_map/ppermute | solution.py:68
  285.3 33.5 %copy-start.1 = (bf16[128,2048]{1,0:T(8,128)(2,1)S(1)}, bf16[128,2048]{1,0:T(8,128)(2,1)}, u32[]{:S(2)}) copy-start(bf16[128,2048]{1,0:T(8,128)(2,1)} %reduce-scatter.5.cloned.1.call-done) | copy-start | bytes 1572868
  285.3 35.1 %copy-start.7 = (bf16[1,128,2048]{2,1,0:T(8,128)(2,1)S(1)}, bf16[1,128,2048]{2,1,0:T(8,128)(2,1)}, u32[]{:S(2)}) copy-start(bf16[1,128,2048]{2,1,0:T(8,128)(2,1)} %param.23) | copy-start | bytes 1572868
  322.6 124.4 %reduce-scatter.9.cloned.1.call-start = ((), (), s32[]{:S(2)}) async-start(), calls=%async_computation.13 | async-start | bytes 4718592 | tf_op jit(solution)/shard_map/reduce_scatter | solution.py:109
  322.9 34.8 %collective-permute-start.14 = (bf16[8,64,1408]{2,1,0:T(8,128)(2,1)}, bf16[8,64,1408]{2,1,0:T(8,128)(2,1)S(1)}, u32[]{:S(2)}, u32[]{:S(2)}) collective-permute-start(bf16[8,64,1408]{2,1,0:T(8,128)(2,1)} %get-tuple-element.86), channel_id=1, source_target_pairs={{0,3},{1,2},{2,1},{3,0},{4,7},{5,6},{6,5},{7,4},{8,11},{9,10},{10,... | collective-permute-start | bytes 4325384 | tf_op jit(solution)/shard_map/ppermute | solution.py:68
  375.9 47.8 %collective-permute-start.15 = (bf16[176,2048]{1,0:T(8,128)(2,1)}, bf16[176,2048]{1,0:T(8,128)(2,1)}, u32[]{:S(2)}, u32[]{:S(2)}) collective-permute-start(bf16[176,2048]{1,0:T(8,128)(2,1)} %get-tuple-element.94), channel_id=1, source_target_pairs={{0,1},{1,0},{2,3},{3,2},{4,5},{5,4},{6,7},{7,6},{8,9},{9,8},{10,11... | collective-permute-start | bytes 2162696 | tf_op jit(solution)/shard_map/ppermute | solution.py:68
  377.1 51.3 %collective-permute-start.16 = (bf16[176,2048]{1,0:T(8,128)(2,1)}, bf16[176,2048]{1,0:T(8,128)(2,1)}, u32[]{:S(2)}, u32[]{:S(2)}) collective-permute-start(bf16[176,2048]{1,0:T(8,128)(2,1)} %get-tuple-element.93), channel_id=1, source_target_pairs={{0,2},{1,3},{2,0},{3,1},{4,6},{5,7},{6,4},{7,5},{8,10},{9,11},{10,... | collective-permute-start | bytes 2162696 | tf_op jit(solution)/shard_map/ppermute | solution.py:68
  378.3 50.1 %collective-permute-start.17 = (bf16[176,2048]{1,0:T(8,128)(2,1)}, bf16[176,2048]{1,0:T(8,128)(2,1)}, u32[]{:S(2)}, u32[]{:S(2)}) collective-permute-start(bf16[176,2048]{1,0:T(8,128)(2,1)} %get-tuple-element.92), channel_id=1, source_target_pairs={{0,3},{1,2},{2,1},{3,0},{4,7},{5,6},{6,5},{7,4},{8,11},{9,10},{10,... | collective-permute-start | bytes 2162696 | tf_op jit(solution)/shard_map/ppermute | solution.py:68
  396.9 50.2 %all-to-all-start.2 = ((bf16[8,64,1408]{2,1,0:T(8,128)(2,1)}), bf16[8,64,1408]{2,1,0:T(8,128)(2,1)}, u32[]{:S(2)}, u32[]{:S(2)}) async-start(bf16[8,64,1408]{2,1,0:T(8,128)(2,1)} %add_convert_fusion), calls=%async_computation.5 | async-start | bytes 2883584 | tf_op jit(solution)/shard_map/all_to_all | solution.py:317
  404.0 104.9 %reduce-scatter.11.cloned.1.call-start = ((), (), s32[]{:S(2)}) async-start(), calls=%async_computation.14 | async-start | bytes 4718592 | tf_op jit(solution)/shard_map/reduce_scatter | solution.py:109
  421.4 13.5 %collective-permute-start.18 = (bf16[8,64,512]{2,1,0:T(8,128)(2,1)}, bf16[8,64,512]{2,1,0:T(8,128)(2,1)}, u32[]{:S(2)}, u32[]{:S(2)}) collective-permute-start(bf16[8,64,512]{2,1,0:T(8,128)(2,1)} %get-tuple-element.98), channel_id=1, source_target_pairs={{0,1},{1,0},{2,3},{3,2},{4,5},{5,4},{6,7},{7,6},{8,9},{9,8},{10,11... | collective-permute-start | bytes 1572872 | tf_op jit(solution)/shard_map/ppermute | solution.py:68
  422.6 13.2 %collective-permute-start.19 = (bf16[8,64,512]{2,1,0:T(8,128)(2,1)}, bf16[8,64,512]{2,1,0:T(8,128)(2,1)}, u32[]{:S(2)}, u32[]{:S(2)}) collective-permute-start(bf16[8,64,512]{2,1,0:T(8,128)(2,1)} %get-tuple-element.96), channel_id=1, source_target_pairs={{0,2},{1,3},{2,0},{3,1},{4,6},{5,7},{6,4},{7,5},{8,10},{9,11},{10,... | collective-permute-start | bytes 1572872 | tf_op jit(solution)/shard_map/ppermute | solution.py:68
  423.7 23.2 %collective-permute-start.20 = (bf16[8,64,512]{2,1,0:T(8,128)(2,1)}, bf16[8,64,512]{2,1,0:T(8,128)(2,1)}, u32[]{:S(2)}, u32[]{:S(2)}) collective-permute-start(bf16[8,64,512]{2,1,0:T(8,128)(2,1)} %get-tuple-element.97), channel_id=1, source_target_pairs={{0,3},{1,2},{2,1},{3,0},{4,7},{5,6},{6,5},{7,4},{8,11},{9,10},{10,... | collective-permute-start | bytes 1572872 | tf_op jit(solution)/shard_map/ppermute | solution.py:68
  428.4 18.7 %copy-start.14 = (bf16[1024,256]{1,0:T(8,128)(2,1)S(1)}, bf16[1024,256]{1,0:T(8,128)(2,1)}, u32[]{:S(2)}) copy-start(bf16[1024,256]{1,0:T(8,128)(2,1)} %shard_map.203) | copy-start | bytes 1572868
  450.7 6.5 %collective-permute-start.21 = (bf16[64,2048]{1,0:T(8,128)(2,1)S(1)}, bf16[64,2048]{1,0:T(8,128)(2,1)S(1)}, u32[]{:S(2)}, u32[]{:S(2)}) collective-permute-start(bf16[64,2048]{1,0:T(8,128)(2,1)S(1)} %get-tuple-element.107), channel_id=1, source_target_pairs={{0,1},{1,0},{2,3},{3,2},{4,5},{5,4},{6,7},{7,6},{8,9},{9,8},{10,11... | collective-permute-start | bytes 786440 | tf_op jit(solution)/shard_map/ppermute | solution.py:68
  452.0 7.5 %collective-permute-start.22 = (bf16[64,2048]{1,0:T(8,128)(2,1)S(1)}, bf16[64,2048]{1,0:T(8,128)(2,1)S(1)}, u32[]{:S(2)}, u32[]{:S(2)}) collective-permute-start(bf16[64,2048]{1,0:T(8,128)(2,1)S(1)} %get-tuple-element.106), channel_id=1, source_target_pairs={{0,2},{1,3},{2,0},{3,1},{4,6},{5,7},{6,4},{7,5},{8,10},{9,11},{10,... | collective-permute-start | bytes 786440 | tf_op jit(solution)/shard_map/ppermute | solution.py:68
  453.2 10.6 %collective-permute-start.23 = (bf16[64,2048]{1,0:T(8,128)(2,1)S(1)}, bf16[64,2048]{1,0:T(8,128)(2,1)S(1)}, u32[]{:S(2)}, u32[]{:S(2)}) collective-permute-start(bf16[64,2048]{1,0:T(8,128)(2,1)S(1)} %get-tuple-element.105), channel_id=1, source_target_pairs={{0,3},{1,2},{2,1},{3,0},{4,7},{5,6},{6,5},{7,4},{8,11},{9,10},{10,... | collective-permute-start | bytes 786440 | tf_op jit(solution)/shard_map/ppermute | solution.py:68
  466.2 30.8 %all-to-all-start.3 = ((bf16[8,64,512]{2,1,0:T(8,128)(2,1)}), bf16[8,64,512]{2,1,0:T(8,128)(2,1)}, u32[]{:S(2)}, u32[]{:S(2)}) async-start(bf16[8,64,512]{2,1,0:T(8,128)(2,1)} %add_convert_fusion.2), calls=%async_computation.7 | async-start | bytes 1048576 | tf_op jit(solution)/shard_map/all_to_all | solution.py:317
  490.3 20.0 %copy-start.6 = (bf16[128,2048]{1,0:T(8,128)(2,1)S(1)}, bf16[128,2048]{1,0:T(8,128)(2,1)}, u32[]{:S(2)}) copy-start(bf16[128,2048]{1,0:T(8,128)(2,1)} %reduce-scatter.7.cloned.1.call-done) | copy-start | bytes 1572868
  490.3 20.0 %copy-start.8 = (bf16[1,128,2048]{2,1,0:T(8,128)(2,1)S(1)}, bf16[1,128,2048]{2,1,0:T(8,128)(2,1)}, u32[]{:S(2)}) copy-start(bf16[1,128,2048]{2,1,0:T(8,128)(2,1)} %param.23) | copy-start | bytes 1572868
  490.3 20.0 %copy-start.27 = (bf16[128,2048]{1,0:T(8,128)(2,1)S(1)}, bf16[128,2048]{1,0:T(8,128)(2,1)}, u32[]{:S(2)}) copy-start(bf16[128,2048]{1,0:T(8,128)(2,1)} %reduce-scatter.9.cloned.1.call-done) | copy-start | bytes 1572868
  (27 other events, 169.2 us)
Sparse Core Ops, SparseCore 0:
  9.6 69.1 all-gather.11
  95.6 47.6 all-gather.5
  145.6 48.3 reduce-scatter.4
  197.5 45.6 all-gather.7
  270.2 48.5 reduce-scatter.6
  322.8 45.4 all-gather.9
  370.5 75.5 reduce-scatter.8
  448.5 60.3 reduce-scatter.10

commit v5 on v4

--- a/solution.py
+++ b/solution.py
@@ -254,7 +254,7 @@
     )(q, k, v, do, cos, sin, col, row)
 
 
-def ffn_kernel(h_ref, g_ref, wgu_ref, wd_ref, z_ref, dgu_ref, out_ref, dh_ref):
+def ffn_kernel(h_ref, g_ref, wgu_ref, wd_ref, z_ref, dgu_ref, dh_ref):
     ff = z_ref.shape[1]
     gu = dot(h_ref[...], wgu_ref[...])
     gate, up = gu[:, :ff], gu[:, ff:]
@@ -268,7 +268,6 @@
     dgu = jnp.concatenate([dgb, dub], axis=1)
     dgu_ref[...] = dgu
     dh_ref[...] = dot_nt(dgu, wgu_ref[...]).astype(BF)
-    out_ref[...] = dot(z, wd_ref[...]).astype(BF)
 
 
 def ffn(h, g, w_gu, w_d, block):
@@ -279,8 +278,8 @@
         ffn_kernel,
         grid=(seq // block,),
         in_specs=[rows, rows, whole(w_gu.shape), whole(w_d.shape)],
-        out_specs=[pl.BlockSpec((block, ff), lambda i: (i, 0)), pl.BlockSpec((block, 2 * ff), lambda i: (i, 0)), rows, rows],
-        out_shape=[jax.ShapeDtypeStruct((seq, ff), BF), jax.ShapeDtypeStruct((seq, 2 * ff), BF), jax.ShapeDtypeStruct((seq, width), BF), jax.ShapeDtypeStruct((seq, width), BF)],
+        out_specs=[pl.BlockSpec((block, ff), lambda i: (i, 0)), pl.BlockSpec((block, 2 * ff), lambda i: (i, 0)), rows],
+        out_shape=[jax.ShapeDtypeStruct((seq, ff), BF), jax.ShapeDtypeStruct((seq, 2 * ff), BF), jax.ShapeDtypeStruct((seq, width), BF)],
         compiler_params=pltpu.CompilerParams(vmem_limit_bytes=56 * 2**20),
     )(h, g, w_gu, w_d)
 
@@ -373,14 +372,15 @@
     h2_rows = after((normed_f * gain_f).astype(BF), w_gu, w_d)
     h2 = gather_c(h2_rows)
 
-    z, dgu, out_part, dh2_part = ffn(h2, g_all, w_gu, w_d, FFN_ROWS)
+    z, dgu, dh2_part = ffn(h2, g_all, w_gu, w_d, FFN_ROWS)
     dh2 = scatter_c(dh2_part)
     grad_gu_low = dot_tn(after(h2, dh2_part), dgu).astype(BF)
     sent_gu = send_f(grad_gu_low.reshape(c_count, f_count, rows, -1), 1, f_index, f_count)
     grad_down_low = dot_tn(z, after(g_all, grad_gu_low)).astype(BF)
     sent_down = send_f(grad_down_low.reshape(f_count, -1, width), 0, f_index, f_count)
 
-    d_h = after(dh2, grad_down_low, *sent_gu[:3]).astype(F32)
+    out_part = dot(after(z, grad_down_low), w_d).astype(BF)
+    d_h = after(dh2, out_part, *sent_gu[:3]).astype(F32)
     gain_terms_f = jnp.sum(d_h * normed_f, axis=0)
     d_res = cotangent[0].astype(F32) + norm_back(d_h * gain_f, normed_f, recip_f)
     ab_rows = d_res.astype(BF)

time: 527 us -> 525 us (level)
    dot_general x2 -> x3, matrix products: 6.39 us -> 11.3 us  [dot(): return jnp.dot(a, b, preferred_element_type=F32)]
    unnamed x84 -> x80, local copies, waits for them, and re-layouts: 13.4 us -> 11 us
  transfers between devices with their start and end apart: 36 -> 36, of which waited for: 24 -> 25; matrix products, arithmetic and copies ran while one was open for 25% -> 25% of each run, Pallas kernels for 5% -> 5%
where the time goes in v5:
time: 525 us; the launch traced here: 519 us
  waiting for transfers between devices  249 us (47%)
  local copies, waits for them, and re-layouts  58.8 us (11%)
  starting transfers between devices  56.7 us (11%)
  Pallas kernels  50.2 us (10%)
  other arithmetic  48.3 us (9%)
  matrix products  40.3 us (8%)
  between operations  15.4 us (3%)
    ppermute x24, waiting for transfers between devices, swap_f(): return lax.ppermute(value, 'fsdp', [(i, i ^ step) for i in range(f_count)])  136 us
    all_gather x4, waiting for transfers between devices, gather_c(): return lax.all_gather(rows, 'ctx', axis=0, tiled=True)  66.1 us
    all_to_all x4, starting transfers between devices, to_dest(): lax.all_to_all(packed, 'ctx', split_axis=0, concat_axis=0, tiled=True)  30.2 us
    all_to_all x4, waiting for transfers between devices, to_dest(): lax.all_to_all(packed, 'ctx', split_axis=0, concat_axis=0, tiled=True)  28.1 us
    pallas_call x1, Pallas kernels, ffn(): pl.pallas_call(ffn_kernel, grid=(seq // block,), in_specs=[rows, rows, wh...  25.3 us
    ppermute x24, starting transfers between devices, swap_f(): return lax.ppermute(value, 'fsdp', [(i, i ^ step) for i in range(f_count)])  25 us
    dot_general x5, matrix products, dot_tn(): lax.dot_general(a, b, (((0,), (0,)), ((), ())), preferred_element_type=F32)  22.2 us
    reduce_scatter x4, waiting for transfers between devices, scatter_c(): return lax.psum_scatter(full, 'ctx', scatter_dimension=0, tiled=True)  18 us
  transfers between devices with their start and end apart: 36, of which 25 were waited for; matrix products, arithmetic and copies ran while one was open for 25% of the time, Pallas kernels for 5%

profile of v5, /device:TPU:9, one launch (start us, length us, event | category | flops | bytes accessed | tf_op | source)
XLA Modules:
  0.0 518.9 jit_solution(11836151598114090865)
XLA Ops:
  18.0 7.1 %all-to-all-start = ((bf16[8,64,512]{2,1,0:T(8,128)(2,1)}), bf16[8,64,512]{2,1,0:T(8,128)(2,1)}, u32[]{:S(2)}, u32[]{:S(2)}) async-start(bf16[8,64,512]{2,1,0:T(8,128)(2,1)} %copy.141), calls=%async_computation | async-start | bytes 1048576 | tf_op jit(solution)/shard_map/all_to_all | solution.py:316
  26.9 3.1 multiply_sine_fusion
  33.7 16.8 %all-to-all-done = bf16[8,64,512]{2,1,0:T(8,128)(2,1)} async-done(((bf16[8,64,512]{2,1,0:T(8,128)(2,1)}), bf16[8,64,512]{2,1,0:T(8,128)(2,1)}, u32[]{:S(2)}, u32[]{:S(2)}) %all-to-all-start) | async-done | bytes 524320 | tf_op jit(solution)/shard_map/all_to_all | solution.py:316
  50.5 7.9 %all-to-all-start.1 = ((bf16[8,64,1408]{2,1,0:T(8,128)(2,1)}), bf16[8,64,1408]{2,1,0:T(8,128)(2,1)S(1)}, u32[]{:S(2)}, u32[]{:S(2)}) async-start(bf16[8,64,1408]{2,1,0:T(8,128)(2,1)} %pad_maximum_fusion.1), calls=%async_computation.1 | async-start | bytes 2883584 | tf_op jit(solution)/shard_map/all_to_all | solution.py:316
  64.5 4.0 collective-permute-done.8
  71.2 7.7 %collective-permute-done.3 = bf16[8,64,512]{2,1,0:T(8,128)(2,1)S(1)} collective-permute-done((bf16[8,64,512]{2,1,0:T(8,128)(2,1)}, bf16[8,64,512]{2,1,0:T(8,128)(2,1)S(1)}, u32[]{:S(2)}, u32[]{:S(2)}) %collective-permute-start.3) | collective-permute-done | bytes 524320 | tf_op jit(solution)/shard_map/ppermute | solution.py:68
  81.0 9.9 %collective-permute-done.5 = bf16[8,64,512]{2,1,0:T(8,128)(2,1)S(1)} collective-permute-done((bf16[8,64,512]{2,1,0:T(8,128)(2,1)}, bf16[8,64,512]{2,1,0:T(8,128)(2,1)S(1)}, u32[]{:S(2)}, u32[]{:S(2)}) %collective-permute-start.5) | collective-permute-done | bytes 524320 | tf_op jit(solution)/shard_map/ppermute | solution.py:68
  91.0 4.4 all-to-all-done.1
  99.4 3.1 fusion
  108.7 3.1 fusion.33
  112.7 8.8 %shard_map.203 = bf16[1024,256]{1,0:T(8,128)(2,1)} custom-call(bf16[1024,256]{1,0:T(8,128)(2,1)} %copy.151.q_ref, bf16[1024,64]{1,0:T(8,128)(2,1)} %pad_maximum_fusion.5.k_ref, bf16[1024,64]{1,0:T(8,128)(2,1)} %copy.173.v_ref, s32[1024,1]{1,0:T(8,128)} %fusion.23.col_ref, s32[2,512]{1,0:T(2,128)} %reshape.347.row_ref), custom_call_target="tpu_custom_call" | custom-call | tf_op jit(solution)/shard_map/pallas_call | solution.py:233
  121.4 4.3 convolution_convert_fusion.3
  125.7 4.1 collective-permute-done.9
  130.7 13.0 %all-gather.6.cloned.1.call-done.g_ref = bf16[1024,2048]{1,0:T(8,128)(2,1)} async-done(((bf16[128,2048]{1,0:T(8,128)(2,1)}), bf16[1024,2048]{1,0:T(8,128)(2,1)}) %all-gather.6.cloned.1.call-update) | async-done | bytes 4194320 | tf_op jit(solution)/shard_map/all_gather | solution.py:105
  149.5 3.2 broadcast_in_dim.126
  153.9 2.6 bitcast_dynamic-update-slice_fusion.1
  156.5 2.6 bitcast_dynamic-update-slice_fusion
  159.1 22.6 %collective-permute-done.11 = bf16[8,64,1408]{2,1,0:T(8,128)(2,1)S(1)} collective-permute-done((bf16[8,64,1408]{2,1,0:T(8,128)(2,1)S(1)}, bf16[8,64,1408]{2,1,0:T(8,128)(2,1)S(1)}, u32[]{:S(2)}, u32[]{:S(2)}) %collective-permute-start.11) | collective-permute-done | bytes 1441824 | tf_op jit(solution)/shard_map/ppermute | solution.py:68
  182.9 11.0 %reduce-scatter.5.cloned.1.call-done = bf16[128,2048]{1,0:T(8,128)(2,1)} async-done(((bf16[1024,2048]{1,0:T(8,128)(2,1)}), bf16[128,2048]{1,0:T(8,128)(2,1)}) %reduce-scatter.5.cloned.1.call-update) | async-done | bytes 524304 | tf_op jit(solution)/shard_map/reduce_scatter | solution.py:109
  197.5 45.6 %all-gather.8.cloned.1.call-done.h_ref = bf16[1024,2048]{1,0:T(8,128)(2,1)} async-done(((bf16[128,2048]{1,0:T(8,128)(2,1)}), bf16[1024,2048]{1,0:T(8,128)(2,1)}) %all-gather.8.cloned.1.call-update) | async-done | bytes 4194320 | tf_op jit(solution)/shard_map/all_gather | solution.py:105
  243.2 25.3 %shard_map.204 = (bf16[1024,704]{1,0:T(8,128)(2,1)}, bf16[1024,1408]{1,0:T(8,128)(2,1)}, bf16[1024,2048]{1,0:T(8,128)(2,1)}) custom-call(bf16[1024,2048]{1,0:T(8,128)(2,1)} %all-gather.8.cloned.1.call-done.h_ref, bf16[1024,2048]{1,0:T(8,128)(2,1)} %all-gather.6.cloned.1.call-done.g_ref, bf16[2048,1408]{1,0:T(8,128)(2,1)} %bitcast.41.wgu_ref, ...), custom_call_target="tpu_custom_call" | custom-call | tf_op jit(solution)/shard_map/pallas_call | solution.py:277
  270.2 9.4 %convolution_convert_fusion = bf16[2048,1408]{1,0:T(8,128)(2,1)S(1)} fusion(bf16[1024,2048]{1,0:T(8,128)(2,1)} %all-gather.8.cloned.1.call-done.h_ref, bf16[1024,1408]{1,0:T(8,128)(2,1)S(1)} %copy-done.35), kind=kOutput, calls=%fused_computation.5 | convolution fusion | flops 5908463616 | bytes 12845056 | tf_op jit(solution)/shard_map/dot_general | solution.py:135
  284.4 4.6 convolution_convert_fusion.4
  289.0 5.0 convolution_convert_fusion.2
  294.0 21.3 %collective-permute-done.12 = bf16[8,64,1408]{2,1,0:T(8,128)(2,1)} collective-permute-done((bf16[8,64,1408]{2,1,0:T(8,128)(2,1)}, bf16[8,64,1408]{2,1,0:T(8,128)(2,1)}, u32[]{:S(2)}, u32[]{:S(2)}) %collective-permute-start.12) | collective-permute-done | bytes 1441824 | tf_op jit(solution)/shard_map/ppermute | solution.py:68
  323.5 32.0 %collective-permute-done.14 = bf16[8,64,1408]{2,1,0:T(8,128)(2,1)S(1)} collective-permute-done((bf16[8,64,1408]{2,1,0:T(8,128)(2,1)}, bf16[8,64,1408]{2,1,0:T(8,128)(2,1)S(1)}, u32[]{:S(2)}, u32[]{:S(2)}) %collective-permute-start.14) | collective-permute-done | bytes 1441824 | tf_op jit(solution)/shard_map/ppermute | solution.py:68
  355.6 3.7 add_convert_fusion
  359.2 7.5 %all-gather.10.cloned.1.call-done = bf16[1024,2048]{1,0:T(8,128)(2,1)} async-done(((bf16[128,2048]{1,0:T(8,128)(2,1)}), bf16[1024,2048]{1,0:T(8,128)(2,1)}) %all-gather.10.cloned.1.call-update) | async-done | bytes 4194320 | tf_op jit(solution)/shard_map/all_gather | solution.py:105
  368.1 2.6 copy.166
  370.7 3.6 dynamic-slice_bitcast_fusion.4
  379.0 16.2 %shard_map.205 = (bf16[1024,256]{1,0:T(8,128)(2,1)}, bf16[1024,64]{1,0:T(8,128)(2,1)}, bf16[1024,64]{1,0:T(8,128)(2,1)}) custom-call(bf16[1024,256]{1,0:T(8,128)(2,1)} %copy.151.q_ref, bf16[1024,64]{1,0:T(8,128)(2,1)} %pad_maximum_fusion.5.k_ref, bf16[1024,64]{1,0:T(8,128)(2,1)} %copy.173.v_ref, bf16[1024,256]{1,0:T(8,128)(2,1)} %convolution_convert_fusion.7.do_ref, ...), custom_call_target="tpu_custom_call" | custom-call | tf_op jit(solution)/shard_map/pallas_call | solution.py:246
  395.2 7.1 %all-to-all-start.2 = ((bf16[8,64,1408]{2,1,0:T(8,128)(2,1)}), bf16[8,64,1408]{2,1,0:T(8,128)(2,1)}, u32[]{:S(2)}, u32[]{:S(2)}) async-start(bf16[8,64,1408]{2,1,0:T(8,128)(2,1)} %add_convert_fusion), calls=%async_computation.5 | async-start | bytes 2883584 | tf_op jit(solution)/shard_map/all_to_all | solution.py:316
  404.8 4.4 fusion.7
  412.8 4.0 copy.160
  416.7 3.0 dynamic-slice_bitcast_fusion.9
  422.4 4.4 convolution_convert_fusion.1
  426.8 6.5 %collective-permute-done.18 = bf16[8,64,512]{2,1,0:T(8,128)(2,1)} collective-permute-done((bf16[8,64,512]{2,1,0:T(8,128)(2,1)}, bf16[8,64,512]{2,1,0:T(8,128)(2,1)}, u32[]{:S(2)}, u32[]{:S(2)}) %collective-permute-start.18) | collective-permute-done | bytes 524320 | tf_op jit(solution)/shard_map/ppermute | solution.py:68
  434.0 11.4 %collective-permute-done.20 = bf16[8,64,512]{2,1,0:T(8,128)(2,1)} collective-permute-done((bf16[8,64,512]{2,1,0:T(8,128)(2,1)}, bf16[8,64,512]{2,1,0:T(8,128)(2,1)}, u32[]{:S(2)}, u32[]{:S(2)}) %collective-permute-start.20) | collective-permute-done | bytes 524320 | tf_op jit(solution)/shard_map/ppermute | solution.py:68
  445.5 3.5 convolution_convert_fusion.5
  451.9 4.8 collective-permute-done.23
  456.6 7.4 %collective-permute-done.22 = bf16[64,2048]{1,0:T(8,128)(2,1)S(1)} collective-permute-done((bf16[64,2048]{1,0:T(8,128)(2,1)S(1)}, bf16[64,2048]{1,0:T(8,128)(2,1)S(1)}, u32[]{:S(2)}, u32[]{:S(2)}) %collective-permute-start.22) | collective-permute-done | bytes 262176 | tf_op jit(solution)/shard_map/ppermute | solution.py:68
  464.1 2.4 add_convert_fusion.2
  466.5 8.2 %all-to-all-start.3 = ((bf16[8,64,512]{2,1,0:T(8,128)(2,1)}), bf16[8,64,512]{2,1,0:T(8,128)(2,1)}, u32[]{:S(2)}, u32[]{:S(2)}) async-start(bf16[8,64,512]{2,1,0:T(8,128)(2,1)} %add_convert_fusion.2), calls=%async_computation.7 | async-start | bytes 1048576 | tf_op jit(solution)/shard_map/all_to_all | solution.py:316
  475.6 3.1 convert_bitcast_fusion
  485.4 3.1 convert_add_fusion.1
  488.5 6.7 %all-to-all-done.3 = bf16[8,64,512]{2,1,0:T(8,128)(2,1)} async-done(((bf16[8,64,512]{2,1,0:T(8,128)(2,1)}), bf16[8,64,512]{2,1,0:T(8,128)(2,1)}, u32[]{:S(2)}, u32[]{:S(2)}) %all-to-all-start.3) | async-done | bytes 524320 | tf_op jit(solution)/shard_map/all_to_all | solution.py:316
  501.4 5.8 %reduce-scatter.11.cloned.1.call-done = bf16[128,2048]{1,0:T(8,128)(2,1)} async-done(((bf16[1024,2048]{1,0:T(8,128)(2,1)}), bf16[128,2048]{1,0:T(8,128)(2,1)}) %reduce-scatter.11.cloned.1.call-update) | async-done | bytes 524304 | tf_op jit(solution)/shard_map/reduce_scatter | solution.py:109
  508.7 2.9 fusion.26
  (223 shorter events, 99.0 us)
Async XLA Ops:
  7.2 88.2 %all-gather.12.cloned.1.call-start = ((), (), s32[]{:S(2)}) async-start(), calls=%async_computation.15 | async-start | bytes 4718592 | tf_op jit(solution)/shard_map/all_gather | solution.py:105
  7.9 53.8 %collective-permute-start = (bf16[176,2048]{1,0:T(8,128)(2,1)}, bf16[176,2048]{1,0:T(8,128)(2,1)}, u32[]{:S(2)}, u32[]{:S(2)}) collective-permute-start(bf16[176,2048]{1,0:T(8,128)(2,1)} %param.22), channel_id=1, source_target_pairs={{0,1},{1,0},{2,3},{3,2},{4,5},{5,4},{6,7},{7,6},{8,9},{9,8},{10,11... | collective-permute-start | bytes 2162696 | tf_op jit(solution)/shard_map/ppermute | solution.py:68
  9.2 52.6 %collective-permute-start.1 = (bf16[176,2048]{1,0:T(8,128)(2,1)}, bf16[176,2048]{1,0:T(8,128)(2,1)}, u32[]{:S(2)}, u32[]{:S(2)}) collective-permute-start(bf16[176,2048]{1,0:T(8,128)(2,1)} %param.22), channel_id=1, source_target_pairs={{0,2},{1,3},{2,0},{3,1},{4,6},{5,7},{6,4},{7,5},{8,10},{9,11},{10,... | collective-permute-start | bytes 2162696 | tf_op jit(solution)/shard_map/ppermute | solution.py:68
  10.4 51.3 %collective-permute-start.2 = (bf16[176,2048]{1,0:T(8,128)(2,1)}, bf16[176,2048]{1,0:T(8,128)(2,1)}, u32[]{:S(2)}, u32[]{:S(2)}) collective-permute-start(bf16[176,2048]{1,0:T(8,128)(2,1)} %param.22), channel_id=1, source_target_pairs={{0,3},{1,2},{2,1},{3,0},{4,7},{5,6},{6,5},{7,4},{8,11},{9,10},{10,... | collective-permute-start | bytes 2162696 | tf_op jit(solution)/shard_map/ppermute | solution.py:68
  10.6 49.1 %collective-permute-start.6 = (bf16[64,2048]{1,0:T(8,128)(2,1)}, bf16[64,2048]{1,0:T(8,128)(2,1)}, u32[]{:S(2)}, u32[]{:S(2)}) collective-permute-start(bf16[64,2048]{1,0:T(8,128)(2,1)} %param.18), channel_id=1, source_target_pairs={{0,1},{1,0},{2,3},{3,2},{4,5},{5,4},{6,7},{7,6},{8,9},{9,8},{10,11... | collective-permute-start | bytes 786440 | tf_op jit(solution)/shard_map/ppermute | solution.py:68
  11.8 48.9 %collective-permute-start.7 = (bf16[64,2048]{1,0:T(8,128)(2,1)}, bf16[64,2048]{1,0:T(8,128)(2,1)}, u32[]{:S(2)}, u32[]{:S(2)}) collective-permute-start(bf16[64,2048]{1,0:T(8,128)(2,1)} %param.18), channel_id=1, source_target_pairs={{0,2},{1,3},{2,0},{3,1},{4,6},{5,7},{6,4},{7,5},{8,10},{9,11},{10,... | collective-permute-start | bytes 786440 | tf_op jit(solution)/shard_map/ppermute | solution.py:68
  18.0 32.5 %all-to-all-start = ((bf16[8,64,512]{2,1,0:T(8,128)(2,1)}), bf16[8,64,512]{2,1,0:T(8,128)(2,1)}, u32[]{:S(2)}, u32[]{:S(2)}) async-start(bf16[8,64,512]{2,1,0:T(8,128)(2,1)} %copy.141), calls=%async_computation | async-start | bytes 1048576 | tf_op jit(solution)/shard_map/all_to_all | solution.py:316
  26.9 69.2 %copy-start.30 = (f32[32]{0:T(128)}, f32[32]{0:T(128)S(1)}, u32[]{:S(2)}) copy-start(f32[32]{0:T(128)S(1)} %negate_power_fusion) | copy-start | bytes 388
  26.9 69.2 %copy-start.29 = (f32[1024]{0:T(1024)}, f32[1024]{0:T(1024)S(1)}, u32[]{:S(2)}) copy-start(f32[1024]{0:T(1024)S(1)} %fusion.49) | copy-start | bytes 12292
  31.9 26.5 %copy-start.18 = (f32[1024,1,32]{2,0,1:T(8,128)S(1)}, f32[1024,1,32]{2,0,1:T(8,128)}, u32[]{:S(2)}) copy-start(f32[1024,1,32]{2,0,1:T(8,128)} %get-tuple-element.118) | copy-start | bytes 393220
  32.8 25.6 %copy-start.19 = (f32[1024,1,32]{2,0,1:T(8,128)S(1)}, f32[1024,1,32]{2,0,1:T(8,128)}, u32[]{:S(2)}) copy-start(f32[1024,1,32]{2,0,1:T(8,128)} %get-tuple-element.119) | copy-start | bytes 393220
  50.5 44.9 %all-to-all-start.1 = ((bf16[8,64,1408]{2,1,0:T(8,128)(2,1)}), bf16[8,64,1408]{2,1,0:T(8,128)(2,1)S(1)}, u32[]{:S(2)}, u32[]{:S(2)}) async-start(bf16[8,64,1408]{2,1,0:T(8,128)(2,1)} %pad_maximum_fusion.1), calls=%async_computation.1 | async-start | bytes 2883584 | tf_op jit(solution)/shard_map/all_to_all | solution.py:316
  58.4 85.3 %all-gather.6.cloned.1.call-start = ((), (), s32[]{:S(2)}) async-start(), calls=%async_computation.8 | async-start | bytes 4718592 | tf_op jit(solution)/shard_map/all_gather | solution.py:105
  59.8 8.7 %collective-permute-start.8 = (bf16[64,2048]{1,0:T(8,128)(2,1)}, bf16[64,2048]{1,0:T(8,128)(2,1)S(1)}, u32[]{:S(2)}, u32[]{:S(2)}) collective-permute-start(bf16[64,2048]{1,0:T(8,128)(2,1)} %param.18), channel_id=1, source_target_pairs={{0,3},{1,2},{2,1},{3,0},{4,7},{5,6},{6,5},{7,4},{8,11},{9,10},{10,... | collective-permute-start | bytes 786440 | tf_op jit(solution)/shard_map/ppermute | solution.py:68
  61.8 17.1 %collective-permute-start.3 = (bf16[8,64,512]{2,1,0:T(8,128)(2,1)}, bf16[8,64,512]{2,1,0:T(8,128)(2,1)S(1)}, u32[]{:S(2)}, u32[]{:S(2)}) collective-permute-start(bf16[8,64,512]{2,1,0:T(8,128)(2,1)} %all-to-all-done), channel_id=1, source_target_pairs={{0,1},{1,0},{2,3},{3,2},{4,5},{5,4},{6,7},{7,6},{8,9},{9,8},{10,11... | collective-permute-start | bytes 1572872 | tf_op jit(solution)/shard_map/ppermute | solution.py:68
  63.4 17.6 %collective-permute-start.4 = (bf16[8,64,512]{2,1,0:T(8,128)(2,1)}, bf16[8,64,512]{2,1,0:T(8,128)(2,1)S(1)}, u32[]{:S(2)}, u32[]{:S(2)}) collective-permute-start(bf16[8,64,512]{2,1,0:T(8,128)(2,1)} %all-to-all-done), channel_id=1, source_target_pairs={{0,2},{1,3},{2,0},{3,1},{4,6},{5,7},{6,4},{7,5},{8,10},{9,11},{10,... | collective-permute-start | bytes 1572872 | tf_op jit(solution)/shard_map/ppermute | solution.py:68
  69.5 21.4 %collective-permute-start.5 = (bf16[8,64,512]{2,1,0:T(8,128)(2,1)}, bf16[8,64,512]{2,1,0:T(8,128)(2,1)S(1)}, u32[]{:S(2)}, u32[]{:S(2)}) collective-permute-start(bf16[8,64,512]{2,1,0:T(8,128)(2,1)} %all-to-all-done), channel_id=1, source_target_pairs={{0,3},{1,2},{2,1},{3,0},{4,7},{5,6},{6,5},{7,4},{8,11},{9,10},{10,... | collective-permute-start | bytes 1572872 | tf_op jit(solution)/shard_map/ppermute | solution.py:68
  95.5 98.5 %reduce-scatter.5.cloned.1.call-start = ((), (), s32[]{:S(2)}) async-start(), calls=%async_computation.9 | async-start | bytes 4718592 | tf_op jit(solution)/shard_map/reduce_scatter | solution.py:109
  96.9 32.9 %collective-permute-start.9 = (bf16[8,64,1408]{2,1,0:T(8,128)(2,1)S(1)}, bf16[8,64,1408]{2,1,0:T(8,128)(2,1)}, u32[]{:S(2)}, u32[]{:S(2)}) collective-permute-start(bf16[8,64,1408]{2,1,0:T(8,128)(2,1)S(1)} %all-to-all-done.1), channel_id=1, source_target_pairs={{0,1},{1,0},{2,3},{3,2},{4,5},{5,4},{6,7},{7,6},{8,9},{9,8},{10,11... | collective-permute-start | bytes 4325384 | tf_op jit(solution)/shard_map/ppermute | solution.py:68
  98.2 32.5 %collective-permute-start.10 = (bf16[8,64,1408]{2,1,0:T(8,128)(2,1)S(1)}, bf16[8,64,1408]{2,1,0:T(8,128)(2,1)}, u32[]{:S(2)}, u32[]{:S(2)}) collective-permute-start(bf16[8,64,1408]{2,1,0:T(8,128)(2,1)S(1)} %all-to-all-done.1), channel_id=1, source_target_pairs={{0,2},{1,3},{2,0},{3,1},{4,6},{5,7},{6,4},{7,5},{8,10},{9,11},{10,... | collective-permute-start | bytes 4325384 | tf_op jit(solution)/shard_map/ppermute | solution.py:68
  143.7 99.4 %all-gather.8.cloned.1.call-start = ((), (), s32[]{:S(2)}) async-start(), calls=%async_computation.10 | async-start | bytes 4718592 | tf_op jit(solution)/shard_map/all_gather | solution.py:105
  147.8 33.9 %collective-permute-start.11 = (bf16[8,64,1408]{2,1,0:T(8,128)(2,1)S(1)}, bf16[8,64,1408]{2,1,0:T(8,128)(2,1)S(1)}, u32[]{:S(2)}, u32[]{:S(2)}) collective-permute-start(bf16[8,64,1408]{2,1,0:T(8,128)(2,1)S(1)} %all-to-all-done.1), channel_id=1, source_target_pairs={{0,3},{1,2},{2,1},{3,0},{4,7},{5,6},{6,5},{7,4},{8,11},{9,10},{10,... | collective-permute-start | bytes 4325384 | tf_op jit(solution)/shard_map/ppermute | solution.py:68
  156.5 37.4 %copy-start = (bf16[1,128,2048]{2,1,0:T(8,128)(2,1)S(1)}, bf16[1,128,2048]{2,1,0:T(8,128)(2,1)}, u32[]{:S(2)}) copy-start(bf16[1,128,2048]{2,1,0:T(8,128)(2,1)} %param.12) | copy-start | bytes 1572868
  197.3 119.9 %reduce-scatter.7.cloned.1.call-start = ((), (), s32[]{:S(2)}) async-start(), calls=%async_computation.11 | async-start | bytes 4718592 | tf_op jit(solution)/shard_map/reduce_scatter | solution.py:109
  268.5 98.2 %all-gather.10.cloned.1.call-start = ((), (), s32[]{:S(2)}) async-start(), calls=%async_computation.12 | async-start | bytes 4718592 | tf_op jit(solution)/shard_map/all_gather | solution.py:105
  282.0 33.2 %collective-permute-start.12 = (bf16[8,64,1408]{2,1,0:T(8,128)(2,1)}, bf16[8,64,1408]{2,1,0:T(8,128)(2,1)}, u32[]{:S(2)}, u32[]{:S(2)}) collective-permute-start(bf16[8,64,1408]{2,1,0:T(8,128)(2,1)} %get-tuple-element.88), channel_id=1, source_target_pairs={{0,1},{1,0},{2,3},{3,2},{4,5},{5,4},{6,7},{7,6},{8,9},{9,8},{10,11... | collective-permute-start | bytes 4325384 | tf_op jit(solution)/shard_map/ppermute | solution.py:68
  283.2 32.9 %collective-permute-start.13 = (bf16[8,64,1408]{2,1,0:T(8,128)(2,1)}, bf16[8,64,1408]{2,1,0:T(8,128)(2,1)}, u32[]{:S(2)}, u32[]{:S(2)}) collective-permute-start(bf16[8,64,1408]{2,1,0:T(8,128)(2,1)} %get-tuple-element.87), channel_id=1, source_target_pairs={{0,2},{1,3},{2,0},{3,1},{4,6},{5,7},{6,4},{7,5},{8,10},{9,11},{10,... | collective-permute-start | bytes 4325384 | tf_op jit(solution)/shard_map/ppermute | solution.py:68
  289.0 28.3 %copy-start.1 = (bf16[128,2048]{1,0:T(8,128)(2,1)S(1)}, bf16[128,2048]{1,0:T(8,128)(2,1)}, u32[]{:S(2)}) copy-start(bf16[128,2048]{1,0:T(8,128)(2,1)} %reduce-scatter.5.cloned.1.call-done) | copy-start | bytes 1572868
  289.0 29.8 %copy-start.8 = (bf16[1,128,2048]{2,1,0:T(8,128)(2,1)S(1)}, bf16[1,128,2048]{2,1,0:T(8,128)(2,1)}, u32[]{:S(2)}) copy-start(bf16[1,128,2048]{2,1,0:T(8,128)(2,1)} %param.23) | copy-start | bytes 1572868
  321.1 124.3 %reduce-scatter.9.cloned.1.call-start = ((), (), s32[]{:S(2)}) async-start(), calls=%async_computation.13 | async-start | bytes 4718592 | tf_op jit(solution)/shard_map/reduce_scatter | solution.py:109
  321.4 34.2 %collective-permute-start.14 = (bf16[8,64,1408]{2,1,0:T(8,128)(2,1)}, bf16[8,64,1408]{2,1,0:T(8,128)(2,1)S(1)}, u32[]{:S(2)}, u32[]{:S(2)}) collective-permute-start(bf16[8,64,1408]{2,1,0:T(8,128)(2,1)} %get-tuple-element.86), channel_id=1, source_target_pairs={{0,3},{1,2},{2,1},{3,0},{4,7},{5,6},{6,5},{7,4},{8,11},{9,10},{10,... | collective-permute-start | bytes 4325384 | tf_op jit(solution)/shard_map/ppermute | solution.py:68
  374.3 47.8 %collective-permute-start.15 = (bf16[176,2048]{1,0:T(8,128)(2,1)}, bf16[176,2048]{1,0:T(8,128)(2,1)}, u32[]{:S(2)}, u32[]{:S(2)}) collective-permute-start(bf16[176,2048]{1,0:T(8,128)(2,1)} %get-tuple-element.94), channel_id=1, source_target_pairs={{0,1},{1,0},{2,3},{3,2},{4,5},{5,4},{6,7},{7,6},{8,9},{9,8},{10,11... | collective-permute-start | bytes 2162696 | tf_op jit(solution)/shard_map/ppermute | solution.py:68
  375.5 51.3 %collective-permute-start.16 = (bf16[176,2048]{1,0:T(8,128)(2,1)}, bf16[176,2048]{1,0:T(8,128)(2,1)}, u32[]{:S(2)}, u32[]{:S(2)}) collective-permute-start(bf16[176,2048]{1,0:T(8,128)(2,1)} %get-tuple-element.93), channel_id=1, source_target_pairs={{0,2},{1,3},{2,0},{3,1},{4,6},{5,7},{6,4},{7,5},{8,10},{9,11},{10,... | collective-permute-start | bytes 2162696 | tf_op jit(solution)/shard_map/ppermute | solution.py:68
  376.6 50.1 %collective-permute-start.17 = (bf16[176,2048]{1,0:T(8,128)(2,1)}, bf16[176,2048]{1,0:T(8,128)(2,1)}, u32[]{:S(2)}, u32[]{:S(2)}) collective-permute-start(bf16[176,2048]{1,0:T(8,128)(2,1)} %get-tuple-element.92), channel_id=1, source_target_pairs={{0,3},{1,2},{2,1},{3,0},{4,7},{5,6},{6,5},{7,4},{8,11},{9,10},{10,... | collective-permute-start | bytes 2162696 | tf_op jit(solution)/shard_map/ppermute | solution.py:68
  395.2 50.2 %all-to-all-start.2 = ((bf16[8,64,1408]{2,1,0:T(8,128)(2,1)}), bf16[8,64,1408]{2,1,0:T(8,128)(2,1)}, u32[]{:S(2)}, u32[]{:S(2)}) async-start(bf16[8,64,1408]{2,1,0:T(8,128)(2,1)} %add_convert_fusion), calls=%async_computation.5 | async-start | bytes 2883584 | tf_op jit(solution)/shard_map/all_to_all | solution.py:316
  402.3 104.9 %reduce-scatter.11.cloned.1.call-start = ((), (), s32[]{:S(2)}) async-start(), calls=%async_computation.14 | async-start | bytes 4718592 | tf_op jit(solution)/shard_map/reduce_scatter | solution.py:109
  419.7 13.5 %collective-permute-start.18 = (bf16[8,64,512]{2,1,0:T(8,128)(2,1)}, bf16[8,64,512]{2,1,0:T(8,128)(2,1)}, u32[]{:S(2)}, u32[]{:S(2)}) collective-permute-start(bf16[8,64,512]{2,1,0:T(8,128)(2,1)} %get-tuple-element.98), channel_id=1, source_target_pairs={{0,1},{1,0},{2,3},{3,2},{4,5},{5,4},{6,7},{7,6},{8,9},{9,8},{10,11... | collective-permute-start | bytes 1572872 | tf_op jit(solution)/shard_map/ppermute | solution.py:68
  420.9 13.2 %collective-permute-start.19 = (bf16[8,64,512]{2,1,0:T(8,128)(2,1)}, bf16[8,64,512]{2,1,0:T(8,128)(2,1)}, u32[]{:S(2)}, u32[]{:S(2)}) collective-permute-start(bf16[8,64,512]{2,1,0:T(8,128)(2,1)} %get-tuple-element.96), channel_id=1, source_target_pairs={{0,2},{1,3},{2,0},{3,1},{4,6},{5,7},{6,4},{7,5},{8,10},{9,11},{10,... | collective-permute-start | bytes 1572872 | tf_op jit(solution)/shard_map/ppermute | solution.py:68
  422.0 23.4 %collective-permute-start.20 = (bf16[8,64,512]{2,1,0:T(8,128)(2,1)}, bf16[8,64,512]{2,1,0:T(8,128)(2,1)}, u32[]{:S(2)}, u32[]{:S(2)}) collective-permute-start(bf16[8,64,512]{2,1,0:T(8,128)(2,1)} %get-tuple-element.97), channel_id=1, source_target_pairs={{0,3},{1,2},{2,1},{3,0},{4,7},{5,6},{6,5},{7,4},{8,11},{9,10},{10,... | collective-permute-start | bytes 1572872 | tf_op jit(solution)/shard_map/ppermute | solution.py:68
  426.7 18.8 %copy-start.15 = (bf16[1024,256]{1,0:T(8,128)(2,1)S(1)}, bf16[1024,256]{1,0:T(8,128)(2,1)}, u32[]{:S(2)}) copy-start(bf16[1024,256]{1,0:T(8,128)(2,1)} %shard_map.203) | copy-start | bytes 1572868
  445.5 18.5 %copy-start.17 = (bf16[8,64,512]{2,1,0:T(8,128)(2,1)S(1)}, bf16[8,64,512]{2,1,0:T(8,128)(2,1)}, u32[]{:S(2)}) copy-start(bf16[8,64,512]{2,1,0:T(8,128)(2,1)} %get-tuple-element.71) | copy-start | bytes 1572868
  449.1 7.5 %collective-permute-start.23 = (bf16[64,2048]{1,0:T(8,128)(2,1)S(1)}, bf16[64,2048]{1,0:T(8,128)(2,1)S(1)}, u32[]{:S(2)}, u32[]{:S(2)}) collective-permute-start(bf16[64,2048]{1,0:T(8,128)(2,1)S(1)} %get-tuple-element.105), channel_id=1, source_target_pairs={{0,3},{1,2},{2,1},{3,0},{4,7},{5,6},{6,5},{7,4},{8,11},{9,10},{10,... | collective-permute-start | bytes 786440 | tf_op jit(solution)/shard_map/ppermute | solution.py:68
  451.3 12.8 %collective-permute-start.22 = (bf16[64,2048]{1,0:T(8,128)(2,1)S(1)}, bf16[64,2048]{1,0:T(8,128)(2,1)S(1)}, u32[]{:S(2)}, u32[]{:S(2)}) collective-permute-start(bf16[64,2048]{1,0:T(8,128)(2,1)S(1)} %get-tuple-element.106), channel_id=1, source_target_pairs={{0,2},{1,3},{2,0},{3,1},{4,6},{5,7},{6,4},{7,5},{8,10},{9,11},{10,... | collective-permute-start | bytes 786440 | tf_op jit(solution)/shard_map/ppermute | solution.py:68
  451.6 12.5 %collective-permute-start.21 = (bf16[64,2048]{1,0:T(8,128)(2,1)S(1)}, bf16[64,2048]{1,0:T(8,128)(2,1)S(1)}, u32[]{:S(2)}, u32[]{:S(2)}) collective-permute-start(bf16[64,2048]{1,0:T(8,128)(2,1)S(1)} %get-tuple-element.107), channel_id=1, source_target_pairs={{0,1},{1,0},{2,3},{3,2},{4,5},{5,4},{6,7},{7,6},{8,9},{9,8},{10,11... | collective-permute-start | bytes 786440 | tf_op jit(solution)/shard_map/ppermute | solution.py:68
  466.5 28.7 %all-to-all-start.3 = ((bf16[8,64,512]{2,1,0:T(8,128)(2,1)}), bf16[8,64,512]{2,1,0:T(8,128)(2,1)}, u32[]{:S(2)}, u32[]{:S(2)}) async-start(bf16[8,64,512]{2,1,0:T(8,128)(2,1)} %add_convert_fusion.2), calls=%async_computation.7 | async-start | bytes 1048576 | tf_op jit(solution)/shard_map/all_to_all | solution.py:316
  488.5 20.2 %copy-start.7 = (bf16[128,2048]{1,0:T(8,128)(2,1)S(1)}, bf16[128,2048]{1,0:T(8,128)(2,1)}, u32[]{:S(2)}) copy-start(bf16[128,2048]{1,0:T(8,128)(2,1)} %reduce-scatter.7.cloned.1.call-done) | copy-start | bytes 1572868
  488.5 20.2 %copy-start.9 = (bf16[1,128,2048]{2,1,0:T(8,128)(2,1)S(1)}, bf16[1,128,2048]{2,1,0:T(8,128)(2,1)}, u32[]{:S(2)}) copy-start(bf16[1,128,2048]{2,1,0:T(8,128)(2,1)} %param.23) | copy-start | bytes 1572868
  488.5 20.2 %copy-start.25 = (bf16[128,2048]{1,0:T(8,128)(2,1)S(1)}, bf16[128,2048]{1,0:T(8,128)(2,1)}, u32[]{:S(2)}) copy-start(bf16[128,2048]{1,0:T(8,128)(2,1)} %reduce-scatter.9.cloned.1.call-done) | copy-start | bytes 1572868
  (25 other events, 175.1 us)
Sparse Core Ops, SparseCore 0:
  9.6 69.1 all-gather.11
  95.6 48.0 all-gather.5
  146.0 47.8 reduce-scatter.4
  197.4 45.6 all-gather.7
  268.6 48.6 reduce-scatter.6
  321.3 45.3 all-gather.9
  369.0 75.6 reduce-scatter.8
  447.0 60.2 reduce-scatter.10
